TPU v7x, 32 devices: a whole 2x2x4 slice. The times are simulated.
32 devices in a mesh: dp: 8 (over y, x, core), tensor: 4 (over z).
Axes of the slice: x: 2, y: 2, z: 4, core: 2. Of those that a mesh axis runs over, the one named last changes fastest.
Arguments:
- tokens: bfloat16 [192, 8192], P('dp', 'tensor'), may hold values from -6 to 6
- gate_weight: bfloat16 [8192, 28672], P('tensor', 'dp'), may hold values from -0.0625 to 0.0625
- up_weight: bfloat16 [8192, 28672], P('tensor', 'dp'), may hold values from -0.0625 to 0.0625
- down_weight: bfloat16 [28672, 8192], P('dp', 'tensor'), may hold values from -0.03125 to 0.03125
- adapter_proj_in: bfloat16 [256, 32, 8192], P('dp', None, 'tensor'), may hold values from -0.0625 to 0.0625
- adapter_lift_in: bfloat16 [256, 2, 16, 28672], P('tensor', None, None, 'dp'), may hold values from -1.5 to 1.5
- adapter_proj_out: bfloat16 [256, 16, 28672], P('tensor', None, 'dp'), may hold values from -0.03125 to 0.03125
- adapter_lift_out: bfloat16 [256, 16, 8192], P('dp', None, 'tensor'), may hold values from -1.5 to 1.5
- token_request: int32 [192], replicated, may hold values from 0 to 31, never falling along the last dimension, each value on 1 to 12 neighbouring positions
- request_adapter: int32 [32], replicated, may hold values from 0 to 255
- adapter_slot: int32 [256], replicated, may hold values from 0 to 255, each once
Outputs:
- mixed: bfloat16 [192, 8192], P('dp', 'tensor')
Inputs may be any that keep to these rules, and one draw needn't show every extreme that they name: `token_request`: request numbers never fall along the tokens; every request has one or more tokens. `adapter_slot`: every slot holds exactly one adapter.
All inputs are finite; a program needn't handle non-finite values.
Results may differ from a plain program's by a relative error of at most 0.02.
Values may be sent and summed in bfloat16 or wider, within the bound.
No kernel may reach another device: no remote copies, remote signals or barrier semaphores. Data moves between devices by JAX's collectives and lax.ppermute only.
A program may use at most 192 MiB of HBM per device.

v0:
```python
import jax
import jax.numpy as jnp
from jax import lax
from jax.sharding import PartitionSpec as P


def lookup(keys, table):
    hits = keys[:, None] == jnp.arange(table.shape[0], dtype=jnp.int32)[None, :]
    return jnp.sum(jnp.where(hits, table[None, :], 0), axis=1)


def owned(slot_of, first_slot, amount):
    places = first_slot + jnp.arange(amount, dtype=jnp.int32)
    return (slot_of[:, None] == places[None, :]).astype(jnp.bfloat16)


def per_device(
    tokens,
    gate_weight,
    up_weight,
    down_weight,
    adapter_proj_in,
    adapter_lift_in,
    adapter_proj_out,
    adapter_lift_out,
    token_request,
    request_adapter,
    adapter_slot,
):
    slot_of = lookup(lookup(token_request, request_adapter), adapter_slot)
    dp_index = lax.axis_index("dp")
    tensor_index = lax.axis_index("tensor")
    per_dp = adapter_proj_in.shape[0]
    per_tensor = adapter_lift_in.shape[0]
    rank = adapter_lift_out.shape[1]
    gathered = lax.all_gather(tokens, "dp", axis=0, tiled=True)
    total_rows = gathered.shape[0]
    mask_store_dp = owned(slot_of, dp_index * per_dp, per_dp)
    mask_store_tensor = owned(slot_of, tensor_index * per_tensor, per_tensor)
    projected = jnp.einsum(
        "td,srd->tsr", gathered, adapter_proj_in, preferred_element_type=jnp.float32
    )
    rank_part = jnp.sum(projected * mask_store_dp.astype(jnp.float32)[:, :, None], axis=1)
    rank_in = lax.psum(rank_part, ("dp", "tensor")).astype(jnp.bfloat16)
    rank_in = rank_in.reshape(total_rows, 2, rank)
    spread = rank_in[:, None, :, :] * mask_store_tensor[:, :, None, None]
    adapt_in = jnp.einsum(
        "tscr,scrf->tcf", spread, adapter_lift_in, preferred_element_type=jnp.float32
    )
    row_block = gathered
    gate_part = jnp.dot(row_block, gate_weight, preferred_element_type=jnp.float32)
    up_part = jnp.dot(row_block, up_weight, preferred_element_type=jnp.float32)
    extra = adapt_in
    shares = lax.psum_scatter(
        (jnp.stack([gate_part, up_part], axis=1) + extra).astype(jnp.bfloat16),
        "tensor",
        scatter_dimension=0,
        tiled=True,
    ).astype(jnp.float32)
    hidden = (jax.nn.silu(shares[:, 0]) * shares[:, 1]).astype(jnp.bfloat16)
    hidden_all = lax.all_gather(hidden, "tensor", axis=0, tiled=True)
    projected_out = jnp.einsum(
        "tf,srf->tsr", hidden_all, adapter_proj_out, preferred_element_type=jnp.float32
    )
    rank_part_out = jnp.sum(
        projected_out * mask_store_tensor.astype(jnp.float32)[:, :, None], axis=1
    )
    rank_out = lax.psum(rank_part_out, ("dp", "tensor")).astype(jnp.bfloat16)
    spread_out = rank_out[:, None, :] * mask_store_dp[:, :, None]
    adapt_out = jnp.einsum(
        "tsr,srd->td", spread_out, adapter_lift_out, preferred_element_type=jnp.float32
    )
    row_block = hidden_all
    extra = adapt_out
    return lax.psum_scatter(
        (jnp.dot(row_block, down_weight, preferred_element_type=jnp.float32) + extra).astype(
            jnp.bfloat16
        ),
        "dp",
        scatter_dimension=0,
        tiled=True,
    )


def solution(mesh):
    placed = (
        P("dp", "tensor"),
        P("tensor", "dp"),
        P("tensor", "dp"),
        P("dp", "tensor"),
        P("dp", None, "tensor"),
        P("tensor", None, None, "dp"),
        P("tensor", None, "dp"),
        P("dp", None, "tensor"),
        P(),
        P(),
        P(),
    )
    return jax.shard_map(
        per_device, mesh=mesh, in_specs=placed, out_specs=P("dp", "tensor"), check_vma=False
    )
```

profile of v0, /device:TPU:0, one launch (start us, length us, event | category | flops | bytes accessed | tf_op | source)
XLA Modules:
  0.0 295.1 jit_solution(11368564628392029252)
XLA Ops:
  6.5 0.9 select_reduce_fusion.1
  7.5 0.9 select_reduce_fusion
  8.3 0.1 compare_convert_fusion.1
  8.4 0.1 fusion.28
  8.5 12.2 %all_gather.6 = bf16[192,2048]{1,0:T(8,128)(2,1)S(1)} all-gather(bf16[24,2048]{1,0:T(8,128)(2,1)} %param.11), channel_id=1, replica_groups=mesh['dp'=8,'tensor'=4] {'dp'}, dimensions={0}, use_global_device_ids=true | all-gather | bytes 884736 | tf_op jit(solution)/shard_map/all_gather | solution.py:36
  20.7 3.5 %fusion.17 = f32[192,32]{0,1:T(8,128)S(1)} fusion(bf16[32,32,2048]{2,1,0:T(8,128)(2,1)} %param.15, bf16[192,2048]{1,0:T(8,128)(2,1)S(1)} %all_gather.6, f32[192,32]{0,1:T(8,128)S(1)} %get-tuple-element.8), kind=kOutput, calls=%fused_computation.15 | convolution fusion | flops 805693440 | bytes 5029888 | tf_op jit(solution)/shard_map/td,srd->tsr/dot_general | solution.py:40
  24.2 39.7 %psum.14 = bf16[192,32]{0,1:T(8,128)(2,1)S(1)} all-reduce(f32[192,32]{0,1:T(8,128)S(1)} %fusion.17), channel_id=1, replica_groups=mesh['dp'=8,'tensor'=4] {'dp','tensor'}, use_global_device_ids=true, to_apply=%region_3.4 | all-reduce | flops 6144 | bytes 36864 | tf_op jit(solution)/shard_map/psum | solution.py:44
  63.9 6.8 %convolution_bitcast_fusion = f32[192,1,3584]{2,0,1:T(8,128)S(1)} fusion(bf16[192,2048]{1,0:T(8,128)(2,1)S(1)} %all_gather.6, bf16[2048,3584]{1,0:T(8,128)(2,1)} %param.13), kind=kOutput, calls=%fused_computation.7 | convolution fusion | flops 2818572288 | bytes 18219008 | tf_op jit(solution)/shard_map/dot_general | solution.py:52
  70.7 7.0 %convolution_bitcast_fusion.1 = f32[192,1,3584]{2,0,1:T(8,128)S(1)} fusion(bf16[192,2048]{1,0:T(8,128)(2,1)S(1)} %all_gather.6, bf16[2048,3584]{1,0:T(8,128)(2,1)} %param.12), kind=kOutput, calls=%fused_computation.8 | convolution fusion | flops 2818572288 | bytes 18219008 | tf_op jit(solution)/shard_map/dot_general | solution.py:51
  77.7 24.2 %fusion.10 = bf16[192,2,3584]{2,0,1:T(8,128)(2,1)} fusion(bf16[64,2,16,3584]{3,2,1,0:T(8,128)(2,1)} %param.16, f32[192,1,3584]{2,0,1:T(8,128)S(1)} %convolution_bitcast_fusion, f32[192,1,3584]{2,0,1:T(8,128)S(1)} %convolution_bitcast_fusion.1, bf16[192,64]{0,1:T(8,128)(2,1)S(1)} %get-tuple-element.6, bf16[192,2,16]{0,2,1:T(8,128)(2,1)S(1)} %bitcast.43), kind=kOutput, calls=%fused_computation.6 | convolution fusion | flops 2823094272 | bytes 22974464 | tf_op jit(solution)/shard_map/tscr,scrf->tcf/dot_general | solution.py:47
  101.9 0.0 reduce-scatter.3.cloned.1.call-update
  101.9 0.0 all-gather.2.cloned.1.call-start
  101.9 54.7 %reduce-scatter.3.cloned.1.call-done = bf16[48,2,3584]{2,0,1:T(8,128)(2,1)} async-done(((bf16[192,2,3584]{2,0,1:T(8,128)(2,1)}), bf16[48,2,3584]{2,0,1:T(8,128)(2,1)}) %reduce-scatter.3.cloned.1.call-update) | async-done | bytes 688144 | tf_op jit(solution)/shard_map/reduce_scatter | solution.py:54
  156.6 1.2 convert_element_type.58
  157.8 0.9 fusion.22
  158.8 0.0 all-gather.2.cloned.1.call-update
  158.8 0.0 reduce-scatter.5.cloned.1.call-start
  158.8 33.7 %all-gather.2.cloned.1.call-done = bf16[192,3584]{1,0:T(8,128)(2,1)} async-done(((bf16[48,3584]{1,0:T(8,128)(2,1)}), bf16[192,3584]{1,0:T(8,128)(2,1)}) %all-gather.2.cloned.1.call-update) | async-done | bytes 1376272 | tf_op jit(solution)/shard_map/all_gather | solution.py:61
  192.5 11.3 %fusion.2 = f32[192,64,16]{0,1,2:T(8,128)S(1)} fusion(bf16[64,16,3584]{2,1,0:T(8,128)(2,1)} %param.17, bf16[192,3584]{1,0:T(8,128)(2,1)} %all-gather.2.cloned.1.call-done), kind=kOutput, calls=%fused_computation.2 | convolution fusion | flops 1409286144 | bytes 9502720 | tf_op jit(solution)/shard_map/tf,srf->tsr/dot_general | solution.py:62
  203.9 0.6 fusion.18
  204.5 39.7 %psum.15 = bf16[192,16]{0,1:T(8,128)(2,1)S(1)} all-reduce(f32[192,16]{0,1:T(8,128)S(1)} %fusion.18), channel_id=1, replica_groups=mesh['dp'=8,'tensor'=4] {'dp','tensor'}, use_global_device_ids=true, to_apply=%region_6.7 | all-reduce | flops 3072 | bytes 18432 | tf_op jit(solution)/shard_map/psum | solution.py:68
  244.1 7.2 %fusion.30 = f32[192,2048]{1,0:T(8,128)S(1)} fusion(bf16[192,3584]{1,0:T(8,128)(2,1)} %all-gather.2.cloned.1.call-done, bf16[3584,2048]{1,0:T(8,128)(2,1)} %param.14), kind=kOutput, calls=%fused_computation.39 | convolution fusion | flops 2818572288 | bytes 17629184 | tf_op jit(solution)/shard_map/dot_general | solution.py:76
  251.3 2.3 fusion.14
  253.7 34.8 %reduce-scatter.5.cloned.1.call-done = bf16[24,2048]{1,0:T(8,128)(2,1)} async-done(((bf16[192,2048]{1,0:T(8,128)(2,1)}), bf16[24,2048]{1,0:T(8,128)(2,1)}) %reduce-scatter.5.cloned.1.call-update) | async-done | bytes 98320 | tf_op jit(solution)/shard_map/reduce_scatter | solution.py:75
  (6 shorter events, 0.0 us)
Async XLA Ops:
  6.5 244.8 %copy-start = (bf16[32,16,2048]{2,1,0:T(8,128)(2,1)S(1)}, bf16[32,16,2048]{2,1,0:T(8,128)(2,1)}, u32[]{:S(2)}) copy-start(bf16[32,16,2048]{2,1,0:T(8,128)(2,1)} %param.18) | copy-start | bytes 6291460
  6.5 150.1 %reduce-scatter.3.cloned.1.call-start = ((), (), s32[]{:S(2)}) async-start(), calls=%async_computation.2 | async-start | bytes 3440640 | tf_op jit(solution)/shard_map/reduce_scatter | solution.py:54
  101.9 90.6 %all-gather.2.cloned.1.call-start = ((), (), s32[]{:S(2)}) async-start(), calls=%async_computation.3 | async-start | bytes 1720320 | tf_op jit(solution)/shard_map/all_gather | solution.py:61
  158.8 129.8 %reduce-scatter.5.cloned.1.call-start = ((), (), s32[]{:S(2)}) async-start(), calls=%async_computation.4 | async-start | bytes 884736 | tf_op jit(solution)/shard_map/reduce_scatter | solution.py:75
Sparse Core Ops, SparseCore 0:
  102.0 54.5 reduce-scatter.2
  158.9 33.5 all-gather.1
  253.8 34.6 reduce-scatter.4
where the time goes:
time: 296 us; the launch traced here: 295 us
  waiting for transfers between devices  123 us (42%)
  blocking collectives  91.6 us (31%)
  matrix products  62.2 us (21%)
  between operations  13.2 us (4%)
  other arithmetic  4.72 us (2%)
    reduce_scatter x1, waiting for transfers between devices, per_device(): lax.psum_scatter((jnp.stack([gate_part, up_part], axis=1) + extra).astype...  54.7 us
    psum x1, blocking collectives, per_device(): rank_in = lax.psum(rank_part, ('dp', 'tensor')).astype(jnp.bfloat16)  39.7 us
    psum x1, blocking collectives, per_device(): rank_out = lax.psum(rank_part_out, ('dp', 'tensor')).astype(jnp.bfloat16)  39.7 us
    reduce_scatter x1, waiting for transfers between devices, per_device(): lax.psum_scatter((jnp.dot(row_block, down_weight, preferred_element_type=...  34.8 us
    all_gather x1, waiting for transfers between devices, per_device(): hidden_all = lax.all_gather(hidden, 'tensor', axis=0, tiled=True)  33.7 us
    dot_general x1, matrix products, per_device(): jnp.einsum('tscr,scrf->tcf', spread, adapter_lift_in, preferred_element_t...  24.2 us
    all_gather x1, blocking collectives, per_device(): gathered = lax.all_gather(tokens, 'dp', axis=0, tiled=True)  12.2 us
    dot_general x1, matrix products, per_device(): jnp.einsum('tf,srf->tsr', hidden_all, adapter_proj_out, preferred_element...  11.3 us
  transfers between devices with their start and end apart: 3, of which 3 were waited for; matrix products, arithmetic and copies ran while one was open for 0% of the time, Pallas kernels for 0%

commit v1 on v0

--- a/solution.py
+++ b/solution.py
@@ -1,7 +1,15 @@
+import functools
+
 import jax
 import jax.numpy as jnp
 from jax import lax
+from jax.experimental import pallas as pl
+from jax.experimental.pallas import tpu as pltpu
 from jax.sharding import PartitionSpec as P
+
+CHUNKS = 4
+F32 = jnp.float32
+BF16 = jnp.bfloat16
 
 
 def lookup(keys, table):
@@ -14,7 +22,7 @@
     return (slot_of[:, None] == places[None, :]).astype(jnp.bfloat16)
 
 
-def per_device(
+def general_device(
     tokens,
     gate_weight,
     up_weight,
@@ -82,7 +90,294 @@
     )
 
 
+INWARD = [(0, 1), (3, 2)]
+MIDDLE = [(1, 2), (2, 1)]
+OUTWARD = [(1, 0), (2, 3)]
+
+
+def masked_project(block, rows, slot_row, first):
+    slots, rank, depth = block.shape
+    full = lax.dot_general(
+        block.reshape(slots * rank, depth), rows, (((1,), (1,)), ((), ())), preferred_element_type=F32
+    ).reshape(slots, rank, rows.shape[0])
+    ids = first + lax.broadcasted_iota(jnp.int32, full.shape, 0)
+    return jnp.sum(jnp.where(ids == slot_row[None], full, 0.0), axis=0)
+
+
+def spread_rows(rank_t, slot_col, slots):
+    rank = rank_t.shape[0]
+    width = slots * rank
+    lane = lax.broadcasted_iota(jnp.int32, (rank, width), 1)
+    row = lax.broadcasted_iota(jnp.int32, (rank, width), 0)
+    copies = (lax.rem(lane, rank) == row).astype(F32).astype(BF16)
+    tiled = lax.dot_general(
+        rank_t.astype(F32).T.astype(BF16), copies, (((1,), (0,)), ((), ())), preferred_element_type=F32
+    )
+    owner = lax.div(lax.broadcasted_iota(jnp.int32, tiled.shape, 1), rank)
+    return jnp.where(owner == slot_col, tiled, 0.0).astype(BF16)
+
+
+def rank_in_kernel(slot_ref, rows_ref, proj_ref, out_ref):
+    step = pl.program_id(0)
+    part = masked_project(proj_ref[...], rows_ref[...], slot_ref[...], step * proj_ref.shape[0])
+
+    @pl.when(step == 0)
+    def _():
+        out_ref[...] = part
+
+    @pl.when(step > 0)
+    def _():
+        out_ref[...] += part
+
+
+def rank_in_call(slot_row, rows, proj):
+    slots, rank, depth = proj.shape
+    total = rows.shape[0]
+    group = 8
+    return pl.pallas_call(
+        rank_in_kernel,
+        grid=(slots // group,),
+        in_specs=[
+            pl.BlockSpec((1, total), lambda s: (0, 0)),
+            pl.BlockSpec((total, depth), lambda s: (0, 0)),
+            pl.BlockSpec((group, rank, depth), lambda s: (s, 0, 0)),
+        ],
+        out_specs=pl.BlockSpec((rank, total), lambda s: (0, 0)),
+        out_shape=jax.ShapeDtypeStruct((rank, total), F32),
+        compiler_params=pltpu.CompilerParams(vmem_limit_bytes=32 << 20),
+        cost_estimate=pl.CostEstimate(
+            flops=2 * total * slots * rank * depth,
+            bytes_accessed=2 * proj.size + 2 * rows.size,
+            transcendentals=0,
+        ),
+        name="rank_in",
+    )(slot_row, rows, proj)
+
+
+def lift_kernel(side_ref, slot_ref, rank_ref, gate_ref, up_ref, lift_ref, near_ref, far_ref, total_ref):
+    slots, _, rank, width = lift_ref.shape
+    half = near_ref.shape[1]
+    side = side_ref[0]
+    for c, main_ref in ((0, gate_ref), (1, up_ref)):
+        spread = spread_rows(rank_ref[c * rank:(c + 1) * rank, :], slot_ref[...], slots)
+        matrix = lift_ref[:, c].reshape(slots * rank, width)
+        total_ref[c] = main_ref[...] + jnp.dot(spread, matrix, preferred_element_type=F32)
+        near_ref[c] = total_ref[c, pl.ds(pl.multiple_of(side * half, 16), half), :].astype(BF16)
+        far_ref[c] = total_ref[c, pl.ds(pl.multiple_of((1 - side) * half, 16), half), :].astype(BF16)
+
+
+def lift_call(chunk, side, slot_col, rank_t, gate_part, up_part, lift):
+    slots, _, rank, wide = lift.shape
+    width = wide // CHUNKS
+    total = gate_part.shape[0]
+    sub = 1
+    cell = width // sub
+    piece = jax.ShapeDtypeStruct((2, total // 2, width), BF16)
+    return pl.pallas_call(
+        lift_kernel,
+        grid_spec=pltpu.PrefetchScalarGridSpec(
+            num_scalar_prefetch=1,
+            grid=(sub,),
+            in_specs=[
+                pl.BlockSpec((total, 1), lambda s, _: (0, 0)),
+                pl.BlockSpec((2 * rank, total), lambda s, _: (0, 0)),
+                pl.BlockSpec((total, cell), lambda s, _: (0, chunk * sub + s)),
+                pl.BlockSpec((total, cell), lambda s, _: (0, chunk * sub + s)),
+                pl.BlockSpec((slots, 2, rank, cell), lambda s, _: (0, 0, 0, chunk * sub + s)),
+            ],
+            out_specs=[pl.BlockSpec((2, total // 2, cell), lambda s, _: (0, 0, s))] * 2,
+            scratch_shapes=[pltpu.VMEM((2, total, cell), F32)],
+        ),
+        out_shape=[piece, piece],
+        compiler_params=pltpu.CompilerParams(vmem_limit_bytes=40 << 20),
+        cost_estimate=pl.CostEstimate(
+            flops=4 * total * slots * rank * width,
+            bytes_accessed=4 * slots * rank * width + 16 * total * width,
+            transcendentals=0,
+        ),
+        name="lift",
+    )(side, slot_col, rank_t, gate_part, up_part, lift)
+
+
+def down_kernel(first, side_ref, slot_ref, near_ref, far_ref, down_ref, proj_ref, *rest):
+    if first:
+        sum_ref, rank_ref, hidden_ref = rest
+    else:
+        sum_in_ref, rank_in_ref, sum_ref, rank_ref, hidden_ref = rest
+    step = pl.program_id(0)
+    half = near_ref.shape[0]
+    side = side_ref[0]
+
+    @pl.when(step == 0)
+    def _():
+        hidden_ref[pl.ds(pl.multiple_of(side * half, 16), half), :] = near_ref[...]
+        hidden_ref[pl.ds(pl.multiple_of((1 - side) * half, 16), half), :] = far_ref[...]
+        rank_ref[...] = jnp.zeros_like(rank_ref) if first else rank_in_ref[...]
+
+    hidden = hidden_ref[...]
+    product = jnp.dot(hidden, down_ref[...], preferred_element_type=F32)
+    sum_ref[...] = product if first else product + sum_in_ref[...]
+    rank_ref[...] += masked_project(proj_ref[...], hidden, slot_ref[...], step * proj_ref.shape[0])
+
+
+def down_call(chunk, side, slot_row, near, far, down, proj, carried):
+    slots, rank, wide = proj.shape
+    half, width = near.shape
+    total = 2 * half
+    out = down.shape[1]
+    steps = 4
+    cell = out // steps
+    first = carried is None
+    in_specs = [
+        pl.BlockSpec((1, total), lambda s, _: (0, 0)),
+        pl.BlockSpec((half, width), lambda s, _: (0, 0)),
+        pl.BlockSpec((half, width), lambda s, _: (0, 0)),
+        pl.BlockSpec((width, cell), lambda s, _: (chunk, s)),
+        pl.BlockSpec((slots // steps, rank, width), lambda s, _: (s, 0, chunk)),
+    ]
+    out_specs = [
+        pl.BlockSpec((total, cell), lambda s, _: (0, s)),
+        pl.BlockSpec((rank, total), lambda s, _: (0, 0)),
+    ]
+    if not first:
+        in_specs += out_specs
+    return pl.pallas_call(
+        functools.partial(down_kernel, first),
+        grid_spec=pltpu.PrefetchScalarGridSpec(
+            num_scalar_prefetch=1,
+            grid=(steps,),
+            in_specs=in_specs,
+            out_specs=out_specs,
+            scratch_shapes=[pltpu.VMEM((total, width), BF16)],
+        ),
+        out_shape=[
+            jax.ShapeDtypeStruct((total, out), F32),
+            jax.ShapeDtypeStruct((rank, total), F32),
+        ],
+        compiler_params=pltpu.CompilerParams(vmem_limit_bytes=32 << 20),
+        cost_estimate=pl.CostEstimate(
+            flops=2 * total * width * (out + slots * rank),
+            bytes_accessed=2 * width * (out + slots * rank) + 8 * total * out,
+            transcendentals=0,
+        ),
+        name="down",
+    )(side, slot_row, near, far, down, proj, *(() if first else carried))
+
+
+def last_kernel(slot_ref, rank_ref, sum_ref, lift_ref, out_ref):
+    slots, rank, width = lift_ref.shape
+    spread = spread_rows(rank_ref[...], slot_ref[...], slots)
+    extra = jnp.dot(spread, lift_ref[...].reshape(slots * rank, width), preferred_element_type=F32)
+    out_ref[...] = (sum_ref[...] + extra).astype(BF16)
+
+
+def last_call(slot_col, rank_t, sums, lift):
+    slots, rank, out = lift.shape
+    total = sums.shape[0]
+    cell = out // 4
+    return pl.pallas_call(
+        last_kernel,
+        grid=(4,),
+        in_specs=[
+            pl.BlockSpec((total, 1), lambda s: (0, 0)),
+            pl.BlockSpec((rank, total), lambda s: (0, 0)),
+            pl.BlockSpec((total, cell), lambda s: (0, s)),
+            pl.BlockSpec((slots, rank, cell), lambda s: (0, 0, s)),
+        ],
+        out_specs=pl.BlockSpec((total, cell), lambda s: (0, s)),
+        out_shape=jax.ShapeDtypeStruct((total, out), BF16),
+        compiler_params=pltpu.CompilerParams(vmem_limit_bytes=32 << 20),
+        cost_estimate=pl.CostEstimate(
+            flops=2 * total * slots * rank * out,
+            bytes_accessed=2 * slots * rank * out + 6 * total * out,
+            transcendentals=0,
+        ),
+        name="last",
+    )(slot_col, rank_t, sums, lift)
+
+
+def swap(value, axis, size, mask):
+    return lax.ppermute(value, axis, [(i, i ^ mask) for i in range(size)])
+
+
+def sum_everywhere(value):
+    value = value + swap(value, "dp", 8, 1)
+    value = value + swap(value, "dp", 8, 2) + swap(value, "dp", 8, 4) + swap(value, "dp", 8, 6)
+    return value + swap(value, "tensor", 4, 1) + swap(value, "tensor", 4, 2) + swap(value, "tensor", 4, 3)
+
+
+def widen_sum(one, two):
+    return (one.astype(F32) + two.astype(F32)).astype(BF16)
+
+
+def scatter_dp(rows):
+    total, width = rows.shape
+    me = lax.axis_index("dp")
+    core = me % 2
+    blocks = rows.reshape(4, 2, total // 8, width)
+    mine = lax.dynamic_index_in_dim(blocks, core, 1, keepdims=False)
+    other = lax.dynamic_index_in_dim(blocks, 1 - core, 1, keepdims=False)
+    both = widen_sum(mine, swap(other, "dp", 8, 1))
+    chip = me // 2
+    kept = lax.dynamic_index_in_dim(both, chip, 0, keepdims=False).astype(F32)
+    for mask in (3, 1, 2):
+        sent = lax.dynamic_index_in_dim(both, chip ^ mask, 0, keepdims=False)
+        kept = kept + swap(sent, "dp", 8, 2 * mask).astype(F32)
+    return kept.astype(BF16)
+
+
+def line_device(
+    tokens,
+    gate_weight,
+    up_weight,
+    down_weight,
+    adapter_proj_in,
+    adapter_lift_in,
+    adapter_proj_out,
+    adapter_lift_out,
+    token_request,
+    request_adapter,
+    adapter_slot,
+):
+    slot_of = lookup(lookup(token_request, request_adapter), adapter_slot)
+    dp_index = lax.axis_index("dp")
+    tensor_index = lax.axis_index("tensor")
+    side = (tensor_index // 2).astype(jnp.int32).reshape(1)
+    is_end = (tensor_index == 0) | (tensor_index == 3)
+    slot_dp = slot_of - dp_index * adapter_proj_in.shape[0]
+    slot_tensor = slot_of - tensor_index * adapter_lift_in.shape[0]
+    gathered = lax.all_gather(tokens, "dp", axis=0, tiled=True)
+    rank_part = rank_in_call(slot_dp[None, :], gathered, adapter_proj_in)
+    gate_part = jnp.dot(gathered, gate_weight, preferred_element_type=F32)
+    up_part = jnp.dot(gathered, up_weight, preferred_element_type=F32)
+    rank_in = sum_everywhere(rank_part).astype(BF16)
+    carried = None
+    for chunk in range(CHUNKS):
+        near, far = lift_call(
+            chunk, side, slot_tensor[:, None], rank_in, gate_part, up_part, adapter_lift_in
+        )
+        arrived = lax.ppermute(far, "tensor", INWARD)
+        arrived = lax.ppermute(widen_sum(far, arrived), "tensor", MIDDLE)
+        near = widen_sum(near, arrived)
+        arrived = lax.ppermute(near, "tensor", OUTWARD)
+        gate = near[0].astype(F32) + arrived[0].astype(F32)
+        up = near[1].astype(F32) + arrived[1].astype(F32)
+        hidden = (jax.nn.silu(gate) * up).astype(BF16)
+        arrived = lax.ppermute(hidden, "tensor", INWARD)
+        hidden_near = jnp.where(is_end, hidden, arrived)
+        crossed = lax.ppermute(arrived, "tensor", MIDDLE)
+        returned = lax.ppermute(crossed, "tensor", OUTWARD)
+        hidden_far = jnp.where(is_end, returned, crossed)
+        carried = down_call(
+            chunk, side, slot_tensor[None, :], hidden_near, hidden_far, down_weight, adapter_proj_out, carried
+        )
+    sums, rank_part_out = carried
+    rank_out = sum_everywhere(rank_part_out).astype(BF16)
+    return scatter_dp(last_call(slot_dp[:, None], rank_out, sums, adapter_lift_out))
+
+
 def solution(mesh):
+    on_line = mesh.shape["tensor"] == 4 and mesh.shape["dp"] == 8
     placed = (
         P("dp", "tensor"),
         P("tensor", "dp"),
@@ -97,5 +392,5 @@
         P(),
     )
     return jax.shard_map(
-        per_device, mesh=mesh, in_specs=placed, out_specs=P("dp", "tensor"), check_vma=False
-    )
+        line_device if on_line else general_device, mesh=mesh, in_specs=placed, out_specs=P("dp", "tensor"), check_vma=False
+    )

time: 296 us -> 188 us (0.64)
  blocking collectives: 91.6 us -> 12.2 us
  waiting for transfers between devices: 123 us -> 55.1 us
  starting transfers between devices: 0.09 us -> 57.1 us
  matrix products: 62.2 us -> 12 us
  Pallas kernels: 0 us -> 35 us
  between operations: 13.2 us -> 0.83 us
  local copies, waits for them, and re-layouts: 0.01 us -> 8.64 us
    reduce_scatter x2 -> x0, waiting for transfers between devices: 89.5 us -> none  [the longest x1 54.7 us: per_device(): lax.psum_scatter((jnp.stack([gate_part, up_part], axis=1) + extra).astype...]
    psum x2 -> x0, blocking collectives: 79.4 us -> none  [the longest x1 39.7 us: per_device(): rank_in = lax.psum(rank_part, ('dp', 'tensor')).astype(jnp.bfloat16)]
    ppermute x0 -> x42, starting transfers between devices: none -> 57.1 us  [the longest x18 19.9 us: swap(): return lax.ppermute(value, axis, [(i, i ^ mask) for i in range(size)])]
    ppermute x0 -> x42, waiting for transfers between devices: none -> 55.1 us  [the longest x4 16.8 us: line_device(): arrived = lax.ppermute(near, 'tensor', OUTWARD)]
    dot_general x7 -> x2, matrix products: 62.2 us -> 12 us  [the longest x1 7.43 us: line_device(): gate_part = jnp.dot(gathered, gate_weight, preferred_element_type=F32)]
    pallas_call x0 -> x10, Pallas kernels: none -> 35 us  [the longest x4 16.9 us: down_call(): pl.pallas_call(functools.partial(down_kernel, first), grid_spec=pltpu.Pre...]
    all_gather x1 -> x0, waiting for transfers between devices: 33.7 us -> none  [per_device(): hidden_all = lax.all_gather(hidden, 'tensor', axis=0, tiled=True)]
    unnamed x2 -> x26, local copies, waits for them, and re-layouts: 0.01 us -> 8.35 us
  transfers between devices with their start and end apart: 3 -> 42, of which waited for: 3 -> 19; matrix products, arithmetic and copies ran while one was open for 0% -> 8% of each run, Pallas kernels for 0% -> 10%
where the time goes in v1:
time: 188 us; the launch traced here: 187 us
  starting transfers between devices  57.1 us (30%)
  waiting for transfers between devices  55.1 us (29%)
  Pallas kernels  35 us (19%)
  blocking collectives  12.2 us (6%)
  matrix products  12 us (6%)
  local copies, waits for them, and re-layouts  8.64 us (5%)
  other arithmetic  6.39 us (3%)
    ppermute x18, starting transfers between devices, swap(): return lax.ppermute(value, axis, [(i, i ^ mask) for i in range(size)])  19.9 us
    pallas_call x4, Pallas kernels, down_call(): pl.pallas_call(functools.partial(down_kernel, first), grid_spec=pltpu.Pre...  16.9 us
    ppermute x4, waiting for transfers between devices, line_device(): arrived = lax.ppermute(near, 'tensor', OUTWARD)  16.8 us
    ppermute x4, waiting for transfers between devices, line_device(): returned = lax.ppermute(crossed, 'tensor', OUTWARD)  15 us
    pallas_call x4, Pallas kernels, lift_call(): pl.pallas_call(lift_kernel, grid_spec=pltpu.PrefetchScalarGridSpec(num_sc...  14.1 us
    ppermute x18, waiting for transfers between devices, swap(): return lax.ppermute(value, axis, [(i, i ^ mask) for i in range(size)])  13.8 us
    ppermute x4, starting transfers between devices, line_device(): arrived = lax.ppermute(hidden, 'tensor', INWARD)  12.9 us
    all_gather x1, blocking collectives, line_device(): gathered = lax.all_gather(tokens, 'dp', axis=0, tiled=True)  12.2 us
  transfers between devices with their start and end apart: 42, of which 19 were waited for; matrix products, arithmetic and copies ran while one was open for 8% of the time, Pallas kernels for 10%

profile of v1, /device:TPU:0, one launch (start us, length us, event | category | flops | bytes accessed | tf_op | source)
XLA Modules:
  0.0 187.1 jit_solution(4889322440360686373)
XLA Ops:
  0.0 12.2 %all_gather.3.rows_ref = bf16[192,2048]{1,0:T(8,128)(2,1)S(1)} all-gather(bf16[24,2048]{1,0:T(8,128)(2,1)} %param.11), channel_id=1, replica_groups=mesh['dp'=8,'tensor'=4] {'dp'}, dimensions={0}, use_global_device_ids=true | all-gather | bytes 884736 | tf_op jit(solution)/shard_map/all_gather | solution.py:349
  13.9 2.2 %copy-done.2 = bf16[32,32,2048]{2,1,0:T(8,128)(2,1)S(1)} copy-done((bf16[32,32,2048]{2,1,0:T(8,128)(2,1)S(1)}, bf16[32,32,2048]{2,1,0:T(8,128)(2,1)}, u32[]{:S(2)}) %copy-start.2) | copy-done | bytes 4194328
  22.8 7.4 %fusion.20.gate_ref = f32[192,3584]{1,0:T(8,128)S(1)} fusion(bf16[192,2048]{1,0:T(8,128)(2,1)S(1)} %all_gather.3.rows_ref, bf16[2048,3584]{1,0:T(8,128)(2,1)} %param.12), kind=kOutput, calls=%fused_computation.64 | convolution fusion | flops 2818572288 | bytes 18219008 | tf_op jit(solution)/shard_map/dot_general | solution.py:351
  30.9 3.6 %collective-permute-start.6 = (f32[32,192]{1,0:T(8,128)}, f32[32,192]{1,0:T(8,128)}, u32[]{:S(2)}, u32[]{:S(2)}) collective-permute-start(f32[32,192]{1,0:T(8,128)} %add_add_fusion), channel_id=1, source_target_pairs={{0,3},{1,2},{2,1},{3,0},{4,7},{5,6},{6,5},{7,4},{8,11},{9,10},{10,... | collective-permute-start | bytes 73736 | tf_op jit(solution)/shard_map/ppermute | solution.py:300
  35.3 4.6 %fusion.21.up_ref = f32[192,3584]{1,0:T(8,128)} fusion(bf16[192,2048]{1,0:T(8,128)(2,1)S(1)} %all_gather.3.rows_ref, bf16[2048,3584]{1,0:T(8,128)(2,1)S(1)} %copy-done.10), kind=kOutput, calls=%fused_computation.65 | convolution fusion | flops 2818572288 | bytes 18219008 | tf_op jit(solution)/shard_map/dot_general | solution.py:352
  42.6 3.5 %lift.4 = (bf16[2,96,896]{2,1,0:T(8,128)(2,1)S(1)}, bf16[2,96,896]{2,1,0:T(8,128)(2,1)S(1)}) custom-call(s32[1]{0:T(128)} %bitcast.1.side_ref, s32[192,1]{1,0:T(8,128)S(1)} %copy.19.slot_ref, bf16[32,192]{1,0:T(8,128)(2,1)S(1)} %add_convert_fusion.8.rank_ref, f32[192,3584]{1,0:T(8,128)S(1)} %fusion.20.gate_ref, f32[192,3584]{1,0:T(8,128)S(1)} %copy-done, ...), custom_call_target="tpu_custom_call" | custom-call | flops 704643072 | bytes 6422528 | tf_op jit(solution)/shard_map/lift/pallas_call | solution.py:176
  46.1 3.9 %collective-permute-start.7 = (bf16[2,96,896]{2,1,0:T(8,128)(2,1)S(1)}, bf16[2,96,896]{2,1,0:T(8,128)(2,1)}, u32[]{:S(2)}, u32[]{:S(2)}) collective-permute-start(bf16[2,96,896]{2,1,0:T(8,128)(2,1)S(1)} %get-tuple-element.22), channel_id=1, source_target_pairs={{0,1},{3,2},{4,5},{7,6},{8,9},{11,10},{12,13},{15,14},{16,17},{19,... | collective-permute-start | bytes 1032200 | tf_op jit(solution)/shard_map/ppermute | solution.py:359
  51.8 3.5 %lift.5 = (bf16[2,96,896]{2,1,0:T(8,128)(2,1)S(1)}, bf16[2,96,896]{2,1,0:T(8,128)(2,1)S(1)}) custom-call(s32[1]{0:T(128)} %bitcast.1.side_ref, s32[192,1]{1,0:T(8,128)S(1)} %copy.19.slot_ref, bf16[32,192]{1,0:T(8,128)(2,1)S(1)} %add_convert_fusion.8.rank_ref, f32[192,3584]{1,0:T(8,128)S(1)} %fusion.20.gate_ref, f32[192,3584]{1,0:T(8,128)S(1)} %copy-done.1, ...), custom_call_target="tpu_custom_call" | custom-call | flops 704643072 | bytes 6422528 | tf_op jit(solution)/shard_map/lift/pallas_call | solution.py:176
  56.7 3.5 %lift.6 = (bf16[2,96,896]{2,1,0:T(8,128)(2,1)S(1)}, bf16[2,96,896]{2,1,0:T(8,128)(2,1)S(1)}) custom-call(s32[1]{0:T(128)} %bitcast.1.side_ref, s32[192,1]{1,0:T(8,128)S(1)} %copy.19.slot_ref, bf16[32,192]{1,0:T(8,128)(2,1)S(1)} %add_convert_fusion.8.rank_ref, f32[192,3584]{1,0:T(8,128)S(1)} %fusion.20.gate_ref, f32[192,3584]{1,0:T(8,128)S(1)} %copy-done.1, ...), custom_call_target="tpu_custom_call" | custom-call | flops 704643072 | bytes 6422528 | tf_op jit(solution)/shard_map/lift/pallas_call | solution.py:176
  61.5 3.5 %lift.7 = (bf16[2,96,896]{2,1,0:T(8,128)(2,1)S(1)}, bf16[2,96,896]{2,1,0:T(8,128)(2,1)S(1)}) custom-call(s32[1]{0:T(128)} %bitcast.1.side_ref, s32[192,1]{1,0:T(8,128)S(1)} %copy.19.slot_ref, bf16[32,192]{1,0:T(8,128)(2,1)S(1)} %add_convert_fusion.8.rank_ref, f32[192,3584]{1,0:T(8,128)S(1)} %fusion.20.gate_ref, f32[192,3584]{1,0:T(8,128)S(1)} %copy-done.1, ...), custom_call_target="tpu_custom_call" | custom-call | flops 704643072 | bytes 6422528 | tf_op jit(solution)/shard_map/lift/pallas_call | solution.py:176
  69.2 3.3 %collective-permute-done.19 = bf16[2,96,896]{2,1,0:T(8,128)(2,1)S(1)} collective-permute-done((bf16[2,96,896]{2,1,0:T(8,128)(2,1)S(1)}, bf16[2,96,896]{2,1,0:T(8,128)(2,1)S(1)}, u32[]{:S(2)}, u32[]{:S(2)}) %collective-permute-start.19) | collective-permute-done | bytes 344096 | tf_op jit(solution)/shard_map/ppermute | solution.py:359
  73.3 4.7 %collective-permute-done.25 = bf16[2,96,896]{2,1,0:T(8,128)(2,1)S(1)} collective-permute-done((bf16[2,96,896]{2,1,0:T(8,128)(2,1)S(1)}, bf16[2,96,896]{2,1,0:T(8,128)(2,1)S(1)}, u32[]{:S(2)}, u32[]{:S(2)}) %collective-permute-start.25) | collective-permute-done | bytes 344096 | tf_op jit(solution)/shard_map/ppermute | solution.py:359
  84.8 9.4 %collective-permute-done.9 = bf16[2,96,896]{2,1,0:T(8,128)(2,1)S(1)} collective-permute-done((bf16[2,96,896]{2,1,0:T(8,128)(2,1)S(1)}, bf16[2,96,896]{2,1,0:T(8,128)(2,1)S(1)}, u32[]{:S(2)}, u32[]{:S(2)}) %collective-permute-start.9) | collective-permute-done | bytes 344096 | tf_op jit(solution)/shard_map/ppermute | solution.py:362
  94.4 8.7 %collective-permute-start.10 = (bf16[96,896]{1,0:T(8,128)(2,1)S(1)}, bf16[96,896]{1,0:T(8,128)(2,1)S(1)}, u32[]{:S(2)}, u32[]{:S(2)}) collective-permute-start(bf16[96,896]{1,0:T(8,128)(2,1)S(1)} %fusion.13), channel_id=1, source_target_pairs={{0,1},{3,2},{4,5},{7,6},{8,9},{11,10},{12,13},{15,14},{16,17},{19,... | collective-permute-start | bytes 516104 | tf_op jit(solution)/shard_map/ppermute | solution.py:366
  104.6 4.4 %collective-permute-done.21 = bf16[2,96,896]{2,1,0:T(8,128)(2,1)S(1)} collective-permute-done((bf16[2,96,896]{2,1,0:T(8,128)(2,1)S(1)}, bf16[2,96,896]{2,1,0:T(8,128)(2,1)S(1)}, u32[]{:S(2)}, u32[]{:S(2)}) %collective-permute-start.21) | collective-permute-done | bytes 344096 | tf_op jit(solution)/shard_map/ppermute | solution.py:362
  110.6 2.9 %collective-permute-done.27 = bf16[2,96,896]{2,1,0:T(8,128)(2,1)S(1)} collective-permute-done((bf16[2,96,896]{2,1,0:T(8,128)(2,1)S(1)}, bf16[2,96,896]{2,1,0:T(8,128)(2,1)S(1)}, u32[]{:S(2)}, u32[]{:S(2)}) %collective-permute-start.27) | collective-permute-done | bytes 344096 | tf_op jit(solution)/shard_map/ppermute | solution.py:362
  124.7 11.3 %collective-permute-done.30 = bf16[96,896]{1,0:T(8,128)(2,1)S(1)} collective-permute-done((bf16[96,896]{1,0:T(8,128)(2,1)S(1)}, bf16[96,896]{1,0:T(8,128)(2,1)S(1)}, u32[]{:S(2)}, u32[]{:S(2)}) %collective-permute-start.30) | collective-permute-done | bytes 172064 | tf_op jit(solution)/shard_map/ppermute | solution.py:369
  136.0 3.7 %collective-permute-done.24 = bf16[96,896]{1,0:T(8,128)(2,1)S(1)} collective-permute-done((bf16[96,896]{1,0:T(8,128)(2,1)S(1)}, bf16[96,896]{1,0:T(8,128)(2,1)S(1)}, u32[]{:S(2)}, u32[]{:S(2)}) %collective-permute-start.24) | collective-permute-done | bytes 172064 | tf_op jit(solution)/shard_map/ppermute | solution.py:369
  139.8 4.2 %down.4 = (f32[192,2048]{1,0:T(8,128)S(1)}, f32[16,192]{1,0:T(8,128)S(1)}) custom-call(s32[1]{0:T(128)} %bitcast.1.side_ref, s32[1,192]{1,0:T(1,128)S(1)} %bitcast.99, bf16[96,896]{1,0:T(8,128)(2,1)S(1)} %broadcast_select_fusion.1.near_ref, bf16[96,896]{1,0:T(8,128)(2,1)S(1)} %get-tuple-element.42.far_ref, bf16[3584,2048]{1,0:T(8,128)(2,1)} %down_ref.7, ...), custom_call_target="tpu_custom_call" | custom-call | flops 1056964608 | bytes 8650752 | tf_op jit(solution)/shard_map/down/pallas_call | solution.py:244
  144.0 4.2 %down.5 = (f32[192,2048]{1,0:T(8,128)S(1)}, f32[16,192]{1,0:T(8,128)S(1)}) custom-call(s32[1]{0:T(128)} %bitcast.1.side_ref, s32[1,192]{1,0:T(1,128)S(1)} %bitcast.100, bf16[96,896]{1,0:T(8,128)(2,1)S(1)} %broadcast_select_fusion.3.near_ref, bf16[96,896]{1,0:T(8,128)(2,1)S(1)} %get-tuple-element.43.far_ref, bf16[3584,2048]{1,0:T(8,128)(2,1)} %down_ref.7, ...), custom_call_target="tpu_custom_call" | custom-call | flops 1056964608 | bytes 8650752 | tf_op jit(solution)/shard_map/down/pallas_call | solution.py:244
  148.3 4.2 %down.6 = (f32[192,2048]{1,0:T(8,128)S(1)}, f32[16,192]{1,0:T(8,128)S(1)}) custom-call(s32[1]{0:T(128)} %bitcast.1.side_ref, s32[1,192]{1,0:T(1,128)S(1)} %bitcast.101, bf16[96,896]{1,0:T(8,128)(2,1)S(1)} %broadcast_select_fusion.5.near_ref, bf16[96,896]{1,0:T(8,128)(2,1)S(1)} %get-tuple-element.44.far_ref, bf16[3584,2048]{1,0:T(8,128)(2,1)} %down_ref.7, ...), custom_call_target="tpu_custom_call" | custom-call | flops 1056964608 | bytes 8650752 | tf_op jit(solution)/shard_map/down/pallas_call | solution.py:244
  152.5 4.3 %down.7 = (f32[192,2048]{1,0:T(8,128)S(1)}, f32[16,192]{1,0:T(8,128)S(1)}) custom-call(s32[1]{0:T(128)} %bitcast.1.side_ref, s32[1,192]{1,0:T(1,128)S(1)} %bitcast.102, bf16[96,896]{1,0:T(8,128)(2,1)S(1)} %broadcast_select_fusion.7.near_ref, bf16[96,896]{1,0:T(8,128)(2,1)S(1)} %get-tuple-element.45.far_ref, bf16[3584,2048]{1,0:T(8,128)(2,1)} %down_ref.7, ...), custom_call_target="tpu_custom_call" | custom-call | flops 1056964608 | bytes 8650752 | tf_op jit(solution)/shard_map/down/pallas_call | solution.py:244
  165.6 2.4 %collective-permute-start.37 = (f32[16,192]{1,0:T(8,128)S(1)}, f32[16,192]{1,0:T(8,128)S(1)}, u32[]{:S(2)}, u32[]{:S(2)}) collective-permute-start(f32[16,192]{1,0:T(8,128)S(1)} %add_add_fusion.1), channel_id=1, source_target_pairs={{0,3},{1,2},{2,1},{3,0},{4,7},{5,6},{6,5},{7,4},{8,11},{9,10},{10,... | collective-permute-start | bytes 36872 | tf_op jit(solution)/shard_map/ppermute | solution.py:300
  174.1 2.2 %last.1 = bf16[192,2048]{1,0:T(8,128)(2,1)S(1)} custom-call(s32[192,1]{1,0:T(8,128)S(1)} %copy.23.slot_ref, bf16[16,192]{1,0:T(8,128)(2,1)S(1)} %add_convert_fusion.9.rank_ref, f32[192,2048]{1,0:T(8,128)S(1)} %copy-done.5, bf16[32,16,2048]{2,1,0:T(8,128)(2,1)S(1)} %copy-done.3), custom_call_target="tpu_custom_call" | custom-call | flops 402653184 | bytes 4456448 | tf_op jit(solution)/shard_map/last/pallas_call | solution.py:278
  (133 shorter events, 68.5 us)
Async XLA Ops:
  19.2 11.0 %collective-permute-start.3 = (f32[32,192]{1,0:T(8,128)S(1)}, f32[32,192]{1,0:T(8,128)S(1)}, u32[]{:S(2)}, u32[]{:S(2)}) collective-permute-start(f32[32,192]{1,0:T(8,128)S(1)} %add.166), channel_id=1, source_target_pairs={{0,24},{4,28},{8,16},{12,20},{16,8},{20,12},{24,0},{28,4},{1,25},{... | collective-permute-start | bytes 73736 | tf_op jit(solution)/shard_map/ppermute | solution.py:300
  20.8 9.5 %collective-permute-start.2 = (f32[32,192]{1,0:T(8,128)S(1)}, f32[32,192]{1,0:T(8,128)S(1)}, u32[]{:S(2)}, u32[]{:S(2)}) collective-permute-start(f32[32,192]{1,0:T(8,128)S(1)} %add.166), channel_id=1, source_target_pairs={{0,16},{4,20},{8,24},{12,28},{16,0},{20,4},{24,8},{28,12},{1,17},{... | collective-permute-start | bytes 73736 | tf_op jit(solution)/shard_map/ppermute | solution.py:300
  21.9 8.3 %collective-permute-start.1 = (f32[32,192]{1,0:T(8,128)S(1)}, f32[32,192]{1,0:T(8,128)S(1)}, u32[]{:S(2)}, u32[]{:S(2)}) collective-permute-start(f32[32,192]{1,0:T(8,128)S(1)} %add.166), channel_id=1, source_target_pairs={{0,8},{4,12},{8,0},{12,4},{16,24},{20,28},{24,16},{28,20},{1,9},{5... | collective-permute-start | bytes 73736 | tf_op jit(solution)/shard_map/ppermute | solution.py:300
  30.9 9.1 %collective-permute-start.6 = (f32[32,192]{1,0:T(8,128)}, f32[32,192]{1,0:T(8,128)}, u32[]{:S(2)}, u32[]{:S(2)}) collective-permute-start(f32[32,192]{1,0:T(8,128)} %add_add_fusion), channel_id=1, source_target_pairs={{0,3},{1,2},{2,1},{3,0},{4,7},{5,6},{6,5},{7,4},{8,11},{9,10},{10,... | collective-permute-start | bytes 73736 | tf_op jit(solution)/shard_map/ppermute | solution.py:300
  46.1 20.5 %collective-permute-start.7 = (bf16[2,96,896]{2,1,0:T(8,128)(2,1)S(1)}, bf16[2,96,896]{2,1,0:T(8,128)(2,1)}, u32[]{:S(2)}, u32[]{:S(2)}) collective-permute-start(bf16[2,96,896]{2,1,0:T(8,128)(2,1)S(1)} %get-tuple-element.22), channel_id=1, source_target_pairs={{0,1},{3,2},{4,5},{7,6},{8,9},{11,10},{12,13},{15,14},{16,17},{19,... | collective-permute-start | bytes 1032200 | tf_op jit(solution)/shard_map/ppermute | solution.py:359
  55.3 13.1 %collective-permute-start.13 = (bf16[2,96,896]{2,1,0:T(8,128)(2,1)S(1)}, bf16[2,96,896]{2,1,0:T(8,128)(2,1)S(1)}, u32[]{:S(2)}, u32[]{:S(2)}) collective-permute-start(bf16[2,96,896]{2,1,0:T(8,128)(2,1)S(1)} %get-tuple-element.24), channel_id=1, source_target_pairs={{0,1},{3,2},{4,5},{7,6},{8,9},{11,10},{12,13},{15,14},{16,17},{19,... | collective-permute-start | bytes 1032200 | tf_op jit(solution)/shard_map/ppermute | solution.py:359
  60.2 12.3 %collective-permute-start.19 = (bf16[2,96,896]{2,1,0:T(8,128)(2,1)S(1)}, bf16[2,96,896]{2,1,0:T(8,128)(2,1)S(1)}, u32[]{:S(2)}, u32[]{:S(2)}) collective-permute-start(bf16[2,96,896]{2,1,0:T(8,128)(2,1)S(1)} %get-tuple-element.26), channel_id=1, source_target_pairs={{0,1},{3,2},{4,5},{7,6},{8,9},{11,10},{12,13},{15,14},{16,17},{19,... | collective-permute-start | bytes 1032200 | tf_op jit(solution)/shard_map/ppermute | solution.py:359
  65.0 12.9 %collective-permute-start.25 = (bf16[2,96,896]{2,1,0:T(8,128)(2,1)S(1)}, bf16[2,96,896]{2,1,0:T(8,128)(2,1)S(1)}, u32[]{:S(2)}, u32[]{:S(2)}) collective-permute-start(bf16[2,96,896]{2,1,0:T(8,128)(2,1)S(1)} %get-tuple-element.28), channel_id=1, source_target_pairs={{0,1},{3,2},{4,5},{7,6},{8,9},{11,10},{12,13},{15,14},{16,17},{19,... | collective-permute-start | bytes 1032200 | tf_op jit(solution)/shard_map/ppermute | solution.py:359
  67.7 11.0 %collective-permute-start.8 = (bf16[2,96,896]{2,1,0:T(8,128)(2,1)S(1)}, bf16[2,96,896]{2,1,0:T(8,128)(2,1)S(1)}, u32[]{:S(2)}, u32[]{:S(2)}) collective-permute-start(bf16[2,96,896]{2,1,0:T(8,128)(2,1)S(1)} %add_convert_fusion.7), channel_id=1, source_target_pairs={{1,2},{2,1},{5,6},{6,5},{9,10},{10,9},{13,14},{14,13},{17,18},{18,... | collective-permute-start | bytes 1032200 | tf_op jit(solution)/shard_map/ppermute | solution.py:360
  68.5 11.7 %collective-permute-start.14 = (bf16[2,96,896]{2,1,0:T(8,128)(2,1)S(1)}, bf16[2,96,896]{2,1,0:T(8,128)(2,1)S(1)}, u32[]{:S(2)}, u32[]{:S(2)}) collective-permute-start(bf16[2,96,896]{2,1,0:T(8,128)(2,1)S(1)} %add_convert_fusion.5), channel_id=1, source_target_pairs={{1,2},{2,1},{5,6},{6,5},{9,10},{10,9},{13,14},{14,13},{17,18},{18,... | collective-permute-start | bytes 1032200 | tf_op jit(solution)/shard_map/ppermute | solution.py:360
  72.6 9.1 %collective-permute-start.20 = (bf16[2,96,896]{2,1,0:T(8,128)(2,1)S(1)}, bf16[2,96,896]{2,1,0:T(8,128)(2,1)S(1)}, u32[]{:S(2)}, u32[]{:S(2)}) collective-permute-start(bf16[2,96,896]{2,1,0:T(8,128)(2,1)S(1)} %add_convert_fusion.3), channel_id=1, source_target_pairs={{1,2},{2,1},{5,6},{6,5},{9,10},{10,9},{13,14},{14,13},{17,18},{18,... | collective-permute-start | bytes 1032200 | tf_op jit(solution)/shard_map/ppermute | solution.py:360
  78.8 15.4 %collective-permute-start.9 = (bf16[2,96,896]{2,1,0:T(8,128)(2,1)S(1)}, bf16[2,96,896]{2,1,0:T(8,128)(2,1)S(1)}, u32[]{:S(2)}, u32[]{:S(2)}) collective-permute-start(bf16[2,96,896]{2,1,0:T(8,128)(2,1)S(1)} %add_convert_fusion.6), channel_id=1, source_target_pairs={{1,0},{2,3},{5,4},{6,7},{9,8},{10,11},{13,12},{14,15},{17,16},{18,... | collective-permute-start | bytes 1032200 | tf_op jit(solution)/shard_map/ppermute | solution.py:362
  80.2 22.9 %collective-permute-start.15 = (bf16[2,96,896]{2,1,0:T(8,128)(2,1)S(1)}, bf16[2,96,896]{2,1,0:T(8,128)(2,1)S(1)}, u32[]{:S(2)}, u32[]{:S(2)}) collective-permute-start(bf16[2,96,896]{2,1,0:T(8,128)(2,1)S(1)} %add_convert_fusion.4), channel_id=1, source_target_pairs={{1,0},{2,3},{5,4},{6,7},{9,8},{10,11},{13,12},{14,15},{17,16},{18,... | collective-permute-start | bytes 1032200 | tf_op jit(solution)/shard_map/ppermute | solution.py:362
  81.8 27.2 %collective-permute-start.21 = (bf16[2,96,896]{2,1,0:T(8,128)(2,1)S(1)}, bf16[2,96,896]{2,1,0:T(8,128)(2,1)S(1)}, u32[]{:S(2)}, u32[]{:S(2)}) collective-permute-start(bf16[2,96,896]{2,1,0:T(8,128)(2,1)S(1)} %add_convert_fusion.2), channel_id=1, source_target_pairs={{1,0},{2,3},{5,4},{6,7},{9,8},{10,11},{13,12},{14,15},{17,16},{18,... | collective-permute-start | bytes 1032200 | tf_op jit(solution)/shard_map/ppermute | solution.py:362
  83.2 30.3 %collective-permute-start.27 = (bf16[2,96,896]{2,1,0:T(8,128)(2,1)S(1)}, bf16[2,96,896]{2,1,0:T(8,128)(2,1)S(1)}, u32[]{:S(2)}, u32[]{:S(2)}) collective-permute-start(bf16[2,96,896]{2,1,0:T(8,128)(2,1)S(1)} %add_convert_fusion), channel_id=1, source_target_pairs={{1,0},{2,3},{5,4},{6,7},{9,8},{10,11},{13,12},{14,15},{17,16},{18,... | collective-permute-start | bytes 1032200 | tf_op jit(solution)/shard_map/ppermute | solution.py:362
  94.4 21.4 %collective-permute-start.10 = (bf16[96,896]{1,0:T(8,128)(2,1)S(1)}, bf16[96,896]{1,0:T(8,128)(2,1)S(1)}, u32[]{:S(2)}, u32[]{:S(2)}) collective-permute-start(bf16[96,896]{1,0:T(8,128)(2,1)S(1)} %fusion.13), channel_id=1, source_target_pairs={{0,1},{3,2},{4,5},{7,6},{8,9},{11,10},{12,13},{15,14},{16,17},{19,... | collective-permute-start | bytes 516104 | tf_op jit(solution)/shard_map/ppermute | solution.py:366
  103.3 11.9 %collective-permute-start.16 = (bf16[96,896]{1,0:T(8,128)(2,1)S(1)}, bf16[96,896]{1,0:T(8,128)(2,1)S(1)}, u32[]{:S(2)}, u32[]{:S(2)}) collective-permute-start(bf16[96,896]{1,0:T(8,128)(2,1)S(1)} %fusion.9), channel_id=1, source_target_pairs={{0,1},{3,2},{4,5},{7,6},{8,9},{11,10},{12,13},{15,14},{16,17},{19,... | collective-permute-start | bytes 516104 | tf_op jit(solution)/shard_map/ppermute | solution.py:366
  109.2 9.6 %collective-permute-start.22 = (bf16[96,896]{1,0:T(8,128)(2,1)S(1)}, bf16[96,896]{1,0:T(8,128)(2,1)S(1)}, u32[]{:S(2)}, u32[]{:S(2)}) collective-permute-start(bf16[96,896]{1,0:T(8,128)(2,1)S(1)} %fusion.5), channel_id=1, source_target_pairs={{0,1},{3,2},{4,5},{7,6},{8,9},{11,10},{12,13},{15,14},{16,17},{19,... | collective-permute-start | bytes 516104 | tf_op jit(solution)/shard_map/ppermute | solution.py:366
  115.2 7.0 %collective-permute-start.17 = (bf16[96,896]{1,0:T(8,128)(2,1)S(1)}, bf16[96,896]{1,0:T(8,128)(2,1)S(1)}, u32[]{:S(2)}, u32[]{:S(2)}) collective-permute-start(bf16[96,896]{1,0:T(8,128)(2,1)S(1)} %collective-permute-done.16), channel_id=1, source_target_pairs={{1,2},{2,1},{5,6},{6,5},{9,10},{10,9},{13,14},{14,13},{17,18},{18,... | collective-permute-start | bytes 516104 | tf_op jit(solution)/shard_map/ppermute | solution.py:368
  115.9 7.6 %collective-permute-start.11 = (bf16[96,896]{1,0:T(8,128)(2,1)S(1)}, bf16[96,896]{1,0:T(8,128)(2,1)S(1)}, u32[]{:S(2)}, u32[]{:S(2)}) collective-permute-start(bf16[96,896]{1,0:T(8,128)(2,1)S(1)} %collective-permute-done.10), channel_id=1, source_target_pairs={{1,2},{2,1},{5,6},{6,5},{9,10},{10,9},{13,14},{14,13},{17,18},{18,... | collective-permute-start | bytes 516104 | tf_op jit(solution)/shard_map/ppermute | solution.py:368
  119.5 16.6 %collective-permute-start.30 = (bf16[96,896]{1,0:T(8,128)(2,1)S(1)}, bf16[96,896]{1,0:T(8,128)(2,1)S(1)}, u32[]{:S(2)}, u32[]{:S(2)}) collective-permute-start(bf16[96,896]{1,0:T(8,128)(2,1)S(1)} %collective-permute-done.29), channel_id=1, source_target_pairs={{1,0},{2,3},{5,4},{6,7},{9,8},{10,11},{13,12},{14,15},{17,16},{18,... | collective-permute-start | bytes 516104 | tf_op jit(solution)/shard_map/ppermute | solution.py:369
  120.8 18.9 %collective-permute-start.24 = (bf16[96,896]{1,0:T(8,128)(2,1)S(1)}, bf16[96,896]{1,0:T(8,128)(2,1)S(1)}, u32[]{:S(2)}, u32[]{:S(2)}) collective-permute-start(bf16[96,896]{1,0:T(8,128)(2,1)S(1)} %collective-permute-done.23), channel_id=1, source_target_pairs={{1,0},{2,3},{5,4},{6,7},{9,8},{10,11},{13,12},{14,15},{17,16},{18,... | collective-permute-start | bytes 516104 | tf_op jit(solution)/shard_map/ppermute | solution.py:369
  122.1 26.1 %collective-permute-start.18 = (bf16[96,896]{1,0:T(8,128)(2,1)S(1)}, bf16[96,896]{1,0:T(8,128)(2,1)S(1)}, u32[]{:S(2)}, u32[]{:S(2)}) collective-permute-start(bf16[96,896]{1,0:T(8,128)(2,1)S(1)} %collective-permute-done.17), channel_id=1, source_target_pairs={{1,0},{2,3},{5,4},{6,7},{9,8},{10,11},{13,12},{14,15},{17,16},{18,... | collective-permute-start | bytes 516104 | tf_op jit(solution)/shard_map/ppermute | solution.py:369
  123.4 24.8 %collective-permute-start.12 = (bf16[96,896]{1,0:T(8,128)(2,1)S(1)}, bf16[96,896]{1,0:T(8,128)(2,1)S(1)}, u32[]{:S(2)}, u32[]{:S(2)}) collective-permute-start(bf16[96,896]{1,0:T(8,128)(2,1)S(1)} %collective-permute-done.11), channel_id=1, source_target_pairs={{1,0},{2,3},{5,4},{6,7},{9,8},{10,11},{13,12},{14,15},{17,16},{18,... | collective-permute-start | bytes 516104 | tf_op jit(solution)/shard_map/ppermute | solution.py:369
  (31 other events, 382.3 us)

commit v2 on v0

--- a/solution.py
+++ b/solution.py
@@ -1,7 +1,19 @@
+import functools
+
 import jax
 import jax.numpy as jnp
 from jax import lax
+from jax.experimental import pallas as pl
+from jax.experimental.pallas import tpu as pltpu
 from jax.sharding import PartitionSpec as P
+
+CELL = 256
+DOWN_CELL = 512
+CHUNKS = (4, 5, 5)
+VMEM_LIMIT = 40 << 20
+LIGHT = pl.CostEstimate(flops=1024, bytes_accessed=1024, transcendentals=0)
+F32 = jnp.float32
+BF16 = jnp.bfloat16
 
 
 def lookup(keys, table):
@@ -14,7 +26,7 @@
     return (slot_of[:, None] == places[None, :]).astype(jnp.bfloat16)
 
 
-def per_device(
+def general_device(
     tokens,
     gate_weight,
     up_weight,
@@ -82,7 +94,460 @@
     )
 
 
+OUTER = [(0, 1), (1, 0), (2, 3), (3, 2)]
+MIDDLE = [(1, 2), (2, 1)]
+
+
+def masked_project(block, rows, slot_row, first):
+    slots, rank, depth = block.shape
+    full = lax.dot_general(
+        block.reshape(slots * rank, depth), rows, (((1,), (1,)), ((), ())), preferred_element_type=F32
+    ).reshape(slots, rank, rows.shape[0])
+    ids = first + lax.broadcasted_iota(jnp.int32, full.shape, 0)
+    return jnp.sum(jnp.where(ids == slot_row[None], full, 0.0), axis=0)
+
+
+def spread_rows(rank_t, slot_col, slots):
+    rank = rank_t.shape[0]
+    width = slots * rank
+    lane = lax.broadcasted_iota(jnp.int32, (rank, width), 1)
+    row = lax.broadcasted_iota(jnp.int32, (rank, width), 0)
+    copies = (lax.rem(lane, rank) == row).astype(F32).astype(BF16)
+    tiled = lax.dot_general(
+        rank_t.astype(F32).T.astype(BF16), copies, (((1,), (0,)), ((), ())), preferred_element_type=F32
+    )
+    owner = lax.div(lax.broadcasted_iota(jnp.int32, tiled.shape, 1), rank)
+    return jnp.where(owner == slot_col, tiled, 0.0).astype(BF16)
+
+
+def rank_in_kernel(slot_ref, rows_ref, proj_ref, out_ref):
+    step = pl.program_id(0)
+    part = masked_project(proj_ref[...], rows_ref[...], slot_ref[...], step * proj_ref.shape[0])
+
+    @pl.when(step == 0)
+    def _():
+        out_ref[...] = part
+
+    @pl.when(step > 0)
+    def _():
+        out_ref[...] += part
+
+
+def rank_in_call(slot_row, rows, proj):
+    slots, rank, depth = proj.shape
+    total = rows.shape[0]
+    group = 8
+    return pl.pallas_call(
+        rank_in_kernel,
+        grid=(slots // group,),
+        in_specs=[
+            pl.BlockSpec((1, total), lambda s: (0, 0)),
+            pl.BlockSpec((total, depth), lambda s: (0, 0)),
+            pl.BlockSpec((group, rank, depth), lambda s: (s, 0, 0)),
+        ],
+        out_specs=pl.BlockSpec((rank, total), lambda s: (0, 0)),
+        out_shape=jax.ShapeDtypeStruct((rank, total), F32),
+        compiler_params=pltpu.CompilerParams(vmem_limit_bytes=VMEM_LIMIT),
+        cost_estimate=LIGHT,
+        name="rank_in",
+    )(slot_row, rows, proj)
+
+
+def half_rows(side, which, half):
+    start = side * half if which == 0 else (1 - side) * half
+    return pl.ds(pl.multiple_of(start, 16), half)
+
+
+def main_kernel(rows_ref, gate_ref, up_ref, out_ref):
+    for c, main_ref in ((0, gate_ref), (1, up_ref)):
+        out_ref[c] = jnp.dot(rows_ref[...], main_ref[...], preferred_element_type=F32)
+
+
+def main_call(first, cells, rows, gate_weight, up_weight):
+    total, depth = rows.shape
+    weight = pl.BlockSpec((depth, CELL), lambda s: (0, first + s))
+    return pl.pallas_call(
+        main_kernel,
+        grid=(cells,),
+        in_specs=[pl.BlockSpec((total, depth), lambda s: (0, 0)), weight, weight],
+        out_specs=pl.BlockSpec((2, total, CELL), lambda s: (0, 0, s)),
+        out_shape=jax.ShapeDtypeStruct((2, total, cells * CELL), F32),
+        compiler_params=pltpu.CompilerParams(vmem_limit_bytes=VMEM_LIMIT),
+        cost_estimate=LIGHT,
+        name="main",
+    )(rows, gate_weight, up_weight)
+
+
+def halves_out(total_ref, side, near_ref, far_ref):
+    half = near_ref.shape[1]
+    for c in range(2):
+        near_ref[c] = total_ref[c, half_rows(side, 0, half), :].astype(BF16)
+        far_ref[c] = total_ref[c, half_rows(side, 1, half), :].astype(BF16)
+
+
+def lift_part(lift_ref, spread_ref, c):
+    slots, _, rank, width = lift_ref.shape
+    return jnp.dot(spread_ref[c], lift_ref[:, c].reshape(slots * rank, width), preferred_element_type=F32)
+
+
+def first_kernel(side_ref, slot_ref, rank_ref, lift_ref, *rest):
+    *mains, near_ref, far_ref, spread_ref, total_ref = rest
+    slots, _, rank, _ = lift_ref.shape
+    step = pl.program_id(0)
+
+    @pl.when(step == 0)
+    def _():
+        for c in range(2):
+            spread_ref[c] = spread_rows(rank_ref[c * rank:(c + 1) * rank, :], slot_ref[...], slots)
+
+    for c in range(2):
+        total_ref[c] = mains[0][c] + lift_part(lift_ref, spread_ref, c)
+    halves_out(total_ref, side_ref[0], near_ref, far_ref)
+
+
+def first_call(cells, side, slot_col, rank_t, main, lift):
+    slots, _, rank, _ = lift.shape
+    total = main.shape[1]
+    half = total // 2
+    piece = jax.ShapeDtypeStruct((2, half, cells * CELL), BF16)
+    piece_spec = pl.BlockSpec((2, half, CELL), lambda s, _: (0, 0, s))
+    return pl.pallas_call(
+        first_kernel,
+        grid_spec=pltpu.PrefetchScalarGridSpec(
+            num_scalar_prefetch=1,
+            grid=(cells,),
+            in_specs=[
+                pl.BlockSpec((total, 1), lambda s, _: (0, 0)),
+                pl.BlockSpec((2 * rank, total), lambda s, _: (0, 0)),
+                pl.BlockSpec((slots, 2, rank, CELL), lambda s, _: (0, 0, 0, s)),
+                pl.BlockSpec((2, total, CELL), lambda s, _: (0, 0, s)),
+            ],
+            out_specs=[piece_spec, piece_spec, pl.BlockSpec((2, total, slots * rank), lambda s, _: (0, 0, 0))],
+            scratch_shapes=[pltpu.VMEM((2, total, CELL), F32)],
+        ),
+        out_shape=[piece, piece, jax.ShapeDtypeStruct((2, total, slots * rank), BF16)],
+        compiler_params=pltpu.CompilerParams(vmem_limit_bytes=VMEM_LIMIT),
+        cost_estimate=LIGHT,
+        name="first",
+    )(side, slot_col, rank_t, lift, main)
+
+
+def into_kernel(side_ref, rows_ref, gate_ref, up_ref, lift_ref, spread_ref, near_ref, far_ref, total_ref):
+    for c, main_ref in ((0, gate_ref), (1, up_ref)):
+        total_ref[c] = jnp.dot(rows_ref[...], main_ref[...], preferred_element_type=F32) + lift_part(
+            lift_ref, spread_ref, c
+        )
+    halves_out(total_ref, side_ref[0], near_ref, far_ref)
+
+
+def into_call(first, cells, side, spread, rows, gate_weight, up_weight, lift):
+    slots, _, rank, _ = lift.shape
+    total, depth = rows.shape
+    weight = pl.BlockSpec((depth, CELL), lambda s, _: (0, first + s))
+    return pl.pallas_call(
+        into_kernel,
+        grid_spec=pltpu.PrefetchScalarGridSpec(
+            num_scalar_prefetch=1,
+            grid=(cells,),
+            in_specs=[
+                pl.BlockSpec((total, depth), lambda s, _: (0, 0)),
+                weight,
+                weight,
+                pl.BlockSpec((slots, 2, rank, CELL), lambda s, _: (0, 0, 0, first + s)),
+                pl.BlockSpec(spread.shape, lambda s, _: (0, 0, 0)),
+            ],
+            out_specs=[pl.BlockSpec((2, total // 2, CELL), lambda s, _: (0, 0, s))] * 2,
+            scratch_shapes=[pltpu.VMEM((2, total, CELL), F32)],
+        ),
+        out_shape=[jax.ShapeDtypeStruct((2, total // 2, cells * CELL), BF16)] * 2,
+        compiler_params=pltpu.CompilerParams(vmem_limit_bytes=VMEM_LIMIT),
+        cost_estimate=LIGHT,
+        name="into",
+    )(side, rows, gate_weight, up_weight, lift, spread)
+
+
+def project_kernel(pieces, side_ref, slot_ref, proj_ref, *rest):
+    parts, rest = rest[:2 * pieces], rest[2 * pieces:]
+    out_ref, hidden_ref = rest[-2:]
+    step = pl.program_id(0)
+    side = side_ref[0]
+
+    @pl.when(step == 0)
+    def _():
+        at = 0
+        for piece in range(pieces):
+            for which in range(2):
+                part_ref = parts[2 * piece + which]
+                half, width = part_ref.shape
+                for cell in range(width // CELL):
+                    hidden_ref[at + cell, half_rows(side, which, half), :] = part_ref[:, cell * CELL:(cell + 1) * CELL]
+            at += width // CELL
+        out_ref[...] = rest[0][...] if len(rest) == 3 else jnp.zeros(out_ref.shape, F32)
+
+    out_ref[...] += masked_project(proj_ref[...], hidden_ref[step], slot_ref[...], 0)
+
+
+def project_call(first, side, slot_row, parts, proj, carried):
+    slots, rank, _ = proj.shape
+    half = parts[0].shape[0]
+    cells = sum(part.shape[1] for part in parts) // 2 // CELL
+    extra = () if carried is None else (carried,)
+    fixed = lambda shape: pl.BlockSpec(shape, lambda s, _: (0, 0))
+    return pl.pallas_call(
+        functools.partial(project_kernel, len(parts) // 2),
+        grid_spec=pltpu.PrefetchScalarGridSpec(
+            num_scalar_prefetch=1,
+            grid=(cells,),
+            in_specs=[
+                fixed((1, 2 * half)),
+                pl.BlockSpec((slots, rank, CELL), lambda s, _: (0, 0, first + s)),
+            ]
+            + [fixed(part.shape) for part in parts]
+            + [fixed(one.shape) for one in extra],
+            out_specs=fixed((rank, 2 * half)),
+            scratch_shapes=[pltpu.VMEM((cells, 2 * half, CELL), BF16)],
+        ),
+        out_shape=jax.ShapeDtypeStruct((rank, 2 * half), F32),
+        compiler_params=pltpu.CompilerParams(vmem_limit_bytes=VMEM_LIMIT),
+        cost_estimate=LIGHT,
+        name="project",
+    )(side, slot_row, proj, *parts, *extra)
+
+
+def down_kernel(pieces, cells, side_ref, *rest):
+    downs, parts, rest = rest[:cells], rest[cells:cells + 2 * pieces], rest[cells + 2 * pieces:]
+    out_ref, hidden_ref = rest[-2:]
+    side = side_ref[0]
+
+    @pl.when(pl.program_id(0) == 0)
+    def _():
+        at = 0
+        for piece in range(pieces):
+            for which in range(2):
+                part_ref = parts[2 * piece + which]
+                half, width = part_ref.shape
+                hidden_ref[half_rows(side, which, half), at:at + width] = part_ref[...]
+            at += width
+
+    product = rest[0][...] if len(rest) == 3 else 0.0
+    for cell in range(cells):
+        columns = hidden_ref[:, cell * CELL:(cell + 1) * CELL]
+        product += jnp.dot(columns, downs[cell][...], preferred_element_type=F32)
+    out_ref[...] = product
+
+
+def down_call(first, side, parts, down, carried):
+    half = parts[0].shape[0]
+    depth = sum(part.shape[1] for part in parts) // 2
+    cells = depth // CELL
+    out = down.shape[1]
+    extra = () if carried is None else (carried,)
+    wide = pl.BlockSpec((2 * half, DOWN_CELL), lambda s, _: (0, s))
+    return pl.pallas_call(
+        functools.partial(down_kernel, len(parts) // 2, cells),
+        grid_spec=pltpu.PrefetchScalarGridSpec(
+            num_scalar_prefetch=1,
+            grid=(out // DOWN_CELL,),
+            in_specs=[
+                pl.BlockSpec((CELL, DOWN_CELL), lambda s, _, cell=cell: (first + cell, s)) for cell in range(cells)
+            ]
+            + [pl.BlockSpec(part.shape, lambda s, _: (0, 0)) for part in parts]
+            + [wide for _ in extra],
+            out_specs=wide,
+            scratch_shapes=[pltpu.VMEM((2 * half, depth), BF16)],
+        ),
+        out_shape=jax.ShapeDtypeStruct((2 * half, out), F32),
+        compiler_params=pltpu.CompilerParams(vmem_limit_bytes=VMEM_LIMIT),
+        cost_estimate=LIGHT,
+        name="down",
+    )(side, *(down,) * cells, *parts, *extra)
+
+
+def last_kernel(slot_ref, rank_ref, sum_ref, lift_ref, out_ref, spread_ref):
+    slots, rank, width = lift_ref.shape
+
+    @pl.when(pl.program_id(0) == 0)
+    def _():
+        spread_ref[...] = spread_rows(rank_ref[...], slot_ref[...], slots)
+
+    extra = jnp.dot(spread_ref[...], lift_ref[...].reshape(slots * rank, width), preferred_element_type=F32)
+    out_ref[...] = (sum_ref[...] + extra).astype(BF16)
+
+
+def last_call(slot_col, rank_t, sums, lift):
+    slots, rank, out = lift.shape
+    total = sums.shape[0]
+    return pl.pallas_call(
+        last_kernel,
+        grid=(out // DOWN_CELL,),
+        in_specs=[
+            pl.BlockSpec((total, 1), lambda s: (0, 0)),
+            pl.BlockSpec((rank, total), lambda s: (0, 0)),
+            pl.BlockSpec((total, DOWN_CELL), lambda s: (0, s)),
+            pl.BlockSpec((slots, rank, DOWN_CELL), lambda s: (0, 0, s)),
+        ],
+        out_specs=pl.BlockSpec((total, DOWN_CELL), lambda s: (0, s)),
+        out_shape=jax.ShapeDtypeStruct((total, out), BF16),
+        scratch_shapes=[pltpu.VMEM((total, slots * rank), BF16)],
+        compiler_params=pltpu.CompilerParams(vmem_limit_bytes=VMEM_LIMIT),
+        cost_estimate=LIGHT,
+        name="last",
+    )(slot_col, rank_t, sums, lift)
+
+
+def after(value, *behind):
+    return lax.optimization_barrier((value, *behind))[0]
+
+
+def swap(value, axis, size, mask):
+    return lax.ppermute(value, axis, [(i, i ^ mask) for i in range(size)])
+
+
+def sum_everywhere(value, beside=()):
+    made = []
+    for stage, (axis, size, mask) in enumerate(
+        (("dp", 8, 1), ("dp", 8, 2), ("dp", 8, 4), ("tensor", 4, 1), ("tensor", 4, 2))
+    ):
+        other = swap(value, axis, size, mask)
+        for when, work in beside:
+            if when == stage:
+                made.append(work(value, *made[-1:]))
+                other, made[-1] = lax.optimization_barrier((other, made[-1]))
+        value = value + other
+    return value, made
+
+
+def scatter_dp(rows):
+    total, width = rows.shape
+    me = lax.axis_index("dp")
+    core = me & 1
+    blocks = rows.reshape(4, 2, total // 8, width)
+    mine = lax.dynamic_index_in_dim(blocks, core, 1, keepdims=False)
+    other = lax.dynamic_index_in_dim(blocks, 1 - core, 1, keepdims=False)
+    both = (mine.astype(F32) + swap(other, "dp", 8, 1).astype(F32)).astype(BF16)
+    chip = me >> 1
+    kept = lax.dynamic_index_in_dim(both, chip, 0, keepdims=False).astype(F32)
+    for mask in (3, 1, 2):
+        sent = lax.dynamic_index_in_dim(both, chip ^ mask, 0, keepdims=False)
+        kept = kept + swap(sent, "dp", 8, 2 * mask).astype(F32)
+    return kept.astype(BF16)
+
+
+def line_device(
+    tokens,
+    gate_weight,
+    up_weight,
+    down_weight,
+    adapter_proj_in,
+    adapter_lift_in,
+    adapter_proj_out,
+    adapter_lift_out,
+    token_request,
+    request_adapter,
+    adapter_slot,
+):
+    slot_of = lookup(lookup(token_request, request_adapter), adapter_slot)
+    dp_index = lax.axis_index("dp")
+    tensor_index = lax.axis_index("tensor")
+    side = (tensor_index >> 1).astype(jnp.int32).reshape(1)
+    is_end = (tensor_index == 0) | (tensor_index == 3)
+    slot_dp = slot_of - dp_index * adapter_proj_in.shape[0]
+    slot_tensor = slot_of - tensor_index * adapter_lift_in.shape[0]
+    gathered = lax.all_gather(tokens, "dp", axis=0, tiled=True)
+    rank_part = rank_in_call(slot_dp[None, :], gathered, adapter_proj_in)
+    rank_in, mains = sum_everywhere(
+        rank_part,
+        [
+            (1, lambda tie: main_call(0, CHUNKS[0], after(gathered, tie), gate_weight, up_weight)),
+        ],
+    )
+    rank_in = rank_in.astype(BF16)
+    slot_row = slot_tensor[None, :]
+    slot_col = slot_tensor[:, None]
+    chunks = len(CHUNKS)
+    starts = [sum(CHUNKS[:c]) for c in range(chunks)]
+    near, far, hop, hidden_near, hidden_far = ({} for _ in range(5))
+
+    def operand(c, stage):
+        if stage == 0:
+            return far[c]
+        if stage == 1:
+            return (far[c].astype(F32) + hop[c].astype(F32)).astype(BF16)
+        if stage == 2:
+            return (near[c].astype(F32) + hop[c].astype(F32)).astype(BF16)
+        if stage == 3:
+            both = near[c].astype(F32) + hop[c].astype(F32)
+            hidden_near[c] = (jax.nn.silu(both[0]) * both[1]).astype(BF16)[None]
+            return hidden_near[c]
+        if stage == 4:
+            hidden_near[c] = jnp.where(is_end, hidden_near[c], hop[c])
+            return hop[c]
+        hidden_far[c] = hop[c]
+        return hop[c]
+
+    def pair(c):
+        return [hidden_near[c][0], jnp.where(is_end, hop[c], hidden_far[c])[0]]
+
+    def padded(value, shape):
+        return jnp.pad(value, [(0, b - a) for a, b in zip(value.shape, shape)])
+
+    near[0], far[0], spread = first_call(CHUNKS[0], side, slot_col, rank_in, mains[0], adapter_lift_in)
+    sums, ranks = None, None
+    for slot in range(chunks + 5):
+        live = [(slot - stage, stage) for stage in range(6) if 0 <= slot - stage < chunks]
+        values = {stage % 3: operand(c, stage) for c, stage in live}
+        if 0 in values and 2 in values:
+            shape = tuple(max(a, b) for a, b in zip(values[0].shape, values[2].shape))
+            outer = jnp.where(is_end, padded(values[0], shape), padded(values[2], shape))
+        else:
+            outer = values.get(0, values.get(2))
+        sent = [value for value in (outer, values.get(1)) if value is not None]
+        sent = list(lax.optimization_barrier(tuple(sent)))
+        arrived = {}
+        if outer is not None:
+            arrived[0] = lax.ppermute(sent[0], "tensor", OUTER)
+        if 1 in values:
+            arrived[1] = lax.ppermute(sent[-1], "tensor", MIDDLE)
+        made = ()
+        if slot + 1 < chunks:
+            made = into_call(
+                starts[slot + 1], CHUNKS[slot + 1], after(side, *sent), spread, gathered, gate_weight, up_weight, adapter_lift_in
+            )
+        done = slot - 6
+        if done == 0:
+            early = pair(0)
+            ranks = project_call(starts[0], after(side, *sent), slot_row, early, adapter_proj_out, None)
+            sums = down_call(starts[0], after(side, ranks), early, down_weight, None)
+            made = (ranks, sums)
+        elif done > 0:
+            ranks = project_call(starts[done], after(side, *sent), slot_row, pair(done), adapter_proj_out, ranks)
+            made = (ranks,)
+        *came, = lax.optimization_barrier((*arrived.values(), *made))
+        arrived = dict(zip(arrived, came))
+        made = came[len(arrived):]
+        if slot + 1 < chunks:
+            near[slot + 1], far[slot + 1] = made
+        elif done == 0:
+            ranks, sums = made
+        elif done > 0:
+            (ranks,) = made
+        for c, stage in live:
+            value = arrived[stage % 3 % 2]
+            units, width = (2, 1)[stage // 3], CHUNKS[c] * CELL
+            hop[c] = value[:units, :, :width]
+    ranks = project_call(starts[chunks - 1], side, slot_row, pair(chunks - 1), adapter_proj_out, ranks)
+    rank_out, made = sum_everywhere(
+        ranks,
+        [
+            (1, lambda tie: down_call(starts[1], after(side, tie), pair(1), down_weight, sums)),
+            (3, lambda tie, before: down_call(starts[2], after(side, tie), pair(2), down_weight, before)),
+        ],
+    )
+    return scatter_dp(last_call(slot_dp[:, None], rank_out.astype(BF16), made[-1], adapter_lift_out))
+
+
 def solution(mesh):
+    on_line = mesh.shape["tensor"] == 4 and mesh.shape["dp"] == 8
     placed = (
         P("dp", "tensor"),
         P("tensor", "dp"),
@@ -97,5 +562,5 @@
         P(),
     )
     return jax.shard_map(
-        per_device, mesh=mesh, in_specs=placed, out_specs=P("dp", "tensor"), check_vma=False
-    )
+        line_device if on_line else general_device, mesh=mesh, in_specs=placed, out_specs=P("dp", "tensor"), check_vma=False
+    )

time: 296 us -> 166 us (0.56)
  blocking collectives: 91.6 us -> 12.2 us
  waiting for transfers between devices: 123 us -> 49.3 us
  matrix products: 62.2 us -> 0 us
  Pallas kernels: 0 us -> 47.7 us
  starting transfers between devices: 0.09 us -> 42.1 us
  between operations: 13.2 us -> 0.48 us
  local copies, waits for them, and re-layouts: 0.01 us -> 5.63 us
    reduce_scatter x2 -> x0, waiting for transfers between devices: 89.5 us -> none  [the longest x1 54.7 us: per_device(): lax.psum_scatter((jnp.stack([gate_part, up_part], axis=1) + extra).astype...]
    psum x2 -> x0, blocking collectives: 79.4 us -> none  [the longest x1 39.7 us: per_device(): rank_in = lax.psum(rank_part, ('dp', 'tensor')).astype(jnp.bfloat16)]
    dot_general x7 -> x0, matrix products: 62.2 us -> none  [the longest x1 24.2 us: per_device(): jnp.einsum('tscr,scrf->tcf', spread, adapter_lift_in, preferred_element_t...]
    ppermute x0 -> x28, waiting for transfers between devices: none -> 49.3 us  [the longest x8 27.5 us: line_device(): arrived[0] = lax.ppermute(sent[0], 'tensor', OUTER)]
    pallas_call x0 -> x12, Pallas kernels: none -> 47.7 us  [the longest x2 16.7 us: into_call(): pl.pallas_call(into_kernel, grid_spec=pltpu.PrefetchScalarGridSpec(num_sc...]
    ppermute x0 -> x28, starting transfers between devices: none -> 42.1 us  [the longest x8 22.5 us: line_device(): arrived[0] = lax.ppermute(sent[0], 'tensor', OUTER)]
    all_gather x1 -> x0, waiting for transfers between devices: 33.7 us -> none  [per_device(): hidden_all = lax.all_gather(hidden, 'tensor', axis=0, tiled=True)]
    unnamed x2 -> x10, local copies, waits for them, and re-layouts: 0.01 us -> 4.68 us
  transfers between devices with their start and end apart: 3 -> 28, of which waited for: 3 -> 16; matrix products, arithmetic and copies ran while one was open for 0% -> 1% of each run, Pallas kernels for 0% -> 23%
where the time goes in v2:
time: 166 us; the launch traced here: 165 us
  waiting for transfers between devices  49.3 us (30%)
  Pallas kernels  47.7 us (29%)
  starting transfers between devices  42.1 us (25%)
  blocking collectives  12.2 us (7%)
  other arithmetic  7.39 us (4%)
  local copies, waits for them, and re-layouts  5.63 us (3%)
    ppermute x8, waiting for transfers between devices, line_device(): arrived[0] = lax.ppermute(sent[0], 'tensor', OUTER)  27.5 us
    ppermute x8, starting transfers between devices, line_device(): arrived[0] = lax.ppermute(sent[0], 'tensor', OUTER)  22.5 us
    ppermute x14, waiting for transfers between devices, swap(): return lax.ppermute(value, axis, [(i, i ^ mask) for i in range(size)])  21.7 us
    pallas_call x2, Pallas kernels, into_call(): pl.pallas_call(into_kernel, grid_spec=pltpu.PrefetchScalarGridSpec(num_sc...  16.7 us
    ppermute x14, starting transfers between devices, swap(): return lax.ppermute(value, axis, [(i, i ^ mask) for i in range(size)])  14.9 us
    all_gather x1, blocking collectives, line_device(): gathered = lax.all_gather(tokens, 'dp', axis=0, tiled=True)  12.2 us
    pallas_call x3, Pallas kernels, down_call(): pl.pallas_call(functools.partial(down_kernel, len(parts) // 2, cells), gr...  12 us
    pallas_call x3, Pallas kernels, project_call(): pl.pallas_call(functools.partial(project_kernel, len(parts) // 2), grid_s...  5.92 us
  transfers between devices with their start and end apart: 28, of which 16 were waited for; matrix products, arithmetic and copies ran while one was open for 1% of the time, Pallas kernels for 23%

profile of v2, /device:TPU:0, one launch (start us, length us, event | category | flops | bytes accessed | tf_op | source)
XLA Modules:
  0.0 164.8 jit_solution(5093467917528063759)
XLA Ops:
  0.0 12.2 %all_gather.3.rows_ref = bf16[192,2048]{1,0:T(8,128)(2,1)S(1)} all-gather(bf16[24,2048]{1,0:T(8,128)(2,1)} %param.11), channel_id=1, replica_groups=mesh['dp'=8,'tensor'=4] {'dp'}, dimensions={0}, use_global_device_ids=true | all-gather | bytes 884736 | tf_op jit(solution)/shard_map/all_gather | solution.py:456
  13.9 2.2 %copy-done = bf16[32,32,2048]{2,1,0:T(8,128)(2,1)S(1)} copy-done((bf16[32,32,2048]{2,1,0:T(8,128)(2,1)S(1)}, bf16[32,32,2048]{2,1,0:T(8,128)(2,1)}, u32[]{:S(2)}) %copy-start) | copy-done | bytes 4194328
  20.4 5.2 %main.1.rest_0_ = f32[2,192,1024]{2,1,0:T(8,128)S(1)} custom-call(bf16[192,2048]{1,0:T(8,128)(2,1)S(1)} %all_gather.3.rows_ref, bf16[2048,3584]{1,0:T(8,128)(2,1)} %gate_ref.5, bf16[2048,3584]{1,0:T(8,128)(2,1)} %up_ref.5), custom_call_target="tpu_custom_call" | custom-call | flops 1024 | bytes 1024 | tf_op jit(solution)/shard_map/main/pallas_call | solution.py:169
  26.6 3.0 %collective-permute-done.2 = f32[32,192]{1,0:T(8,128)S(1)} collective-permute-done((f32[32,192]{1,0:T(8,128)S(1)}, f32[32,192]{1,0:T(8,128)S(1)}, u32[]{:S(2)}, u32[]{:S(2)}) %collective-permute-start.2) | collective-permute-done | bytes 24608 | tf_op jit(solution)/shard_map/ppermute | solution.py:403
  31.2 2.3 %collective-permute-done.3 = f32[32,192]{1,0:T(8,128)S(1)} collective-permute-done((f32[32,192]{1,0:T(8,128)S(1)}, f32[32,192]{1,0:T(8,128)S(1)}, u32[]{:S(2)}, u32[]{:S(2)}) %collective-permute-start.3) | collective-permute-done | bytes 24608 | tf_op jit(solution)/shard_map/ppermute | solution.py:403
  33.5 2.6 %collective-permute-start.4 = (f32[32,192]{1,0:T(8,128)S(1)}, f32[32,192]{1,0:T(8,128)S(1)}, u32[]{:S(2)}, u32[]{:S(2)}) collective-permute-start(f32[32,192]{1,0:T(8,128)S(1)} %add.115), channel_id=1, source_target_pairs={{0,2},{1,3},{2,0},{3,1},{4,6},{5,7},{6,4},{7,5},{8,10},{9,11},{10,... | collective-permute-start | bytes 73736 | tf_op jit(solution)/shard_map/ppermute | solution.py:403
  39.2 4.3 %first.1 = (bf16[2,96,1024]{2,1,0:T(8,128)(2,1)S(1)}, bf16[2,96,1024]{2,1,0:T(8,128)(2,1)S(1)}, bf16[2,192,1024]{2,1,0:T(8,128)(2,1)S(1)}) custom-call(s32[1]{0:T(128)} %bitcast.1.side_ref, s32[192,1]{1,0:T(8,128)S(1)} %copy-done.2, bf16[32,192]{1,0:T(8,128)(2,1)S(1)} %add_convert_fusion.3.rank_ref, bf16[64,2,16,3584]{3,2,1,0:T(8,128)(2,1)} %lift_ref.6, ...), custom_call_target="tpu_custom_call" | custom-call | flops 1024 | bytes 1024 | tf_op jit(solution)/shard_map/first/pallas_call | solution.py:214
  45.2 8.3 %into.2 = (bf16[2,96,1280]{2,1,0:T(8,128)(2,1)S(1)}, bf16[2,96,1280]{2,1,0:T(8,128)(2,1)S(1)}) custom-call(s32[1]{0:T(128)} %bitcast.1.side_ref, bf16[192,2048]{1,0:T(8,128)(2,1)S(1)} %all_gather.3.rows_ref, bf16[2048,3584]{1,0:T(8,128)(2,1)} %gate_ref.5, bf16[2048,3584]{1,0:T(8,128)(2,1)} %up_ref.5, bf16[64,2,16,3584]{3,2,1,0:T(8,128)(2,1)} %lift_ref.6, ...), custom_call_target="tpu_custom_call" | custom-call | flops 1024 | bytes 1024 | tf_op jit(solution)/shard_map/into/pallas_call | solution.py:247
  56.3 8.3 %into.3 = (bf16[2,96,1280]{2,1,0:T(8,128)(2,1)S(1)}, bf16[2,96,1280]{2,1,0:T(8,128)(2,1)S(1)}) custom-call(s32[1]{0:T(128)} %bitcast.1.side_ref, bf16[192,2048]{1,0:T(8,128)(2,1)S(1)} %all_gather.3.rows_ref, bf16[2048,3584]{1,0:T(8,128)(2,1)} %gate_ref.5, bf16[2048,3584]{1,0:T(8,128)(2,1)} %up_ref.5, bf16[64,2,16,3584]{3,2,1,0:T(8,128)(2,1)} %lift_ref.6, ...), custom_call_target="tpu_custom_call" | custom-call | flops 1024 | bytes 1024 | tf_op jit(solution)/shard_map/into/pallas_call | solution.py:247
  67.0 3.8 %collective-permute-start.8 = (bf16[2,96,1280]{2,1,0:T(8,128)(2,1)S(1)}, bf16[2,96,1280]{2,1,0:T(8,128)(2,1)S(1)}, u32[]{:S(2)}, u32[]{:S(2)}) collective-permute-start(bf16[2,96,1280]{2,1,0:T(8,128)(2,1)S(1)} %pad_select_fusion), channel_id=1, source_target_pairs={{0,1},{1,0},{2,3},{3,2},{4,5},{5,4},{6,7},{7,6},{8,9},{9,8},{10,11... | collective-permute-start | bytes 1474568 | tf_op jit(solution)/shard_map/ppermute | solution.py:508
  71.5 6.5 %collective-permute-done.8 = bf16[2,96,1280]{2,1,0:T(8,128)(2,1)S(1)} collective-permute-done((bf16[2,96,1280]{2,1,0:T(8,128)(2,1)S(1)}, bf16[2,96,1280]{2,1,0:T(8,128)(2,1)S(1)}, u32[]{:S(2)}, u32[]{:S(2)}) %collective-permute-start.8) | collective-permute-done | bytes 491552 | tf_op jit(solution)/shard_map/ppermute | solution.py:508
  78.6 3.7 %collective-permute-start.10 = (bf16[2,96,1280]{2,1,0:T(8,128)(2,1)S(1)}, bf16[2,96,1280]{2,1,0:T(8,128)(2,1)S(1)}, u32[]{:S(2)}, u32[]{:S(2)}) collective-permute-start(bf16[2,96,1280]{2,1,0:T(8,128)(2,1)S(1)} %fusion.4), channel_id=1, source_target_pairs={{0,1},{1,0},{2,3},{3,2},{4,5},{5,4},{6,7},{7,6},{8,9},{9,8},{10,11... | collective-permute-start | bytes 1474568 | tf_op jit(solution)/shard_map/ppermute | solution.py:508
  83.0 6.3 %collective-permute-done.10 = bf16[2,96,1280]{2,1,0:T(8,128)(2,1)S(1)} collective-permute-done((bf16[2,96,1280]{2,1,0:T(8,128)(2,1)S(1)}, bf16[2,96,1280]{2,1,0:T(8,128)(2,1)S(1)}, u32[]{:S(2)}, u32[]{:S(2)}) %collective-permute-start.10) | collective-permute-done | bytes 491552 | tf_op jit(solution)/shard_map/ppermute | solution.py:508
  89.9 4.7 %collective-permute-start.12 = (bf16[2,96,1280]{2,1,0:T(8,128)(2,1)S(1)}, bf16[2,96,1280]{2,1,0:T(8,128)(2,1)S(1)}, u32[]{:S(2)}, u32[]{:S(2)}) collective-permute-start(bf16[2,96,1280]{2,1,0:T(8,128)(2,1)S(1)} %fusion.5), channel_id=1, source_target_pairs={{0,1},{1,0},{2,3},{3,2},{4,5},{5,4},{6,7},{7,6},{8,9},{9,8},{10,11... | collective-permute-start | bytes 1474568 | tf_op jit(solution)/shard_map/ppermute | solution.py:508
  95.2 8.8 %collective-permute-done.12 = bf16[2,96,1280]{2,1,0:T(8,128)(2,1)S(1)} collective-permute-done((bf16[2,96,1280]{2,1,0:T(8,128)(2,1)S(1)}, bf16[2,96,1280]{2,1,0:T(8,128)(2,1)S(1)}, u32[]{:S(2)}, u32[]{:S(2)}) %collective-permute-start.12) | collective-permute-done | bytes 491552 | tf_op jit(solution)/shard_map/ppermute | solution.py:508
  107.2 3.9 %collective-permute-done.14 = bf16[1,96,1280]{2,1,0:T(8,128)(2,1)S(1)} collective-permute-done((bf16[1,96,1280]{2,1,0:T(8,128)(2,1)S(1)}, bf16[1,96,1280]{2,1,0:T(8,128)(2,1)S(1)}, u32[]{:S(2)}, u32[]{:S(2)}) %collective-permute-start.14) | collective-permute-done | bytes 245792 | tf_op jit(solution)/shard_map/ppermute | solution.py:508
  111.1 3.6 %collective-permute-start.16 = (bf16[1,96,1280]{2,1,0:T(8,128)(2,1)S(1)}, bf16[1,96,1280]{2,1,0:T(8,128)(2,1)S(1)}, u32[]{:S(2)}, u32[]{:S(2)}) collective-permute-start(bf16[1,96,1280]{2,1,0:T(8,128)(2,1)S(1)} %collective-permute-done.15), channel_id=1, source_target_pairs={{0,1},{1,0},{2,3},{3,2},{4,5},{5,4},{6,7},{7,6},{8,9},{9,8},{10,11... | collective-permute-start | bytes 737288 | tf_op jit(solution)/shard_map/ppermute | solution.py:508
  117.2 3.8 %down.3.rest_7_ = f32[192,2048]{1,0:T(8,128)S(1)} custom-call(s32[1]{0:T(128)} %bitcast.1.side_ref, bf16[3584,2048]{1,0:T(8,128)(2,1)} %rest_4_.3, bf16[3584,2048]{1,0:T(8,128)(2,1)} %rest_4_.3, bf16[3584,2048]{1,0:T(8,128)(2,1)} %rest_4_.3, bf16[3584,2048]{1,0:T(8,128)(2,1)} %rest_4_.3, bf16[96,1024]{1,0:T(8,128)(2,1)S(1)} %get-tuple-element.117.rest_0_.rest_4_, ...), custom_call_target="tpu_custom_call" | custom-call | flops 1024 | bytes 1024 | tf_op jit(solution)/shard_map/down/pallas_call | solution.py:346
  121.0 2.5 %collective-permute-start.18 = (bf16[1,96,1280]{2,1,0:T(8,128)(2,1)S(1)}, bf16[1,96,1280]{2,1,0:T(8,128)(2,1)S(1)}, u32[]{:S(2)}, u32[]{:S(2)}) collective-permute-start(bf16[1,96,1280]{2,1,0:T(8,128)(2,1)S(1)} %collective-permute-done.17), channel_id=1, source_target_pairs={{0,1},{1,0},{2,3},{3,2},{4,5},{5,4},{6,7},{7,6},{8,9},{9,8},{10,11... | collective-permute-start | bytes 737288 | tf_op jit(solution)/shard_map/ppermute | solution.py:508
  132.0 4.1 %down.4.rest_7_ = f32[192,2048]{1,0:T(8,128)S(1)} custom-call(s32[1]{0:T(128)} %bitcast.1.side_ref, bf16[3584,2048]{1,0:T(8,128)(2,1)} %rest_4_.3, bf16[3584,2048]{1,0:T(8,128)(2,1)} %rest_4_.3, bf16[3584,2048]{1,0:T(8,128)(2,1)} %rest_4_.3, bf16[3584,2048]{1,0:T(8,128)(2,1)} %rest_4_.3, bf16[3584,2048]{1,0:T(8,128)(2,1)} %rest_4_.3, ...), custom_call_target="tpu_custom_call" | custom-call | flops 1024 | bytes 1024 | tf_op jit(solution)/shard_map/down/pallas_call | solution.py:346
  137.4 2.6 %collective-permute-done.21 = f32[16,192]{1,0:T(8,128)S(1)} collective-permute-done((f32[16,192]{1,0:T(8,128)S(1)}, f32[16,192]{1,0:T(8,128)S(1)}, u32[]{:S(2)}, u32[]{:S(2)}) %collective-permute-start.21) | collective-permute-done | bytes 12320 | tf_op jit(solution)/shard_map/ppermute | solution.py:403
  142.0 4.1 %down.5.sum_ref = f32[192,2048]{1,0:T(8,128)S(1)} custom-call(s32[1]{0:T(128)} %bitcast.1.side_ref, bf16[3584,2048]{1,0:T(8,128)(2,1)} %rest_4_.3, bf16[3584,2048]{1,0:T(8,128)(2,1)} %rest_4_.3, bf16[3584,2048]{1,0:T(8,128)(2,1)} %rest_4_.3, bf16[3584,2048]{1,0:T(8,128)(2,1)} %rest_4_.3, bf16[3584,2048]{1,0:T(8,128)(2,1)} %rest_4_.3, ...), custom_call_target="tpu_custom_call" | custom-call | flops 1024 | bytes 1024 | tf_op jit(solution)/shard_map/down/pallas_call | solution.py:346
  146.6 4.2 %collective-permute-done.23 = f32[16,192]{1,0:T(8,128)S(1)} collective-permute-done((f32[16,192]{1,0:T(8,128)S(1)}, f32[16,192]{1,0:T(8,128)S(1)}, u32[]{:S(2)}, u32[]{:S(2)}) %collective-permute-start.23) | collective-permute-done | bytes 12320 | tf_op jit(solution)/shard_map/ppermute | solution.py:403
  159.7 3.0 %collective-permute-done.25 = bf16[24,2048]{1,0:T(8,128)(2,1)S(1)} collective-permute-done((bf16[24,2048]{1,0:T(8,128)(2,1)S(1)}, bf16[24,2048]{1,0:T(8,128)(2,1)S(1)}, u32[]{:S(2)}, u32[]{:S(2)}) %collective-permute-start.25) | collective-permute-done | bytes 98336 | tf_op jit(solution)/shard_map/ppermute | solution.py:403
  (93 shorter events, 50.1 us)
Async XLA Ops:
  19.3 6.3 %collective-permute-start.1 = (f32[32,192]{1,0:T(8,128)S(1)}, f32[32,192]{1,0:T(8,128)S(1)}, u32[]{:S(2)}, u32[]{:S(2)}) collective-permute-start(f32[32,192]{1,0:T(8,128)S(1)} %add.112), channel_id=1, source_target_pairs={{0,8},{4,12},{8,0},{12,4},{16,24},{20,28},{24,16},{28,20},{1,9},{5... | collective-permute-start | bytes 73736 | tf_op jit(solution)/shard_map/ppermute | solution.py:403
  25.6 4.0 %collective-permute-start.2 = (f32[32,192]{1,0:T(8,128)S(1)}, f32[32,192]{1,0:T(8,128)S(1)}, u32[]{:S(2)}, u32[]{:S(2)}) collective-permute-start(f32[32,192]{1,0:T(8,128)S(1)} %add.113), channel_id=1, source_target_pairs={{0,16},{4,20},{8,24},{12,28},{16,0},{20,4},{24,8},{28,12},{1,17},{... | collective-permute-start | bytes 73736 | tf_op jit(solution)/shard_map/ppermute | solution.py:403
  29.6 3.9 %collective-permute-start.3 = (f32[32,192]{1,0:T(8,128)S(1)}, f32[32,192]{1,0:T(8,128)S(1)}, u32[]{:S(2)}, u32[]{:S(2)}) collective-permute-start(f32[32,192]{1,0:T(8,128)S(1)} %add.114), channel_id=1, source_target_pairs={{0,1},{1,0},{2,3},{3,2},{4,5},{5,4},{6,7},{7,6},{8,9},{9,8},{10,11... | collective-permute-start | bytes 73736 | tf_op jit(solution)/shard_map/ppermute | solution.py:403
  33.5 4.8 %collective-permute-start.4 = (f32[32,192]{1,0:T(8,128)S(1)}, f32[32,192]{1,0:T(8,128)S(1)}, u32[]{:S(2)}, u32[]{:S(2)}) collective-permute-start(f32[32,192]{1,0:T(8,128)S(1)} %add.115), channel_id=1, source_target_pairs={{0,2},{1,3},{2,0},{3,1},{4,6},{5,7},{6,4},{7,5},{8,10},{9,11},{10,... | collective-permute-start | bytes 73736 | tf_op jit(solution)/shard_map/ppermute | solution.py:403
  43.6 10.0 %collective-permute-start.5 = (bf16[2,96,1024]{2,1,0:T(8,128)(2,1)S(1)}, bf16[2,96,1024]{2,1,0:T(8,128)(2,1)S(1)}, u32[]{:S(2)}, u32[]{:S(2)}) collective-permute-start(bf16[2,96,1024]{2,1,0:T(8,128)(2,1)S(1)} %get-tuple-element.62), channel_id=1, source_target_pairs={{0,1},{1,0},{2,3},{3,2},{4,5},{5,4},{6,7},{7,6},{8,9},{9,8},{10,11... | collective-permute-start | bytes 1179656 | tf_op jit(solution)/shard_map/ppermute | solution.py:508
  54.5 10.2 %collective-permute-start.6 = (bf16[2,96,1280]{2,1,0:T(8,128)(2,1)S(1)}, bf16[2,96,1280]{2,1,0:T(8,128)(2,1)}, u32[]{:S(2)}, u32[]{:S(2)}) collective-permute-start(bf16[2,96,1280]{2,1,0:T(8,128)(2,1)S(1)} %get-tuple-element.69), channel_id=1, source_target_pairs={{0,1},{1,0},{2,3},{3,2},{4,5},{5,4},{6,7},{7,6},{8,9},{9,8},{10,11... | collective-permute-start | bytes 1474568 | tf_op jit(solution)/shard_map/ppermute | solution.py:508
  54.9 9.7 %collective-permute-start.7 = (bf16[2,96,1024]{2,1,0:T(8,128)(2,1)}, bf16[2,96,1024]{2,1,0:T(8,128)(2,1)}, u32[]{:S(2)}, u32[]{:S(2)}) collective-permute-start(bf16[2,96,1024]{2,1,0:T(8,128)(2,1)} %add_convert_fusion.2), channel_id=1, source_target_pairs={{1,2},{2,1},{5,6},{6,5},{9,10},{10,9},{13,14},{14,13},{17,18},{18,... | collective-permute-start | bytes 1179656 | tf_op jit(solution)/shard_map/ppermute | solution.py:510
  67.0 11.0 %collective-permute-start.8 = (bf16[2,96,1280]{2,1,0:T(8,128)(2,1)S(1)}, bf16[2,96,1280]{2,1,0:T(8,128)(2,1)S(1)}, u32[]{:S(2)}, u32[]{:S(2)}) collective-permute-start(bf16[2,96,1280]{2,1,0:T(8,128)(2,1)S(1)} %pad_select_fusion), channel_id=1, source_target_pairs={{0,1},{1,0},{2,3},{3,2},{4,5},{5,4},{6,7},{7,6},{8,9},{9,8},{10,11... | collective-permute-start | bytes 1474568 | tf_op jit(solution)/shard_map/ppermute | solution.py:508
  70.8 7.2 %collective-permute-start.9 = (bf16[2,96,1280]{2,1,0:T(8,128)(2,1)S(1)}, bf16[2,96,1280]{2,1,0:T(8,128)(2,1)S(1)}, u32[]{:S(2)}, u32[]{:S(2)}) collective-permute-start(bf16[2,96,1280]{2,1,0:T(8,128)(2,1)S(1)} %add_convert_fusion.1), channel_id=1, source_target_pairs={{1,2},{2,1},{5,6},{6,5},{9,10},{10,9},{13,14},{14,13},{17,18},{18,... | collective-permute-start | bytes 1474568 | tf_op jit(solution)/shard_map/ppermute | solution.py:510
  78.6 10.7 %collective-permute-start.10 = (bf16[2,96,1280]{2,1,0:T(8,128)(2,1)S(1)}, bf16[2,96,1280]{2,1,0:T(8,128)(2,1)S(1)}, u32[]{:S(2)}, u32[]{:S(2)}) collective-permute-start(bf16[2,96,1280]{2,1,0:T(8,128)(2,1)S(1)} %fusion.4), channel_id=1, source_target_pairs={{0,1},{1,0},{2,3},{3,2},{4,5},{5,4},{6,7},{7,6},{8,9},{9,8},{10,11... | collective-permute-start | bytes 1474568 | tf_op jit(solution)/shard_map/ppermute | solution.py:508
  82.3 7.0 %collective-permute-start.11 = (bf16[2,96,1280]{2,1,0:T(8,128)(2,1)S(1)}, bf16[2,96,1280]{2,1,0:T(8,128)(2,1)S(1)}, u32[]{:S(2)}, u32[]{:S(2)}) collective-permute-start(bf16[2,96,1280]{2,1,0:T(8,128)(2,1)S(1)} %add_convert_fusion), channel_id=1, source_target_pairs={{1,2},{2,1},{5,6},{6,5},{9,10},{10,9},{13,14},{14,13},{17,18},{18,... | collective-permute-start | bytes 1474568 | tf_op jit(solution)/shard_map/ppermute | solution.py:510
  89.9 14.1 %collective-permute-start.12 = (bf16[2,96,1280]{2,1,0:T(8,128)(2,1)S(1)}, bf16[2,96,1280]{2,1,0:T(8,128)(2,1)S(1)}, u32[]{:S(2)}, u32[]{:S(2)}) collective-permute-start(bf16[2,96,1280]{2,1,0:T(8,128)(2,1)S(1)} %fusion.5), channel_id=1, source_target_pairs={{0,1},{1,0},{2,3},{3,2},{4,5},{5,4},{6,7},{7,6},{8,9},{9,8},{10,11... | collective-permute-start | bytes 1474568 | tf_op jit(solution)/shard_map/ppermute | solution.py:508
  104.5 6.7 %collective-permute-start.14 = (bf16[1,96,1280]{2,1,0:T(8,128)(2,1)S(1)}, bf16[1,96,1280]{2,1,0:T(8,128)(2,1)S(1)}, u32[]{:S(2)}, u32[]{:S(2)}) collective-permute-start(bf16[1,96,1280]{2,1,0:T(8,128)(2,1)S(1)} %get-tuple-element.92), channel_id=1, source_target_pairs={{0,1},{1,0},{2,3},{3,2},{4,5},{5,4},{6,7},{7,6},{8,9},{9,8},{10,11... | collective-permute-start | bytes 737288 | tf_op jit(solution)/shard_map/ppermute | solution.py:508
  106.5 4.6 %collective-permute-start.15 = (bf16[1,96,1280]{2,1,0:T(8,128)(2,1)S(1)}, bf16[1,96,1280]{2,1,0:T(8,128)(2,1)S(1)}, u32[]{:S(2)}, u32[]{:S(2)}) collective-permute-start(bf16[1,96,1280]{2,1,0:T(8,128)(2,1)S(1)} %get-tuple-element.93), channel_id=1, source_target_pairs={{1,2},{2,1},{5,6},{6,5},{9,10},{10,9},{13,14},{14,13},{17,18},{18,... | collective-permute-start | bytes 737288 | tf_op jit(solution)/shard_map/ppermute | solution.py:510
  111.1 9.8 %collective-permute-start.16 = (bf16[1,96,1280]{2,1,0:T(8,128)(2,1)S(1)}, bf16[1,96,1280]{2,1,0:T(8,128)(2,1)S(1)}, u32[]{:S(2)}, u32[]{:S(2)}) collective-permute-start(bf16[1,96,1280]{2,1,0:T(8,128)(2,1)S(1)} %collective-permute-done.15), channel_id=1, source_target_pairs={{0,1},{1,0},{2,3},{3,2},{4,5},{5,4},{6,7},{7,6},{8,9},{9,8},{10,11... | collective-permute-start | bytes 737288 | tf_op jit(solution)/shard_map/ppermute | solution.py:508
  114.8 6.2 %collective-permute-start.17 = (bf16[1,96,1280]{2,1,0:T(8,128)(2,1)S(1)}, bf16[1,96,1280]{2,1,0:T(8,128)(2,1)S(1)}, u32[]{:S(2)}, u32[]{:S(2)}) collective-permute-start(bf16[1,96,1280]{2,1,0:T(8,128)(2,1)S(1)} %collective-permute-done.14), channel_id=1, source_target_pairs={{1,2},{2,1},{5,6},{6,5},{9,10},{10,9},{13,14},{14,13},{17,18},{18,... | collective-permute-start | bytes 737288 | tf_op jit(solution)/shard_map/ppermute | solution.py:510
  121.0 6.7 %collective-permute-start.18 = (bf16[1,96,1280]{2,1,0:T(8,128)(2,1)S(1)}, bf16[1,96,1280]{2,1,0:T(8,128)(2,1)S(1)}, u32[]{:S(2)}, u32[]{:S(2)}) collective-permute-start(bf16[1,96,1280]{2,1,0:T(8,128)(2,1)S(1)} %collective-permute-done.17), channel_id=1, source_target_pairs={{0,1},{1,0},{2,3},{3,2},{4,5},{5,4},{6,7},{7,6},{8,9},{9,8},{10,11... | collective-permute-start | bytes 737288 | tf_op jit(solution)/shard_map/ppermute | solution.py:508
  131.1 5.0 %collective-permute-start.20 = (f32[16,192]{1,0:T(8,128)S(1)}, f32[16,192]{1,0:T(8,128)S(1)}, u32[]{:S(2)}, u32[]{:S(2)}) collective-permute-start(f32[16,192]{1,0:T(8,128)S(1)} %add.129), channel_id=1, source_target_pairs={{0,8},{4,12},{8,0},{12,4},{16,24},{20,28},{24,16},{28,20},{1,9},{5... | collective-permute-start | bytes 36872 | tf_op jit(solution)/shard_map/ppermute | solution.py:403
  136.2 3.8 %collective-permute-start.21 = (f32[16,192]{1,0:T(8,128)S(1)}, f32[16,192]{1,0:T(8,128)S(1)}, u32[]{:S(2)}, u32[]{:S(2)}) collective-permute-start(f32[16,192]{1,0:T(8,128)S(1)} %add.130), channel_id=1, source_target_pairs={{0,16},{4,20},{8,24},{12,28},{16,0},{20,4},{24,8},{28,12},{1,17},{... | collective-permute-start | bytes 36872 | tf_op jit(solution)/shard_map/ppermute | solution.py:403
  140.0 6.2 %collective-permute-start.22 = (f32[16,192]{1,0:T(8,128)S(1)}, f32[16,192]{1,0:T(8,128)S(1)}, u32[]{:S(2)}, u32[]{:S(2)}) collective-permute-start(f32[16,192]{1,0:T(8,128)S(1)} %add.131), channel_id=1, source_target_pairs={{0,1},{1,0},{2,3},{3,2},{4,5},{5,4},{6,7},{7,6},{8,9},{9,8},{10,11... | collective-permute-start | bytes 36872 | tf_op jit(solution)/shard_map/ppermute | solution.py:403
  146.2 4.7 %collective-permute-start.23 = (f32[16,192]{1,0:T(8,128)S(1)}, f32[16,192]{1,0:T(8,128)S(1)}, u32[]{:S(2)}, u32[]{:S(2)}) collective-permute-start(f32[16,192]{1,0:T(8,128)S(1)} %add.132), channel_id=1, source_target_pairs={{0,2},{1,3},{2,0},{3,1},{4,6},{5,7},{6,4},{7,5},{8,10},{9,11},{10,... | collective-permute-start | bytes 36872 | tf_op jit(solution)/shard_map/ppermute | solution.py:403
  156.2 6.6 %collective-permute-start.25 = (bf16[24,2048]{1,0:T(8,128)(2,1)S(1)}, bf16[24,2048]{1,0:T(8,128)(2,1)S(1)}, u32[]{:S(2)}, u32[]{:S(2)}) collective-permute-start(bf16[24,2048]{1,0:T(8,128)(2,1)S(1)} %get-tuple-element.119), channel_id=1, source_target_pairs={{0,24},{4,28},{8,16},{12,20},{16,8},{20,12},{24,0},{28,4},{1,25},{... | collective-permute-start | bytes 294920 | tf_op jit(solution)/shard_map/ppermute | solution.py:403
  157.7 6.1 %collective-permute-start.26 = (bf16[24,2048]{1,0:T(8,128)(2,1)S(1)}, bf16[24,2048]{1,0:T(8,128)(2,1)S(1)}, u32[]{:S(2)}, u32[]{:S(2)}) collective-permute-start(bf16[24,2048]{1,0:T(8,128)(2,1)S(1)} %get-tuple-element.121), channel_id=1, source_target_pairs={{0,8},{4,12},{8,0},{12,4},{16,24},{20,28},{24,16},{28,20},{1,9},{5... | collective-permute-start | bytes 294920 | tf_op jit(solution)/shard_map/ppermute | solution.py:403
  158.8 5.2 %collective-permute-start.27 = (bf16[24,2048]{1,0:T(8,128)(2,1)S(1)}, bf16[24,2048]{1,0:T(8,128)(2,1)S(1)}, u32[]{:S(2)}, u32[]{:S(2)}) collective-permute-start(bf16[24,2048]{1,0:T(8,128)(2,1)S(1)} %get-tuple-element.120), channel_id=1, source_target_pairs={{0,16},{4,20},{8,24},{12,28},{16,0},{20,4},{24,8},{28,12},{1,17},{... | collective-permute-start | bytes 294920 | tf_op jit(solution)/shard_map/ppermute | solution.py:403
  (9 other events, 72.5 us)

commit v3 on v0

--- a/solution.py
+++ b/solution.py
@@ -1,7 +1,18 @@
+import functools
+
 import jax
 import jax.numpy as jnp
 from jax import lax
+from jax.experimental import pallas as pl
+from jax.experimental.pallas import tpu as pltpu
 from jax.sharding import PartitionSpec as P
+
+CELL = 256
+CHUNKS = (4, 5, 5)
+VMEM_LIMIT = 40 << 20
+LIGHT = pl.CostEstimate(flops=1024, bytes_accessed=1024, transcendentals=0)
+F32 = jnp.float32
+BF16 = jnp.bfloat16
 
 
 def lookup(keys, table):
@@ -14,7 +25,7 @@
     return (slot_of[:, None] == places[None, :]).astype(jnp.bfloat16)
 
 
-def per_device(
+def general_device(
     tokens,
     gate_weight,
     up_weight,
@@ -82,7 +93,510 @@
     )
 
 
+OUTER = [(0, 1), (1, 0), (2, 3), (3, 2)]
+MIDDLE = [(1, 2), (2, 1)]
+
+
+def masked_project(block, rows, slot_row, first):
+    slots, rank, depth = block.shape
+    full = lax.dot_general(
+        block.reshape(slots * rank, depth), rows, (((1,), (1,)), ((), ())), preferred_element_type=F32
+    ).reshape(slots, rank, rows.shape[0])
+    ids = first + lax.broadcasted_iota(jnp.int32, full.shape, 0)
+    return jnp.sum(jnp.where(ids == slot_row[None], full, 0.0), axis=0)
+
+
+def spread_rows(rank_t, slot_row, slots):
+    rank, total = rank_t.shape
+    width = slots * rank
+    slot_col = jnp.broadcast_to(slot_row.astype(F32), (8, total)).T[:, :1].astype(jnp.int32)
+    lane = lax.broadcasted_iota(jnp.int32, (rank, width), 1)
+    row = lax.broadcasted_iota(jnp.int32, (rank, width), 0)
+    copies = (lax.rem(lane, rank) == row).astype(F32).astype(BF16)
+    tiled = lax.dot_general(
+        rank_t.astype(F32).T.astype(BF16), copies, (((1,), (0,)), ((), ())), preferred_element_type=F32
+    )
+    owner = lax.div(lax.broadcasted_iota(jnp.int32, tiled.shape, 1), rank)
+    return jnp.where(owner == slot_col, tiled, 0.0).astype(BF16)
+
+
+IN_VMEM = pl.BlockSpec(memory_space=pltpu.VMEM)
+IN_SMEM = pl.BlockSpec(memory_space=pltpu.SMEM)
+ANYWHERE = pl.BlockSpec(memory_space=pl.ANY)
+ROWS = 512
+GROUP = 16
+
+
+def call(kernel, name, in_specs, outs, scratch):
+    return pl.pallas_call(
+        kernel,
+        in_specs=in_specs,
+        out_specs=jax.tree.map(lambda _: IN_VMEM, outs),
+        out_shape=outs,
+        scratch_shapes=scratch,
+        compiler_params=pltpu.CompilerParams(vmem_limit_bytes=VMEM_LIMIT),
+        cost_estimate=LIGHT,
+        name=name,
+    )
+
+
+def fetch(parts, sems):
+    copies = [pltpu.make_async_copy(src, dst, sems.at[at]) for at, (src, dst) in enumerate(parts)]
+    for copy in copies:
+        copy.start()
+    return copies
+
+
+def rank_in_kernel(slot_ref, rows_ref, proj_ref, out_ref):
+    step = pl.program_id(0)
+    part = masked_project(proj_ref[...], rows_ref[...], slot_ref[...], step * proj_ref.shape[0])
+
+    @pl.when(step == 0)
+    def _():
+        out_ref[...] = part
+
+    @pl.when(step > 0)
+    def _():
+        out_ref[...] += part
+
+
+def rank_in_call(slot_row, rows, proj):
+    slots, rank, depth = proj.shape
+    total = rows.shape[0]
+    group = 8
+    return pl.pallas_call(
+        rank_in_kernel,
+        grid=(slots // group,),
+        in_specs=[
+            pl.BlockSpec((1, total), lambda s: (0, 0)),
+            pl.BlockSpec((total, depth), lambda s: (0, 0)),
+            pl.BlockSpec((group, rank, depth), lambda s: (s, 0, 0)),
+        ],
+        out_specs=pl.BlockSpec((rank, total), lambda s: (0, 0)),
+        out_shape=jax.ShapeDtypeStruct((rank, total), F32),
+        compiler_params=pltpu.CompilerParams(vmem_limit_bytes=VMEM_LIMIT),
+        cost_estimate=LIGHT,
+        name="rank_in",
+    )(slot_row, rows, proj)
+
+
+def half_rows(side, which, half):
+    start = side * half if which == 0 else (1 - side) * half
+    return pl.ds(pl.multiple_of(start, 16), half)
+
+
+def weight_parts(weight_ref, held_ref, first):
+    blocks, rows, width = held_ref.shape
+    return [
+        (weight_ref.at[pl.ds(k * rows, rows), pl.ds(first * CELL, width)], held_ref.at[k]) for k in range(blocks)
+    ]
+
+
+def lift_parts(lift_ref, held_ref, first):
+    groups, slots = held_ref.shape[:2]
+    width = held_ref.shape[-1]
+    return [
+        (lift_ref.at[pl.ds(g * slots, slots), :, :, pl.ds(first * CELL, width)], held_ref.at[g])
+        for g in range(groups)
+    ]
+
+
+def add_product(total_ref, fresh, left, right):
+    product = jnp.dot(left, right, preferred_element_type=F32)
+    total_ref[...] = product if fresh else total_ref[...] + product
+
+
+def add_lift(total_ref, spread_ref, held_ref, g):
+    _, slots, _, rank, width = held_ref.shape
+    depth = slots * rank
+    for c in range(2):
+        left = spread_ref[c, :, g * depth:(g + 1) * depth]
+        add_product(total_ref.at[c], False, left, held_ref[g, :, c].reshape(depth, width))
+
+
+def halves_out(total_ref, side, near_ref, far_ref):
+    half = near_ref.shape[1]
+    for c in range(2):
+        near_ref[c] = total_ref[c, half_rows(side, 0, half), :].astype(BF16)
+        far_ref[c] = total_ref[c, half_rows(side, 1, half), :].astype(BF16)
+
+
+def main_kernel(first, rows_ref, weight_ref, out_ref, held_ref, sems):
+    copies = fetch(weight_parts(weight_ref, held_ref, first), sems)
+    for k, copy in enumerate(copies):
+        copy.wait()
+        add_product(out_ref, k == 0, rows_ref[:, k * ROWS:(k + 1) * ROWS], held_ref[k])
+
+
+def main_call(first, cells, rows, weight):
+    total, depth = rows.shape
+    blocks, width = depth // ROWS, cells * CELL
+    return call(
+        functools.partial(main_kernel, first),
+        "main",
+        [IN_VMEM, ANYWHERE],
+        jax.ShapeDtypeStruct((total, width), F32),
+        [pltpu.VMEM((blocks, ROWS, width), BF16), pltpu.SemaphoreType.DMA((blocks,))],
+    )(rows, weight)
+
+
+def first_kernel(side_ref, slot_ref, rank_ref, gate_ref, up_ref, lift_ref, near_ref, far_ref, spread_ref, total_ref, held_ref, sems):
+    copies = fetch(lift_parts(lift_ref, held_ref, 0), sems)
+    slots, _, rank, _ = lift_ref.shape
+    for c, main_ref in ((0, gate_ref), (1, up_ref)):
+        spread_ref[c] = spread_rows(rank_ref[c * rank:(c + 1) * rank, :], slot_ref[...], slots)
+        total_ref[c] = main_ref[...]
+    for g, copy in enumerate(copies):
+        copy.wait()
+        add_lift(total_ref, spread_ref, held_ref, g)
+    halves_out(total_ref, side_ref[0], near_ref, far_ref)
+
+
+def lift_held(lift, width):
+    slots, two, rank, _ = lift.shape
+    return pltpu.VMEM((slots // GROUP, GROUP, two, rank, width), BF16)
+
+
+def first_call(side, slot_row, rank_t, gate, up, lift):
+    slots, _, rank, _ = lift.shape
+    total, width = gate.shape
+    piece = jax.ShapeDtypeStruct((2, total // 2, width), BF16)
+    return call(
+        first_kernel,
+        "first",
+        [IN_SMEM] + [IN_VMEM] * 4 + [ANYWHERE],
+        [piece, piece, jax.ShapeDtypeStruct((2, total, slots * rank), BF16)],
+        [pltpu.VMEM((2, total, width), F32), lift_held(lift, width), pltpu.SemaphoreType.DMA((slots // GROUP,))],
+    )(side, slot_row, rank_t, gate, up, lift)
+
+
+def into_kernel(first, side_ref, rows_ref, spread_ref, gate_ref, up_ref, lift_ref, near_ref, far_ref, total_ref, gate_held, up_held, lift_buf, sems):
+    blocks = gate_held.shape[0]
+    parts = []
+    for pair in zip(weight_parts(gate_ref, gate_held, first), weight_parts(up_ref, up_held, first)):
+        parts += pair
+    copies = fetch(parts + lift_parts(lift_ref, lift_buf, first), sems)
+    for k in range(blocks):
+        for c, held in ((0, gate_held), (1, up_held)):
+            copies[2 * k + c].wait()
+            add_product(total_ref.at[c], k == 0, rows_ref[:, k * ROWS:(k + 1) * ROWS], held[k])
+    for g, copy in enumerate(copies[2 * blocks:]):
+        copy.wait()
+        add_lift(total_ref, spread_ref, lift_buf, g)
+    halves_out(total_ref, side_ref[0], near_ref, far_ref)
+
+
+def into_call(first, cells, side, spread, rows, gate_weight, up_weight, lift):
+    total, depth = rows.shape
+    blocks, width = depth // ROWS, cells * CELL
+    held = pltpu.VMEM((blocks, ROWS, width), BF16)
+    return call(
+        functools.partial(into_kernel, first),
+        "into",
+        [IN_SMEM, IN_VMEM, IN_VMEM] + [ANYWHERE] * 3,
+        [jax.ShapeDtypeStruct((2, total // 2, width), BF16)] * 2,
+        [
+            pltpu.VMEM((2, total, width), F32),
+            held,
+            held,
+            lift_held(lift, width),
+            pltpu.SemaphoreType.DMA((2 * blocks + lift.shape[0] // GROUP,)),
+        ],
+    )(side, rows, spread, gate_weight, up_weight, lift)
+
+
+def whole_hidden(side, near_ref, far_ref, hidden_ref):
+    half = near_ref.shape[0]
+    hidden_ref[half_rows(side, 0, half), :] = near_ref[...]
+    hidden_ref[half_rows(side, 1, half), :] = far_ref[...]
+
+
+def project_parts(proj_ref, held_ref, first):
+    groups, slots = held_ref.shape[:2]
+    columns = pl.ds(first * CELL, held_ref.shape[-1])
+    return [(proj_ref.at[pl.ds(g * slots, slots), :, columns], held_ref.at[g]) for g in range(groups)]
+
+
+def project_kernel(first, later, side_ref, slot_ref, near_ref, far_ref, proj_ref, before_ref, out_ref, brought_ref, hidden_ref, held_ref, sems):
+    parts = project_parts(proj_ref, held_ref, first)
+    copies = fetch(parts + project_parts(proj_ref, brought_ref, later) * (later > 0), sems)
+    whole_hidden(side_ref[0], near_ref, far_ref, hidden_ref)
+    total = before_ref[...]
+    slots = held_ref.shape[1]
+    for g in range(len(parts)):
+        copies[g].wait()
+        total += masked_project(held_ref[g], hidden_ref[...], slot_ref[...], g * slots)
+    out_ref[...] = total
+    for copy in copies[len(parts):]:
+        copy.wait()
+
+
+def project_call(first, later, later_cells, side, slot_row, parts, proj, carried):
+    slots, rank, _ = proj.shape
+    half, width = parts[0].shape
+    groups = slots // GROUP
+    held = (groups, GROUP, rank)
+    return call(
+        functools.partial(project_kernel, first, later),
+        "project",
+        [IN_SMEM] + [IN_VMEM] * 3 + [ANYWHERE, IN_VMEM],
+        [
+            jax.ShapeDtypeStruct((rank, 2 * half), F32),
+            jax.ShapeDtypeStruct((*held, later_cells * CELL), BF16),
+        ],
+        [
+            pltpu.VMEM((2 * half, width), BF16),
+            pltpu.VMEM((*held, width), BF16),
+            pltpu.SemaphoreType.DMA((2 * groups,)),
+        ],
+    )(side, slot_row, *parts, proj, carried)
+
+
+def project_last_kernel(side_ref, slot_ref, near_ref, far_ref, held_ref, before_ref, out_ref, hidden_ref):
+    whole_hidden(side_ref[0], near_ref, far_ref, hidden_ref)
+    total = before_ref[...]
+    slots = held_ref.shape[1]
+    for g in range(held_ref.shape[0]):
+        total += masked_project(held_ref[g], hidden_ref[...], slot_ref[...], g * slots)
+    out_ref[...] = total
+
+
+def project_last_call(side, slot_row, parts, held, carried):
+    half, width = parts[0].shape
+    return call(
+        project_last_kernel,
+        "project",
+        [IN_SMEM] + [IN_VMEM] * 5,
+        jax.ShapeDtypeStruct(carried.shape, F32),
+        [pltpu.VMEM((2 * half, width), BF16)],
+    )(side, slot_row, *parts, held, carried)
+
+
+def down_kernel(first, bring, side_ref, near_ref, far_ref, down_ref, *rest):
+    rest, (hidden_ref, held_ref, sems) = rest[:-3], rest[-3:]
+    if bring:
+        rest, (later_ref, out_ref, brought_ref) = rest[:-3], rest[-3:]
+    else:
+        rest, out_ref = rest[:-1], rest[-1]
+    cells = held_ref.shape[0]
+    parts = [(down_ref.at[pl.ds((first + k) * CELL, CELL), :], held_ref.at[k]) for k in range(cells)]
+    if bring:
+        parts.append((later_ref, brought_ref))
+    copies = fetch(parts, sems)
+    whole_hidden(side_ref[0], near_ref, far_ref, hidden_ref)
+    for k in range(cells):
+        copies[k].wait()
+        product = jnp.dot(hidden_ref[:, k * CELL:(k + 1) * CELL], held_ref[k], preferred_element_type=F32)
+        if k > 0:
+            product += out_ref[...]
+        elif rest:
+            product += rest[0][...]
+        out_ref[...] = product
+    if bring:
+        copies[cells].wait()
+
+
+def down_call(first, side, parts, down, carried, later=None):
+    half, width = parts[0].shape
+    out = down.shape[1]
+    cells = width // CELL
+    extra = () if carried is None else (carried,)
+    bring = () if later is None else (later,)
+    sums = jax.ShapeDtypeStruct((2 * half, out), F32)
+    return call(
+        functools.partial(down_kernel, first, len(bring)),
+        "down",
+        [IN_SMEM, IN_VMEM, IN_VMEM, ANYWHERE] + [IN_VMEM for _ in extra] + [ANYWHERE for _ in bring],
+        [sums, jax.ShapeDtypeStruct(later.shape, later.dtype)] if bring else sums,
+        [
+            pltpu.VMEM((2 * half, width), BF16),
+            pltpu.VMEM((cells, CELL, out), BF16),
+            pltpu.SemaphoreType.DMA((cells + len(bring),)),
+        ],
+    )(side, *parts, down, *extra, *bring)
+
+
+def last_kernel(slot_ref, rank_ref, sum_ref, lift_ref, out_ref):
+    slots, rank, width = lift_ref.shape
+    spread = spread_rows(rank_ref[...], slot_ref[...], slots)
+    extra = jnp.dot(spread, lift_ref[...].reshape(slots * rank, width), preferred_element_type=F32)
+    out_ref[...] = (sum_ref[...] + extra).astype(BF16)
+
+
+def last_call(slot_row, rank_t, sums, lift):
+    return call(
+        last_kernel, "last", [IN_VMEM] * 4, jax.ShapeDtypeStruct(sums.shape, BF16), []
+    )(slot_row, rank_t, sums, lift)
+
+
+def after(value, *behind):
+    return lax.optimization_barrier((value, *behind))[0]
+
+
+def swap(value, axis, size, mask):
+    return lax.ppermute(value, axis, [(i, i ^ mask) for i in range(size)])
+
+
+def gather_dp(block, beside):
+    me = lax.axis_index("dp")
+    chip = me >> 1
+    near = jnp.stack([block] + [swap(block, "dp", 8, 2 * mask) for mask in (1, 2, 3)])
+    near, beside = lax.optimization_barrier((near, beside))
+    other = swap(near, "dp", 8, 1)
+    both = jnp.where((me & 1) == 0, jnp.stack([near, other], 1), jnp.stack([other, near], 1))
+    both = jnp.where((chip & 1) == 0, both, jnp.stack([both[1], both[0], both[3], both[2]]))
+    both = jnp.where((chip & 2) == 0, both, jnp.stack([both[2], both[3], both[0], both[1]]))
+    return both.reshape(8 * block.shape[0], block.shape[1]), beside
+
+
+def sum_everywhere(value, beside=()):
+    made = []
+    for stage, (axis, size, masks) in enumerate(
+        (("dp", 8, (1,)), ("dp", 8, (6, 2, 4)), ("tensor", 4, (1,)), ("tensor", 4, (2,)))
+    ):
+        others = [swap(value, axis, size, mask) for mask in masks]
+        for when, work in beside:
+            if when == stage:
+                made.append(work(value, *made[-1:]))
+                others, made[-1] = lax.optimization_barrier((others, made[-1]))
+        value = sum(others, value)
+    return value, made
+
+
+def scatter_dp(rows):
+    total, width = rows.shape
+    me = lax.axis_index("dp")
+    core = me & 1
+    blocks = rows.reshape(4, 2, total // 8, width)
+    mine = lax.dynamic_index_in_dim(blocks, core, 1, keepdims=False)
+    other = lax.dynamic_index_in_dim(blocks, 1 - core, 1, keepdims=False)
+    both = (mine.astype(F32) + swap(other, "dp", 8, 1).astype(F32)).astype(BF16)
+    chip = me >> 1
+    kept = lax.dynamic_index_in_dim(both, chip, 0, keepdims=False).astype(F32)
+    for mask in (3, 1, 2):
+        sent = lax.dynamic_index_in_dim(both, chip ^ mask, 0, keepdims=False)
+        kept = kept + swap(sent, "dp", 8, 2 * mask).astype(F32)
+    return kept.astype(BF16)
+
+
+def line_device(
+    tokens,
+    gate_weight,
+    up_weight,
+    down_weight,
+    adapter_proj_in,
+    adapter_lift_in,
+    adapter_proj_out,
+    adapter_lift_out,
+    token_request,
+    request_adapter,
+    adapter_slot,
+):
+    slot_of = lookup(lookup(token_request, request_adapter), adapter_slot)
+    gathered, slot_of = gather_dp(tokens, slot_of)
+    dp_index = lax.axis_index("dp")
+    tensor_index = lax.axis_index("tensor")
+    side = (tensor_index >> 1).astype(jnp.int32).reshape(1)
+    is_end = (tensor_index == 0) | (tensor_index == 3)
+    slot_dp = slot_of - dp_index * adapter_proj_in.shape[0]
+    slot_tensor = slot_of - tensor_index * adapter_lift_in.shape[0]
+    rank_part = rank_in_call(slot_dp[None, :], gathered, adapter_proj_in)
+    rank_in, mains = sum_everywhere(
+        rank_part,
+        [
+            (1, lambda tie: main_call(0, CHUNKS[0], after(gathered, tie), gate_weight)),
+            (2, lambda tie, before: main_call(0, CHUNKS[0], after(gathered, tie, before), up_weight)),
+        ],
+    )
+    rank_in = rank_in.astype(BF16)
+    slot_row = slot_tensor[None, :]
+    chunks = len(CHUNKS)
+    starts = [sum(CHUNKS[:c]) for c in range(chunks)]
+    near, far, hop, hidden_near, hidden_far = ({} for _ in range(5))
+
+    def operand(c, stage):
+        if stage == 0:
+            return far[c]
+        if stage == 1:
+            return (far[c].astype(F32) + hop[c].astype(F32)).astype(BF16)
+        if stage == 2:
+            return (near[c].astype(F32) + hop[c].astype(F32)).astype(BF16)
+        if stage == 3:
+            both = near[c].astype(F32) + hop[c].astype(F32)
+            hidden_near[c] = (jax.nn.silu(both[0]) * both[1]).astype(BF16)[None]
+            return hidden_near[c]
+        if stage == 4:
+            hidden_near[c] = jnp.where(is_end, hidden_near[c], hop[c])
+            return hop[c]
+        hidden_far[c] = hop[c]
+        return hop[c]
+
+    def pair(c):
+        return [hidden_near[c][0], jnp.where(is_end, hop[c], hidden_far[c])[0]]
+
+    def padded(value, shape):
+        return jnp.pad(value, [(0, b - a) for a, b in zip(value.shape, shape)])
+
+    near[0], far[0], spread = first_call(side, slot_row, rank_in, *mains, adapter_lift_in)
+    sums, ranks = None, None
+    for slot in range(chunks + 5):
+        live = [(slot - stage, stage) for stage in range(6) if 0 <= slot - stage < chunks]
+        values = {stage % 3: operand(c, stage) for c, stage in live}
+        if 0 in values and 2 in values:
+            shape = tuple(max(a, b) for a, b in zip(values[0].shape, values[2].shape))
+            outer = jnp.where(is_end, padded(values[0], shape), padded(values[2], shape))
+        else:
+            outer = values.get(0, values.get(2))
+        sent = [value for value in (outer, values.get(1)) if value is not None]
+        sent = list(lax.optimization_barrier(tuple(sent)))
+        arrived = {}
+        if outer is not None:
+            arrived[0] = lax.ppermute(sent[0], "tensor", OUTER)
+        if 1 in values:
+            arrived[1] = lax.ppermute(sent[-1], "tensor", MIDDLE)
+        made = ()
+        if slot + 1 < chunks:
+            made = into_call(
+                starts[slot + 1], CHUNKS[slot + 1], after(side, *sent), spread, gathered, gate_weight, up_weight, adapter_lift_in
+            )
+        done = slot - 6
+        if done == 0:
+            early = pair(0)
+            zero = jnp.zeros((adapter_proj_out.shape[1], gathered.shape[0]), F32)
+            ranks, _ = project_call(starts[0], 0, 1, after(side, *sent), slot_row, early, adapter_proj_out, zero)
+            sums = down_call(starts[0], after(side, ranks), early, down_weight, None)
+            made = (ranks, sums)
+        elif done > 0:
+            ranks, ahead = project_call(
+                starts[1], starts[2], CHUNKS[2], after(side, *sent), slot_row, pair(1), adapter_proj_out, ranks
+            )
+            made = (ranks, ahead)
+        *came, = lax.optimization_barrier((*arrived.values(), *made))
+        arrived = dict(zip(arrived, came))
+        made = came[len(arrived):]
+        if slot + 1 < chunks:
+            near[slot + 1], far[slot + 1] = made
+        elif done == 0:
+            ranks, sums = made
+        elif done > 0:
+            ranks, ahead = made
+        for c, stage in live:
+            value = arrived[stage % 3 % 2]
+            units, width = (2, 1)[stage // 3], CHUNKS[c] * CELL
+            hop[c] = value[:units, :, :width]
+    ranks = project_last_call(side, slot_row, pair(2), ahead, ranks)
+    rank_out, made = sum_everywhere(
+        ranks,
+        [
+            (1, lambda tie: down_call(starts[1], after(side, tie), pair(1), down_weight, sums, adapter_lift_out)),
+            (2, lambda tie, before: (down_call(starts[2], after(side, tie), pair(2), down_weight, before[0]), before[1])),
+        ],
+    )
+    return scatter_dp(last_call(slot_dp[None, :], rank_out.astype(BF16), *made[-1]))
+
+
 def solution(mesh):
+    on_line = mesh.shape["tensor"] == 4 and mesh.shape["dp"] == 8
     placed = (
         P("dp", "tensor"),
         P("tensor", "dp"),
@@ -97,5 +611,5 @@
         P(),
     )
     return jax.shard_map(
-        per_device, mesh=mesh, in_specs=placed, out_specs=P("dp", "tensor"), check_vma=False
-    )
+        line_device if on_line else general_device, mesh=mesh, in_specs=placed, out_specs=P("dp", "tensor"), check_vma=False
+    )

time: 296 us -> 151 us (0.51)
  blocking collectives: 91.6 us -> 0 us
  waiting for transfers between devices: 123 us -> 51.7 us
  matrix products: 62.2 us -> 0 us
  starting transfers between devices: 0.09 us -> 48.5 us
  Pallas kernels: 0 us -> 37.5 us
  between operations: 13.2 us -> 0.58 us
  other arithmetic: 4.72 us -> 8.89 us
  local copies, waits for them, and re-layouts: 0.01 us -> 3.45 us
    reduce_scatter x2 -> x0, waiting for transfers between devices: 89.5 us -> none  [the longest x1 54.7 us: per_device(): lax.psum_scatter((jnp.stack([gate_part, up_part], axis=1) + extra).astype...]
    psum x2 -> x0, blocking collectives: 79.4 us -> none  [the longest x1 39.7 us: per_device(): rank_in = lax.psum(rank_part, ('dp', 'tensor')).astype(jnp.bfloat16)]
    dot_general x7 -> x0, matrix products: 62.2 us -> none  [the longest x1 24.2 us: per_device(): jnp.einsum('tscr,scrf->tcf', spread, adapter_lift_in, preferred_element_t...]
    ppermute x0 -> x34, waiting for transfers between devices: none -> 51.7 us  [the longest x8 31 us: line_device(): arrived[0] = lax.ppermute(sent[0], 'tensor', OUTER)]
    ppermute x0 -> x34, starting transfers between devices: none -> 48.5 us  [the longest x20 23.1 us: swap(): return lax.ppermute(value, axis, [(i, i ^ mask) for i in range(size)])]
    pallas_call x0 -> x13, Pallas kernels: none -> 37.5 us  [the longest x2 12.6 us: into_call(): call(functools.partial(into_kernel, first), 'into', [IN_SMEM, IN_VMEM, IN...]
    all_gather x1 -> x0, waiting for transfers between devices: 33.7 us -> none  [per_device(): hidden_all = lax.all_gather(hidden, 'tensor', axis=0, tiled=True)]
    all_gather x1 -> x0, blocking collectives: 12.2 us -> none  [per_device(): gathered = lax.all_gather(tokens, 'dp', axis=0, tiled=True)]
  transfers between devices with their start and end apart: 3 -> 34, of which waited for: 3 -> 21; matrix products, arithmetic and copies ran while one was open for 0% -> 1% of each run, Pallas kernels for 0% -> 21%
where the time goes in v3:
time: 151 us
  waiting for transfers between devices  51.7 us (34%)
  starting transfers between devices  48.5 us (32%)
  Pallas kernels  37.5 us (25%)
  other arithmetic  8.89 us (6%)
  local copies, waits for them, and re-layouts  3.45 us (2%)
    ppermute x8, waiting for transfers between devices, line_device(): arrived[0] = lax.ppermute(sent[0], 'tensor', OUTER)  31 us
    ppermute x20, starting transfers between devices, swap(): return lax.ppermute(value, axis, [(i, i ^ mask) for i in range(size)])  23.1 us
    ppermute x20, waiting for transfers between devices, swap(): return lax.ppermute(value, axis, [(i, i ^ mask) for i in range(size)])  20.7 us
    ppermute x8, starting transfers between devices, line_device(): arrived[0] = lax.ppermute(sent[0], 'tensor', OUTER)  20.4 us
    pallas_call x2, Pallas kernels, into_call(): call(functools.partial(into_kernel, first), 'into', [IN_SMEM, IN_VMEM, IN...  12.6 us
    pallas_call x3, Pallas kernels, down_call(): call(functools.partial(down_kernel, first, len(bring)), 'down', [IN_SMEM,...  8.44 us
    pallas_call x2, Pallas kernels, main_call(): call(functools.partial(main_kernel, first), 'main', [IN_VMEM, ANYWHERE],...  5.2 us
    ppermute x6, starting transfers between devices, line_device(): arrived[1] = lax.ppermute(sent[-1], 'tensor', MIDDLE)  4.94 us
  transfers between devices with their start and end apart: 34, of which 21 were waited for; matrix products, arithmetic and copies ran while one was open for 1% of the time, Pallas kernels for 21%

profile of v3, /device:TPU:0, one launch (start us, length us, event | category | flops | bytes accessed | tf_op | source)
XLA Modules:
  0.0 150.6 jit_solution(11888199507621357171)
XLA Ops:
  0.0 2.9 %collective-permute-start = (bf16[24,2048]{1,0:T(8,128)(2,1)}, bf16[24,2048]{1,0:T(8,128)(2,1)S(1)}, u32[]{:S(2)}, u32[]{:S(2)}) collective-permute-start(bf16[24,2048]{1,0:T(8,128)(2,1)} %param.11), channel_id=1, source_target_pairs={{0,8},{4,12},{8,0},{12,4},{16,24},{20,28},{24,16},{28,20},{1,9},{5... | collective-permute-start | bytes 294920 | tf_op jit(solution)/shard_map/ppermute | solution.py:437
  6.3 2.5 %collective-permute-done.1 = bf16[24,2048]{1,0:T(8,128)(2,1)S(1)} collective-permute-done((bf16[24,2048]{1,0:T(8,128)(2,1)}, bf16[24,2048]{1,0:T(8,128)(2,1)S(1)}, u32[]{:S(2)}, u32[]{:S(2)}) %collective-permute-start.1) | collective-permute-done | bytes 98336 | tf_op jit(solution)/shard_map/ppermute | solution.py:437
  22.0 2.6 %main.2.gate_ref = f32[192,1024]{1,0:T(8,128)S(1)} custom-call(bf16[192,2048]{1,0:T(8,128)(2,1)S(1)} %bitcast.42, bf16[2048,3584]{1,0:T(8,128)(2,1)} %gate_ref.3), custom_call_target="tpu_custom_call" | custom-call | flops 1024 | bytes 1024 | tf_op jit(solution)/shard_map/main/pallas_call | solution.py:234
  26.5 2.6 %main.3.up_ref = f32[192,1024]{1,0:T(8,128)S(1)} custom-call(bf16[192,2048]{1,0:T(8,128)(2,1)S(1)} %bitcast.43, bf16[2048,3584]{1,0:T(8,128)(2,1)} %up_ref.3), custom_call_target="tpu_custom_call" | custom-call | flops 1024 | bytes 1024 | tf_op jit(solution)/shard_map/main/pallas_call | solution.py:234
  29.1 2.7 %collective-permute-start.9 = (f32[32,192]{1,0:T(8,128)S(1)}, f32[32,192]{1,0:T(8,128)S(1)}, u32[]{:S(2)}, u32[]{:S(2)}) collective-permute-start(f32[32,192]{1,0:T(8,128)S(1)} %add.122), channel_id=1, source_target_pairs={{0,2},{1,3},{2,0},{3,1},{4,6},{5,7},{6,4},{7,5},{8,10},{9,11},{10,... | collective-permute-start | bytes 73736 | tf_op jit(solution)/shard_map/ppermute | solution.py:437
  34.0 2.7 %first.1 = (bf16[2,96,1024]{2,1,0:T(8,128)(2,1)S(1)}, bf16[2,96,1024]{2,1,0:T(8,128)(2,1)S(1)}, bf16[2,192,1024]{2,1,0:T(8,128)(2,1)S(1)}) custom-call(s32[1]{0:T(128)} %bitcast.5.side_ref, s32[1,192]{1,0:T(1,128)S(1)} %bitcast.48, bf16[32,192]{1,0:T(8,128)(2,1)S(1)} %add_convert_fusion.3.rank_ref, f32[192,1024]{1,0:T(8,128)S(1)} %main.2.gate_ref, ...), custom_call_target="tpu_custom_call" | custom-call | flops 1024 | bytes 1024 | tf_op jit(solution)/shard_map/first/pallas_call | solution.py:264
  38.0 6.3 %into.2 = (bf16[2,96,1280]{2,1,0:T(8,128)(2,1)S(1)}, bf16[2,96,1280]{2,1,0:T(8,128)(2,1)S(1)}) custom-call(s32[1]{0:T(128)} %bitcast.5.side_ref, bf16[192,2048]{1,0:T(8,128)(2,1)S(1)} %bitcast.44, bf16[2,192,1024]{2,1,0:T(8,128)(2,1)S(1)} %get-tuple-element.88.spread_ref, bf16[2048,3584]{1,0:T(8,128)(2,1)} %gate_ref.3, bf16[2048,3584]{1,0:T(8,128)(2,1)} %up_ref.3, ...), custom_call_target="tpu_custom_call" | custom-call | flops 1024 | bytes 1024 | tf_op jit(solution)/shard_map/into/pallas_call | solution.py:293
  48.4 6.3 %into.3 = (bf16[2,96,1280]{2,1,0:T(8,128)(2,1)S(1)}, bf16[2,96,1280]{2,1,0:T(8,128)(2,1)S(1)}) custom-call(s32[1]{0:T(128)} %bitcast.5.side_ref, bf16[192,2048]{1,0:T(8,128)(2,1)S(1)} %bitcast.45, bf16[2,192,1024]{2,1,0:T(8,128)(2,1)S(1)} %get-tuple-element.88.spread_ref, bf16[2048,3584]{1,0:T(8,128)(2,1)} %gate_ref.3, bf16[2048,3584]{1,0:T(8,128)(2,1)} %up_ref.3, ...), custom_call_target="tpu_custom_call" | custom-call | flops 1024 | bytes 1024 | tf_op jit(solution)/shard_map/into/pallas_call | solution.py:293
  54.7 2.2 %collective-permute-done.11 = bf16[2,96,1280]{2,1,0:T(8,128)(2,1)} collective-permute-done((bf16[2,96,1280]{2,1,0:T(8,128)(2,1)S(1)}, bf16[2,96,1280]{2,1,0:T(8,128)(2,1)}, u32[]{:S(2)}, u32[]{:S(2)}) %collective-permute-start.11) | collective-permute-done | bytes 491552 | tf_op jit(solution)/shard_map/ppermute | solution.py:554
  62.0 6.6 %collective-permute-done.13 = bf16[2,96,1280]{2,1,0:T(8,128)(2,1)S(1)} collective-permute-done((bf16[2,96,1280]{2,1,0:T(8,128)(2,1)S(1)}, bf16[2,96,1280]{2,1,0:T(8,128)(2,1)S(1)}, u32[]{:S(2)}, u32[]{:S(2)}) %collective-permute-start.13) | collective-permute-done | bytes 491552 | tf_op jit(solution)/shard_map/ppermute | solution.py:554
  69.2 3.7 %collective-permute-start.15 = (bf16[2,96,1280]{2,1,0:T(8,128)(2,1)S(1)}, bf16[2,96,1280]{2,1,0:T(8,128)(2,1)S(1)}, u32[]{:S(2)}, u32[]{:S(2)}) collective-permute-start(bf16[2,96,1280]{2,1,0:T(8,128)(2,1)S(1)} %fusion.4), channel_id=1, source_target_pairs={{0,1},{1,0},{2,3},{3,2},{4,5},{5,4},{6,7},{7,6},{8,9},{9,8},{10,11... | collective-permute-start | bytes 1474568 | tf_op jit(solution)/shard_map/ppermute | solution.py:554
  73.6 6.3 %collective-permute-done.15 = bf16[2,96,1280]{2,1,0:T(8,128)(2,1)S(1)} collective-permute-done((bf16[2,96,1280]{2,1,0:T(8,128)(2,1)S(1)}, bf16[2,96,1280]{2,1,0:T(8,128)(2,1)S(1)}, u32[]{:S(2)}, u32[]{:S(2)}) %collective-permute-start.15) | collective-permute-done | bytes 491552 | tf_op jit(solution)/shard_map/ppermute | solution.py:554
  80.5 4.7 %collective-permute-start.17 = (bf16[2,96,1280]{2,1,0:T(8,128)(2,1)S(1)}, bf16[2,96,1280]{2,1,0:T(8,128)(2,1)S(1)}, u32[]{:S(2)}, u32[]{:S(2)}) collective-permute-start(bf16[2,96,1280]{2,1,0:T(8,128)(2,1)S(1)} %fusion.5), channel_id=1, source_target_pairs={{0,1},{1,0},{2,3},{3,2},{4,5},{5,4},{6,7},{7,6},{8,9},{9,8},{10,11... | collective-permute-start | bytes 1474568 | tf_op jit(solution)/shard_map/ppermute | solution.py:554
  85.8 8.8 %collective-permute-done.17 = bf16[2,96,1280]{2,1,0:T(8,128)(2,1)S(1)} collective-permute-done((bf16[2,96,1280]{2,1,0:T(8,128)(2,1)S(1)}, bf16[2,96,1280]{2,1,0:T(8,128)(2,1)S(1)}, u32[]{:S(2)}, u32[]{:S(2)}) %collective-permute-start.17) | collective-permute-done | bytes 491552 | tf_op jit(solution)/shard_map/ppermute | solution.py:554
  97.8 3.9 %collective-permute-done.19 = bf16[1,96,1280]{2,1,0:T(8,128)(2,1)S(1)} collective-permute-done((bf16[1,96,1280]{2,1,0:T(8,128)(2,1)S(1)}, bf16[1,96,1280]{2,1,0:T(8,128)(2,1)S(1)}, u32[]{:S(2)}, u32[]{:S(2)}) %collective-permute-start.19) | collective-permute-done | bytes 245792 | tf_op jit(solution)/shard_map/ppermute | solution.py:554
  101.7 3.6 %collective-permute-start.21 = (bf16[1,96,1280]{2,1,0:T(8,128)(2,1)S(1)}, bf16[1,96,1280]{2,1,0:T(8,128)(2,1)S(1)}, u32[]{:S(2)}, u32[]{:S(2)}) collective-permute-start(bf16[1,96,1280]{2,1,0:T(8,128)(2,1)S(1)} %collective-permute-done.20), channel_id=1, source_target_pairs={{0,1},{1,0},{2,3},{3,2},{4,5},{5,4},{6,7},{7,6},{8,9},{9,8},{10,11... | collective-permute-start | bytes 737288 | tf_op jit(solution)/shard_map/ppermute | solution.py:554
  106.1 2.4 %project.3 = (f32[16,192]{1,0:T(8,128)S(1)}, bf16[4,16,16,256]{3,2,1,0:T(8,128)(2,1)}) custom-call(s32[1]{0:T(128)} %bitcast.5.side_ref, s32[1,192]{1,0:T(1,128)S(1)} %bitcast.49, bf16[96,1024]{1,0:T(8,128)(2,1)S(1)} %get-tuple-element.157.near_ref, bf16[96,1024]{1,0:T(8,128)(2,1)S(1)} %select_bitcast_fusion.4.far_ref, bf16[64,16,3584]{2,1,0:T(8,128)(2,1)S(1)} %bitcast.40, ...), custom_call_target="tpu_custom_call" | custom-call | flops 1024 | bytes 1024 | tf_op jit(solution)/shard_map/project/pallas_call | solution.py:339
  108.5 2.6 %down.3.rest_0_ = f32[192,2048]{1,0:T(8,128)S(1)} custom-call(s32[1]{0:T(128)} %bitcast.5.side_ref, bf16[96,1024]{1,0:T(8,128)(2,1)S(1)} %get-tuple-element.157.near_ref, bf16[96,1024]{1,0:T(8,128)(2,1)S(1)} %select_bitcast_fusion.4.far_ref, bf16[3584,2048]{1,0:T(8,128)(2,1)} %down_ref.5), custom_call_target="tpu_custom_call" | custom-call | flops 1024 | bytes 1024 | tf_op jit(solution)/shard_map/down/pallas_call | solution.py:406
  111.1 2.9 %collective-permute-start.23 = (bf16[1,96,1280]{2,1,0:T(8,128)(2,1)S(1)}, bf16[1,96,1280]{2,1,0:T(8,128)(2,1)S(1)}, u32[]{:S(2)}, u32[]{:S(2)}) collective-permute-start(bf16[1,96,1280]{2,1,0:T(8,128)(2,1)S(1)} %collective-permute-done.22), channel_id=1, source_target_pairs={{0,1},{1,0},{2,3},{3,2},{4,5},{5,4},{6,7},{7,6},{8,9},{9,8},{10,11... | collective-permute-start | bytes 737288 | tf_op jit(solution)/shard_map/ppermute | solution.py:554
  114.1 2.5 %project.4 = (f32[16,192]{1,0:T(8,128)S(1)}, bf16[4,16,16,1280]{3,2,1,0:T(8,128)(2,1)S(1)}) custom-call(s32[1]{0:T(128)} %bitcast.5.side_ref, s32[1,192]{1,0:T(1,128)S(1)} %bitcast.50, bf16[96,1280]{1,0:T(8,128)(2,1)S(1)} %get-tuple-element.155.near_ref, bf16[96,1280]{1,0:T(8,128)(2,1)S(1)} %select_bitcast_fusion.1.far_ref, ...), custom_call_target="tpu_custom_call" | custom-call | flops 1024 | bytes 1024 | tf_op jit(solution)/shard_map/project/pallas_call | solution.py:339
  124.1 2.9 %down.4 = (f32[192,2048]{1,0:T(8,128)S(1)}, bf16[32,16,2048]{2,1,0:T(8,128)(2,1)S(1)}) custom-call(s32[1]{0:T(128)} %bitcast.5.side_ref, bf16[96,1280]{1,0:T(8,128)(2,1)S(1)} %get-tuple-element.155.near_ref, bf16[96,1280]{1,0:T(8,128)(2,1)S(1)} %select_bitcast_fusion.1.far_ref, bf16[3584,2048]{1,0:T(8,128)(2,1)} %down_ref.5, f32[192,2048]{1,0:T(8,128)S(1)} %down.3.rest_0_, ...), custom_call_target="tpu_custom_call" | custom-call | flops 1024 | bytes 1024 | tf_op jit(solution)/shard_map/down/pallas_call | solution.py:406
  129.8 2.9 %down.5.sum_ref = f32[192,2048]{1,0:T(8,128)S(1)} custom-call(s32[1]{0:T(128)} %bitcast.5.side_ref, bf16[96,1280]{1,0:T(8,128)(2,1)S(1)} %get-tuple-element.165.near_ref, bf16[96,1280]{1,0:T(8,128)(2,1)S(1)} %get-tuple-element.164.far_ref, bf16[3584,2048]{1,0:T(8,128)(2,1)} %down_ref.5, f32[192,2048]{1,0:T(8,128)S(1)} %get-tuple-element.142.rest_0_), custom_call_target="tpu_custom_call" | custom-call | flops 1024 | bytes 1024 | tf_op jit(solution)/shard_map/down/pallas_call | solution.py:406
  134.0 3.5 %collective-permute-done.29 = f32[16,192]{1,0:T(8,128)S(1)} collective-permute-done((f32[16,192]{1,0:T(8,128)S(1)}, f32[16,192]{1,0:T(8,128)S(1)}, u32[]{:S(2)}, u32[]{:S(2)}) %collective-permute-start.29) | collective-permute-done | bytes 12320 | tf_op jit(solution)/shard_map/ppermute | solution.py:437
  145.5 3.1 %collective-permute-done.31 = bf16[24,2048]{1,0:T(8,128)(2,1)S(1)} collective-permute-done((bf16[24,2048]{1,0:T(8,128)(2,1)S(1)}, bf16[24,2048]{1,0:T(8,128)(2,1)S(1)}, u32[]{:S(2)}, u32[]{:S(2)}) %collective-permute-start.31) | collective-permute-done | bytes 98336 | tf_op jit(solution)/shard_map/ppermute | solution.py:437
  (111 shorter events, 58.8 us)
Async XLA Ops:
  0.0 6.3 %collective-permute-start = (bf16[24,2048]{1,0:T(8,128)(2,1)}, bf16[24,2048]{1,0:T(8,128)(2,1)S(1)}, u32[]{:S(2)}, u32[]{:S(2)}) collective-permute-start(bf16[24,2048]{1,0:T(8,128)(2,1)} %param.11), channel_id=1, source_target_pairs={{0,8},{4,12},{8,0},{12,4},{16,24},{20,28},{24,16},{28,20},{1,9},{5... | collective-permute-start | bytes 294920 | tf_op jit(solution)/shard_map/ppermute | solution.py:437
  2.9 5.9 %collective-permute-start.1 = (bf16[24,2048]{1,0:T(8,128)(2,1)}, bf16[24,2048]{1,0:T(8,128)(2,1)S(1)}, u32[]{:S(2)}, u32[]{:S(2)}) collective-permute-start(bf16[24,2048]{1,0:T(8,128)(2,1)} %param.11), channel_id=1, source_target_pairs={{0,16},{4,20},{8,24},{12,28},{16,0},{20,4},{24,8},{28,12},{1,17},{... | collective-permute-start | bytes 294920 | tf_op jit(solution)/shard_map/ppermute | solution.py:437
  4.5 5.7 %collective-permute-start.2 = (bf16[24,2048]{1,0:T(8,128)(2,1)}, bf16[24,2048]{1,0:T(8,128)(2,1)S(1)}, u32[]{:S(2)}, u32[]{:S(2)}) collective-permute-start(bf16[24,2048]{1,0:T(8,128)(2,1)} %param.11), channel_id=1, source_target_pairs={{0,24},{4,28},{8,16},{12,20},{16,8},{20,12},{24,0},{28,4},{1,25},{... | collective-permute-start | bytes 294920 | tf_op jit(solution)/shard_map/ppermute | solution.py:437
  18.5 6.1 %collective-permute-start.5 = (f32[32,192]{1,0:T(8,128)S(1)}, f32[32,192]{1,0:T(8,128)S(1)}, u32[]{:S(2)}, u32[]{:S(2)}) collective-permute-start(f32[32,192]{1,0:T(8,128)S(1)} %add.118), channel_id=1, source_target_pairs={{0,24},{4,28},{8,16},{12,20},{16,8},{20,12},{24,0},{28,4},{1,25},{... | collective-permute-start | bytes 73736 | tf_op jit(solution)/shard_map/ppermute | solution.py:437
  19.5 5.2 %collective-permute-start.6 = (f32[32,192]{1,0:T(8,128)S(1)}, f32[32,192]{1,0:T(8,128)S(1)}, u32[]{:S(2)}, u32[]{:S(2)}) collective-permute-start(f32[32,192]{1,0:T(8,128)S(1)} %add.118), channel_id=1, source_target_pairs={{0,8},{4,12},{8,0},{12,4},{16,24},{20,28},{24,16},{28,20},{1,9},{5... | collective-permute-start | bytes 73736 | tf_op jit(solution)/shard_map/ppermute | solution.py:437
  29.1 4.9 %collective-permute-start.9 = (f32[32,192]{1,0:T(8,128)S(1)}, f32[32,192]{1,0:T(8,128)S(1)}, u32[]{:S(2)}, u32[]{:S(2)}) collective-permute-start(f32[32,192]{1,0:T(8,128)S(1)} %add.122), channel_id=1, source_target_pairs={{0,2},{1,3},{2,0},{3,1},{4,6},{5,7},{6,4},{7,5},{8,10},{9,11},{10,... | collective-permute-start | bytes 73736 | tf_op jit(solution)/shard_map/ppermute | solution.py:437
  36.7 9.1 %collective-permute-start.10 = (bf16[2,96,1024]{2,1,0:T(8,128)(2,1)S(1)}, bf16[2,96,1024]{2,1,0:T(8,128)(2,1)S(1)}, u32[]{:S(2)}, u32[]{:S(2)}) collective-permute-start(bf16[2,96,1024]{2,1,0:T(8,128)(2,1)S(1)} %get-tuple-element.86), channel_id=1, source_target_pairs={{0,1},{1,0},{2,3},{3,2},{4,5},{5,4},{6,7},{7,6},{8,9},{9,8},{10,11... | collective-permute-start | bytes 1179656 | tf_op jit(solution)/shard_map/ppermute | solution.py:554
  46.7 10.3 %collective-permute-start.11 = (bf16[2,96,1280]{2,1,0:T(8,128)(2,1)S(1)}, bf16[2,96,1280]{2,1,0:T(8,128)(2,1)}, u32[]{:S(2)}, u32[]{:S(2)}) collective-permute-start(bf16[2,96,1280]{2,1,0:T(8,128)(2,1)S(1)} %get-tuple-element.93), channel_id=1, source_target_pairs={{0,1},{1,0},{2,3},{3,2},{4,5},{5,4},{6,7},{7,6},{8,9},{9,8},{10,11... | collective-permute-start | bytes 1474568 | tf_op jit(solution)/shard_map/ppermute | solution.py:554
  46.9 7.8 %collective-permute-start.12 = (bf16[2,96,1024]{2,1,0:T(8,128)(2,1)}, bf16[2,96,1024]{2,1,0:T(8,128)(2,1)}, u32[]{:S(2)}, u32[]{:S(2)}) collective-permute-start(bf16[2,96,1024]{2,1,0:T(8,128)(2,1)} %add_convert_fusion.2), channel_id=1, source_target_pairs={{1,2},{2,1},{5,6},{6,5},{9,10},{10,9},{13,14},{14,13},{17,18},{18,... | collective-permute-start | bytes 1179656 | tf_op jit(solution)/shard_map/ppermute | solution.py:556
  59.3 9.3 %collective-permute-start.13 = (bf16[2,96,1280]{2,1,0:T(8,128)(2,1)S(1)}, bf16[2,96,1280]{2,1,0:T(8,128)(2,1)S(1)}, u32[]{:S(2)}, u32[]{:S(2)}) collective-permute-start(bf16[2,96,1280]{2,1,0:T(8,128)(2,1)S(1)} %pad_select_fusion), channel_id=1, source_target_pairs={{0,1},{1,0},{2,3},{3,2},{4,5},{5,4},{6,7},{7,6},{8,9},{9,8},{10,11... | collective-permute-start | bytes 1474568 | tf_op jit(solution)/shard_map/ppermute | solution.py:554
  61.1 7.5 %collective-permute-start.14 = (bf16[2,96,1280]{2,1,0:T(8,128)(2,1)S(1)}, bf16[2,96,1280]{2,1,0:T(8,128)(2,1)S(1)}, u32[]{:S(2)}, u32[]{:S(2)}) collective-permute-start(bf16[2,96,1280]{2,1,0:T(8,128)(2,1)S(1)} %add_convert_fusion.1), channel_id=1, source_target_pairs={{1,2},{2,1},{5,6},{6,5},{9,10},{10,9},{13,14},{14,13},{17,18},{18,... | collective-permute-start | bytes 1474568 | tf_op jit(solution)/shard_map/ppermute | solution.py:556
  69.2 10.7 %collective-permute-start.15 = (bf16[2,96,1280]{2,1,0:T(8,128)(2,1)S(1)}, bf16[2,96,1280]{2,1,0:T(8,128)(2,1)S(1)}, u32[]{:S(2)}, u32[]{:S(2)}) collective-permute-start(bf16[2,96,1280]{2,1,0:T(8,128)(2,1)S(1)} %fusion.4), channel_id=1, source_target_pairs={{0,1},{1,0},{2,3},{3,2},{4,5},{5,4},{6,7},{7,6},{8,9},{9,8},{10,11... | collective-permute-start | bytes 1474568 | tf_op jit(solution)/shard_map/ppermute | solution.py:554
  72.9 7.0 %collective-permute-start.16 = (bf16[2,96,1280]{2,1,0:T(8,128)(2,1)S(1)}, bf16[2,96,1280]{2,1,0:T(8,128)(2,1)S(1)}, u32[]{:S(2)}, u32[]{:S(2)}) collective-permute-start(bf16[2,96,1280]{2,1,0:T(8,128)(2,1)S(1)} %add_convert_fusion), channel_id=1, source_target_pairs={{1,2},{2,1},{5,6},{6,5},{9,10},{10,9},{13,14},{14,13},{17,18},{18,... | collective-permute-start | bytes 1474568 | tf_op jit(solution)/shard_map/ppermute | solution.py:556
  80.5 14.1 %collective-permute-start.17 = (bf16[2,96,1280]{2,1,0:T(8,128)(2,1)S(1)}, bf16[2,96,1280]{2,1,0:T(8,128)(2,1)S(1)}, u32[]{:S(2)}, u32[]{:S(2)}) collective-permute-start(bf16[2,96,1280]{2,1,0:T(8,128)(2,1)S(1)} %fusion.5), channel_id=1, source_target_pairs={{0,1},{1,0},{2,3},{3,2},{4,5},{5,4},{6,7},{7,6},{8,9},{9,8},{10,11... | collective-permute-start | bytes 1474568 | tf_op jit(solution)/shard_map/ppermute | solution.py:554
  95.0 6.7 %collective-permute-start.19 = (bf16[1,96,1280]{2,1,0:T(8,128)(2,1)S(1)}, bf16[1,96,1280]{2,1,0:T(8,128)(2,1)S(1)}, u32[]{:S(2)}, u32[]{:S(2)}) collective-permute-start(bf16[1,96,1280]{2,1,0:T(8,128)(2,1)S(1)} %get-tuple-element.116), channel_id=1, source_target_pairs={{0,1},{1,0},{2,3},{3,2},{4,5},{5,4},{6,7},{7,6},{8,9},{9,8},{10,11... | collective-permute-start | bytes 737288 | tf_op jit(solution)/shard_map/ppermute | solution.py:554
  101.7 9.4 %collective-permute-start.21 = (bf16[1,96,1280]{2,1,0:T(8,128)(2,1)S(1)}, bf16[1,96,1280]{2,1,0:T(8,128)(2,1)S(1)}, u32[]{:S(2)}, u32[]{:S(2)}) collective-permute-start(bf16[1,96,1280]{2,1,0:T(8,128)(2,1)S(1)} %collective-permute-done.20), channel_id=1, source_target_pairs={{0,1},{1,0},{2,3},{3,2},{4,5},{5,4},{6,7},{7,6},{8,9},{9,8},{10,11... | collective-permute-start | bytes 737288 | tf_op jit(solution)/shard_map/ppermute | solution.py:554
  105.3 5.7 %collective-permute-start.22 = (bf16[1,96,1280]{2,1,0:T(8,128)(2,1)S(1)}, bf16[1,96,1280]{2,1,0:T(8,128)(2,1)S(1)}, u32[]{:S(2)}, u32[]{:S(2)}) collective-permute-start(bf16[1,96,1280]{2,1,0:T(8,128)(2,1)S(1)} %collective-permute-done.19), channel_id=1, source_target_pairs={{1,2},{2,1},{5,6},{6,5},{9,10},{10,9},{13,14},{14,13},{17,18},{18,... | collective-permute-start | bytes 737288 | tf_op jit(solution)/shard_map/ppermute | solution.py:556
  111.1 7.1 %collective-permute-start.23 = (bf16[1,96,1280]{2,1,0:T(8,128)(2,1)S(1)}, bf16[1,96,1280]{2,1,0:T(8,128)(2,1)S(1)}, u32[]{:S(2)}, u32[]{:S(2)}) collective-permute-start(bf16[1,96,1280]{2,1,0:T(8,128)(2,1)S(1)} %collective-permute-done.22), channel_id=1, source_target_pairs={{0,1},{1,0},{2,3},{3,2},{4,5},{5,4},{6,7},{7,6},{8,9},{9,8},{10,11... | collective-permute-start | bytes 737288 | tf_op jit(solution)/shard_map/ppermute | solution.py:554
  120.4 6.6 %collective-permute-start.25 = (f32[16,192]{1,0:T(8,128)S(1)}, f32[16,192]{1,0:T(8,128)S(1)}, u32[]{:S(2)}, u32[]{:S(2)}) collective-permute-start(f32[16,192]{1,0:T(8,128)S(1)} %add.136), channel_id=1, source_target_pairs={{0,24},{4,28},{8,16},{12,20},{16,8},{20,12},{24,0},{28,4},{1,25},{... | collective-permute-start | bytes 36872 | tf_op jit(solution)/shard_map/ppermute | solution.py:437
  127.8 5.0 %collective-permute-start.28 = (f32[16,192]{1,0:T(8,128)S(1)}, f32[16,192]{1,0:T(8,128)S(1)}, u32[]{:S(2)}, u32[]{:S(2)}) collective-permute-start(f32[16,192]{1,0:T(8,128)S(1)} %add_add_fusion.1), channel_id=1, source_target_pairs={{0,1},{1,0},{2,3},{3,2},{4,5},{5,4},{6,7},{7,6},{8,9},{9,8},{10,11... | collective-permute-start | bytes 36872 | tf_op jit(solution)/shard_map/ppermute | solution.py:437
  132.8 4.7 %collective-permute-start.29 = (f32[16,192]{1,0:T(8,128)S(1)}, f32[16,192]{1,0:T(8,128)S(1)}, u32[]{:S(2)}, u32[]{:S(2)}) collective-permute-start(f32[16,192]{1,0:T(8,128)S(1)} %add.140), channel_id=1, source_target_pairs={{0,2},{1,3},{2,0},{3,1},{4,6},{5,7},{6,4},{7,5},{8,10},{9,11},{10,... | collective-permute-start | bytes 36872 | tf_op jit(solution)/shard_map/ppermute | solution.py:437
  142.0 6.6 %collective-permute-start.31 = (bf16[24,2048]{1,0:T(8,128)(2,1)S(1)}, bf16[24,2048]{1,0:T(8,128)(2,1)S(1)}, u32[]{:S(2)}, u32[]{:S(2)}) collective-permute-start(bf16[24,2048]{1,0:T(8,128)(2,1)S(1)} %get-tuple-element.159), channel_id=1, source_target_pairs={{0,24},{4,28},{8,16},{12,20},{16,8},{20,12},{24,0},{28,4},{1,25},{... | collective-permute-start | bytes 294920 | tf_op jit(solution)/shard_map/ppermute | solution.py:437
  143.3 6.5 %collective-permute-start.32 = (bf16[24,2048]{1,0:T(8,128)(2,1)S(1)}, bf16[24,2048]{1,0:T(8,128)(2,1)S(1)}, u32[]{:S(2)}, u32[]{:S(2)}) collective-permute-start(bf16[24,2048]{1,0:T(8,128)(2,1)S(1)} %get-tuple-element.161), channel_id=1, source_target_pairs={{0,8},{4,12},{8,0},{12,4},{16,24},{20,28},{24,16},{28,20},{1,9},{5... | collective-permute-start | bytes 294920 | tf_op jit(solution)/shard_map/ppermute | solution.py:437
  144.8 5.1 %collective-permute-start.33 = (bf16[24,2048]{1,0:T(8,128)(2,1)S(1)}, bf16[24,2048]{1,0:T(8,128)(2,1)S(1)}, u32[]{:S(2)}, u32[]{:S(2)}) collective-permute-start(bf16[24,2048]{1,0:T(8,128)(2,1)S(1)} %get-tuple-element.160), channel_id=1, source_target_pairs={{0,16},{4,20},{8,24},{12,28},{16,0},{20,4},{24,8},{28,12},{1,17},{... | collective-permute-start | bytes 294920 | tf_op jit(solution)/shard_map/ppermute | solution.py:437
  (16 other events, 107.6 us)

commit v4 on v3

--- a/solution.py
+++ b/solution.py
@@ -148,36 +148,12 @@
 
 
 def rank_in_kernel(slot_ref, rows_ref, proj_ref, out_ref):
-    step = pl.program_id(0)
-    part = masked_project(proj_ref[...], rows_ref[...], slot_ref[...], step * proj_ref.shape[0])
-
-    @pl.when(step == 0)
-    def _():
-        out_ref[...] = part
-
-    @pl.when(step > 0)
-    def _():
-        out_ref[...] += part
+    out_ref[...] = masked_project(proj_ref[...], rows_ref[...], slot_ref[...], 0)
 
 
 def rank_in_call(slot_row, rows, proj):
-    slots, rank, depth = proj.shape
-    total = rows.shape[0]
-    group = 8
-    return pl.pallas_call(
-        rank_in_kernel,
-        grid=(slots // group,),
-        in_specs=[
-            pl.BlockSpec((1, total), lambda s: (0, 0)),
-            pl.BlockSpec((total, depth), lambda s: (0, 0)),
-            pl.BlockSpec((group, rank, depth), lambda s: (s, 0, 0)),
-        ],
-        out_specs=pl.BlockSpec((rank, total), lambda s: (0, 0)),
-        out_shape=jax.ShapeDtypeStruct((rank, total), F32),
-        compiler_params=pltpu.CompilerParams(vmem_limit_bytes=VMEM_LIMIT),
-        cost_estimate=LIGHT,
-        name="rank_in",
-    )(slot_row, rows, proj)
+    outs = jax.ShapeDtypeStruct((proj.shape[1], rows.shape[0]), F32)
+    return call(rank_in_kernel, "rank_in", [IN_VMEM] * 3, outs, [])(slot_row, rows, proj)
 
 
 def half_rows(side, which, half):
@@ -270,39 +246,40 @@
     )(side, slot_row, rank_t, gate, up, lift)
 
 
-def into_kernel(first, side_ref, rows_ref, spread_ref, gate_ref, up_ref, lift_ref, near_ref, far_ref, total_ref, gate_held, up_held, lift_buf, sems):
-    blocks = gate_held.shape[0]
-    parts = []
-    for pair in zip(weight_parts(gate_ref, gate_held, first), weight_parts(up_ref, up_held, first)):
-        parts += pair
-    copies = fetch(parts + lift_parts(lift_ref, lift_buf, first), sems)
-    for k in range(blocks):
-        for c, held in ((0, gate_held), (1, up_held)):
-            copies[2 * k + c].wait()
-            add_product(total_ref.at[c], k == 0, rows_ref[:, k * ROWS:(k + 1) * ROWS], held[k])
-    for g, copy in enumerate(copies[2 * blocks:]):
+def into_kernel(first, ready, side_ref, rows_ref, spread_ref, gate_ref, up_ref, lift_ref, near_ref, far_ref, total_ref, held_ref, lift_buf, sems):
+    gates = [(gate_ref, total_ref.at[0])] if ready else weight_parts(gate_ref, held_ref.at[1], first)
+    ups = weight_parts(up_ref, held_ref.at[0], first)
+    lifts = lift_parts(lift_ref, lift_buf, first)
+    copies = fetch(gates + ups + lifts, sems)
+    at = 0
+    for c, count in ((0, len(gates)), (1, len(ups))):
+        for k in range(count):
+            copies[at].wait()
+            at += 1
+            if c == 1 or not ready:
+                add_product(total_ref.at[c], k == 0, rows_ref[:, k * ROWS:(k + 1) * ROWS], held_ref[1 - c, k])
+    for g, copy in enumerate(copies[at:]):
         copy.wait()
         add_lift(total_ref, spread_ref, lift_buf, g)
     halves_out(total_ref, side_ref[0], near_ref, far_ref)
 
 
-def into_call(first, cells, side, spread, rows, gate_weight, up_weight, lift):
+def into_call(first, cells, side, spread, rows, gate, up_weight, lift, ready):
     total, depth = rows.shape
     blocks, width = depth // ROWS, cells * CELL
-    held = pltpu.VMEM((blocks, ROWS, width), BF16)
+    copies = (1 if ready else blocks) + blocks + lift.shape[0] // GROUP
     return call(
-        functools.partial(into_kernel, first),
+        functools.partial(into_kernel, first, ready),
         "into",
         [IN_SMEM, IN_VMEM, IN_VMEM] + [ANYWHERE] * 3,
         [jax.ShapeDtypeStruct((2, total // 2, width), BF16)] * 2,
         [
             pltpu.VMEM((2, total, width), F32),
-            held,
-            held,
+            pltpu.VMEM((1 if ready else 2, blocks, ROWS, width), BF16),
             lift_held(lift, width),
-            pltpu.SemaphoreType.DMA((2 * blocks + lift.shape[0] // GROUP,)),
+            pltpu.SemaphoreType.DMA((copies,)),
         ],
-    )(side, rows, spread, gate_weight, up_weight, lift)
+    )(side, rows, spread, gate, up_weight, lift)
 
 
 def whole_hidden(side, near_ref, far_ref, hidden_ref):
@@ -537,7 +514,7 @@
     def padded(value, shape):
         return jnp.pad(value, [(0, b - a) for a, b in zip(value.shape, shape)])
 
-    near[0], far[0], spread = first_call(side, slot_row, rank_in, *mains, adapter_lift_in)
+    near[0], far[0], spread = first_call(side, slot_row, rank_in, *mains[:2], adapter_lift_in)
     sums, ranks = None, None
     for slot in range(chunks + 5):
         live = [(slot - stage, stage) for stage in range(6) if 0 <= slot - stage < chunks]
@@ -556,30 +533,39 @@
             arrived[1] = lax.ppermute(sent[-1], "tensor", MIDDLE)
         made = ()
         if slot + 1 < chunks:
+            ready = False
             made = into_call(
-                starts[slot + 1], CHUNKS[slot + 1], after(side, *sent), spread, gathered, gate_weight, up_weight, adapter_lift_in
+                starts[slot + 1],
+                CHUNKS[slot + 1],
+                after(side, *sent),
+                spread,
+                gathered,
+                mains[2] if ready else gate_weight,
+                up_weight,
+                adapter_lift_in,
+                ready,
             )
         done = slot - 6
         if done == 0:
             early = pair(0)
             zero = jnp.zeros((adapter_proj_out.shape[1], gathered.shape[0]), F32)
             ranks, _ = project_call(starts[0], 0, 1, after(side, *sent), slot_row, early, adapter_proj_out, zero)
-            sums = down_call(starts[0], after(side, ranks), early, down_weight, None)
-            made = (ranks, sums)
+            made = (ranks,)
         elif done > 0:
             ranks, ahead = project_call(
                 starts[1], starts[2], CHUNKS[2], after(side, *sent), slot_row, pair(1), adapter_proj_out, ranks
             )
-            made = (ranks, ahead)
+            sums = down_call(starts[0], after(side, ranks), early, down_weight, None)
+            made = (ranks, ahead, sums)
         *came, = lax.optimization_barrier((*arrived.values(), *made))
         arrived = dict(zip(arrived, came))
         made = came[len(arrived):]
         if slot + 1 < chunks:
             near[slot + 1], far[slot + 1] = made
         elif done == 0:
-            ranks, sums = made
+            (ranks,) = made
         elif done > 0:
-            ranks, ahead = made
+            ranks, ahead, sums = made
         for c, stage in live:
             value = arrived[stage % 3 % 2]
             units, width = (2, 1)[stage // 3], CHUNKS[c] * CELL

time: 151 us -> 149 us (0.987)
    ppermute x20, starting transfers between devices: 23.1 us -> 21.6 us  [swap(): return lax.ppermute(value, axis, [(i, i ^ mask) for i in range(size)])]
  transfers between devices with their start and end apart: 34 -> 34, of which waited for: 21 -> 20; matrix products, arithmetic and copies ran while one was open for 1% -> 1% of each run, Pallas kernels for 21% -> 22%
where the time goes in v4:
time: 149 us
  waiting for transfers between devices  50.4 us (34%)
  starting transfers between devices  48 us (32%)
  Pallas kernels  38.4 us (26%)
  other arithmetic  7.88 us (5%)
  local copies, waits for them, and re-layouts  3.45 us (2%)
    ppermute x8, waiting for transfers between devices, line_device(): arrived[0] = lax.ppermute(sent[0], 'tensor', OUTER)  30.1 us
    ppermute x20, starting transfers between devices, swap(): return lax.ppermute(value, axis, [(i, i ^ mask) for i in range(size)])  21.6 us
    ppermute x8, starting transfers between devices, line_device(): arrived[0] = lax.ppermute(sent[0], 'tensor', OUTER)  21.4 us
    ppermute x20, waiting for transfers between devices, swap(): return lax.ppermute(value, axis, [(i, i ^ mask) for i in range(size)])  20.3 us
    pallas_call x2, Pallas kernels, into_call(): call(functools.partial(into_kernel, first, ready), 'into', [IN_SMEM, IN_V...  14.2 us
    pallas_call x3, Pallas kernels, down_call(): call(functools.partial(down_kernel, first, len(bring)), 'down', [IN_SMEM,...  8.44 us
    pallas_call x2, Pallas kernels, main_call(): call(functools.partial(main_kernel, first), 'main', [IN_VMEM, ANYWHERE],...  5.2 us
    ppermute x6, starting transfers between devices, line_device(): arrived[1] = lax.ppermute(sent[-1], 'tensor', MIDDLE)  4.99 us
  transfers between devices with their start and end apart: 34, of which 20 were waited for; matrix products, arithmetic and copies ran while one was open for 1% of the time, Pallas kernels for 22%

profile of v4, /device:TPU:0, one launch (start us, length us, event | category | flops | bytes accessed | tf_op | source)
XLA Modules:
  0.0 148.7 jit_solution(12495691246897805057)
XLA Ops:
  0.0 2.9 %collective-permute-start = (bf16[24,2048]{1,0:T(8,128)(2,1)}, bf16[24,2048]{1,0:T(8,128)(2,1)S(1)}, u32[]{:S(2)}, u32[]{:S(2)}) collective-permute-start(bf16[24,2048]{1,0:T(8,128)(2,1)} %param.11), channel_id=1, source_target_pairs={{0,8},{4,12},{8,0},{12,4},{16,24},{20,28},{24,16},{28,20},{1,9},{5... | collective-permute-start | bytes 294920 | tf_op jit(solution)/shard_map/ppermute | solution.py:414
  6.3 2.5 %collective-permute-done.1 = bf16[24,2048]{1,0:T(8,128)(2,1)S(1)} collective-permute-done((bf16[24,2048]{1,0:T(8,128)(2,1)}, bf16[24,2048]{1,0:T(8,128)(2,1)S(1)}, u32[]{:S(2)}, u32[]{:S(2)}) %collective-permute-start.1) | collective-permute-done | bytes 98336 | tf_op jit(solution)/shard_map/ppermute | solution.py:414
  21.4 2.6 %main.2.gate_ref = f32[192,1024]{1,0:T(8,128)S(1)} custom-call(bf16[192,2048]{1,0:T(8,128)(2,1)S(1)} %bitcast.42, bf16[2048,3584]{1,0:T(8,128)(2,1)} %gate_ref.3), custom_call_target="tpu_custom_call" | custom-call | flops 1024 | bytes 1024 | tf_op jit(solution)/shard_map/main/pallas_call | solution.py:210
  25.8 2.6 %main.3.up_ref = f32[192,1024]{1,0:T(8,128)S(1)} custom-call(bf16[192,2048]{1,0:T(8,128)(2,1)S(1)} %bitcast.43, bf16[2048,3584]{1,0:T(8,128)(2,1)} %up_ref.3), custom_call_target="tpu_custom_call" | custom-call | flops 1024 | bytes 1024 | tf_op jit(solution)/shard_map/main/pallas_call | solution.py:210
  28.5 2.7 %collective-permute-start.9 = (f32[32,192]{1,0:T(8,128)S(1)}, f32[32,192]{1,0:T(8,128)S(1)}, u32[]{:S(2)}, u32[]{:S(2)}) collective-permute-start(f32[32,192]{1,0:T(8,128)S(1)} %add.122), channel_id=1, source_target_pairs={{0,2},{1,3},{2,0},{3,1},{4,6},{5,7},{6,4},{7,5},{8,10},{9,11},{10,... | collective-permute-start | bytes 73736 | tf_op jit(solution)/shard_map/ppermute | solution.py:414
  33.4 2.7 %first.1 = (bf16[2,96,1024]{2,1,0:T(8,128)(2,1)S(1)}, bf16[2,96,1024]{2,1,0:T(8,128)(2,1)S(1)}, bf16[2,192,1024]{2,1,0:T(8,128)(2,1)S(1)}) custom-call(s32[1]{0:T(128)} %bitcast.5.side_ref, s32[1,192]{1,0:T(1,128)S(1)} %bitcast.48, bf16[32,192]{1,0:T(8,128)(2,1)S(1)} %add_convert_fusion.3.rank_ref, f32[192,1024]{1,0:T(8,128)S(1)} %main.2.gate_ref, ...), custom_call_target="tpu_custom_call" | custom-call | flops 1024 | bytes 1024 | tf_op jit(solution)/shard_map/first/pallas_call | solution.py:240
  37.3 7.1 %into.2 = (bf16[2,96,1280]{2,1,0:T(8,128)(2,1)S(1)}, bf16[2,96,1280]{2,1,0:T(8,128)(2,1)S(1)}) custom-call(s32[1]{0:T(128)} %bitcast.5.side_ref, bf16[192,2048]{1,0:T(8,128)(2,1)S(1)} %bitcast.44, bf16[2,192,1024]{2,1,0:T(8,128)(2,1)S(1)} %get-tuple-element.88.spread_ref, bf16[2048,3584]{1,0:T(8,128)(2,1)} %gate_ref.3, bf16[2048,3584]{1,0:T(8,128)(2,1)} %up_ref.3, ...), custom_call_target="tpu_custom_call" | custom-call | flops 1024 | bytes 1024 | tf_op jit(solution)/shard_map/into/pallas_call | solution.py:271
  47.7 7.1 %into.3 = (bf16[2,96,1280]{2,1,0:T(8,128)(2,1)S(1)}, bf16[2,96,1280]{2,1,0:T(8,128)(2,1)S(1)}) custom-call(s32[1]{0:T(128)} %bitcast.5.side_ref, bf16[192,2048]{1,0:T(8,128)(2,1)S(1)} %bitcast.45, bf16[2,192,1024]{2,1,0:T(8,128)(2,1)S(1)} %get-tuple-element.88.spread_ref, bf16[2048,3584]{1,0:T(8,128)(2,1)} %gate_ref.3, bf16[2048,3584]{1,0:T(8,128)(2,1)} %up_ref.3, ...), custom_call_target="tpu_custom_call" | custom-call | flops 1024 | bytes 1024 | tf_op jit(solution)/shard_map/into/pallas_call | solution.py:271
  57.5 2.6 %collective-permute-start.13 = (bf16[2,96,1280]{2,1,0:T(8,128)(2,1)S(1)}, bf16[2,96,1280]{2,1,0:T(8,128)(2,1)S(1)}, u32[]{:S(2)}, u32[]{:S(2)}) collective-permute-start(bf16[2,96,1280]{2,1,0:T(8,128)(2,1)S(1)} %pad_select_fusion), channel_id=1, source_target_pairs={{0,1},{1,0},{2,3},{3,2},{4,5},{5,4},{6,7},{7,6},{8,9},{9,8},{10,11... | collective-permute-start | bytes 1474568 | tf_op jit(solution)/shard_map/ppermute | solution.py:531
  60.8 7.4 %collective-permute-done.13 = bf16[2,96,1280]{2,1,0:T(8,128)(2,1)S(1)} collective-permute-done((bf16[2,96,1280]{2,1,0:T(8,128)(2,1)S(1)}, bf16[2,96,1280]{2,1,0:T(8,128)(2,1)S(1)}, u32[]{:S(2)}, u32[]{:S(2)}) %collective-permute-start.13) | collective-permute-done | bytes 491552 | tf_op jit(solution)/shard_map/ppermute | solution.py:531
  68.7 3.7 %collective-permute-start.15 = (bf16[2,96,1280]{2,1,0:T(8,128)(2,1)S(1)}, bf16[2,96,1280]{2,1,0:T(8,128)(2,1)S(1)}, u32[]{:S(2)}, u32[]{:S(2)}) collective-permute-start(bf16[2,96,1280]{2,1,0:T(8,128)(2,1)S(1)} %fusion.4), channel_id=1, source_target_pairs={{0,1},{1,0},{2,3},{3,2},{4,5},{5,4},{6,7},{7,6},{8,9},{9,8},{10,11... | collective-permute-start | bytes 1474568 | tf_op jit(solution)/shard_map/ppermute | solution.py:531
  73.1 6.4 %collective-permute-done.15 = bf16[2,96,1280]{2,1,0:T(8,128)(2,1)S(1)} collective-permute-done((bf16[2,96,1280]{2,1,0:T(8,128)(2,1)S(1)}, bf16[2,96,1280]{2,1,0:T(8,128)(2,1)S(1)}, u32[]{:S(2)}, u32[]{:S(2)}) %collective-permute-start.15) | collective-permute-done | bytes 491552 | tf_op jit(solution)/shard_map/ppermute | solution.py:531
  80.2 4.0 %collective-permute-start.17 = (bf16[2,96,1280]{2,1,0:T(8,128)(2,1)S(1)}, bf16[2,96,1280]{2,1,0:T(8,128)(2,1)S(1)}, u32[]{:S(2)}, u32[]{:S(2)}) collective-permute-start(bf16[2,96,1280]{2,1,0:T(8,128)(2,1)S(1)} %fusion.5), channel_id=1, source_target_pairs={{0,1},{1,0},{2,3},{3,2},{4,5},{5,4},{6,7},{7,6},{8,9},{9,8},{10,11... | collective-permute-start | bytes 1474568 | tf_op jit(solution)/shard_map/ppermute | solution.py:531
  84.8 8.8 %collective-permute-done.17 = bf16[2,96,1280]{2,1,0:T(8,128)(2,1)S(1)} collective-permute-done((bf16[2,96,1280]{2,1,0:T(8,128)(2,1)S(1)}, bf16[2,96,1280]{2,1,0:T(8,128)(2,1)S(1)}, u32[]{:S(2)}, u32[]{:S(2)}) %collective-permute-start.17) | collective-permute-done | bytes 491552 | tf_op jit(solution)/shard_map/ppermute | solution.py:531
  96.8 4.6 %collective-permute-done.19 = bf16[1,96,1280]{2,1,0:T(8,128)(2,1)S(1)} collective-permute-done((bf16[1,96,1280]{2,1,0:T(8,128)(2,1)S(1)}, bf16[1,96,1280]{2,1,0:T(8,128)(2,1)S(1)}, u32[]{:S(2)}, u32[]{:S(2)}) %collective-permute-start.19) | collective-permute-done | bytes 245792 | tf_op jit(solution)/shard_map/ppermute | solution.py:531
  101.4 3.6 %collective-permute-start.21 = (bf16[1,96,1280]{2,1,0:T(8,128)(2,1)S(1)}, bf16[1,96,1280]{2,1,0:T(8,128)(2,1)S(1)}, u32[]{:S(2)}, u32[]{:S(2)}) collective-permute-start(bf16[1,96,1280]{2,1,0:T(8,128)(2,1)S(1)} %collective-permute-done.20), channel_id=1, source_target_pairs={{0,1},{1,0},{2,3},{3,2},{4,5},{5,4},{6,7},{7,6},{8,9},{9,8},{10,11... | collective-permute-start | bytes 737288 | tf_op jit(solution)/shard_map/ppermute | solution.py:531
  105.9 2.4 %project.3 = (f32[16,192]{1,0:T(8,128)S(1)}, bf16[4,16,16,256]{3,2,1,0:T(8,128)(2,1)}) custom-call(s32[1]{0:T(128)} %bitcast.5.side_ref, s32[1,192]{1,0:T(1,128)S(1)} %bitcast.49, bf16[96,1024]{1,0:T(8,128)(2,1)S(1)} %get-tuple-element.157.near_ref, bf16[96,1024]{1,0:T(8,128)(2,1)S(1)} %select_bitcast_fusion.4.far_ref, bf16[64,16,3584]{2,1,0:T(8,128)(2,1)S(1)} %bitcast.40, ...), custom_call_target="tpu_custom_call" | custom-call | flops 1024 | bytes 1024 | tf_op jit(solution)/shard_map/project/pallas_call | solution.py:316
  109.3 3.8 %collective-permute-start.23 = (bf16[1,96,1280]{2,1,0:T(8,128)(2,1)S(1)}, bf16[1,96,1280]{2,1,0:T(8,128)(2,1)S(1)}, u32[]{:S(2)}, u32[]{:S(2)}) collective-permute-start(bf16[1,96,1280]{2,1,0:T(8,128)(2,1)S(1)} %collective-permute-done.22), channel_id=1, source_target_pairs={{0,1},{1,0},{2,3},{3,2},{4,5},{5,4},{6,7},{7,6},{8,9},{9,8},{10,11... | collective-permute-start | bytes 737288 | tf_op jit(solution)/shard_map/ppermute | solution.py:531
  113.1 2.5 %project.4 = (f32[16,192]{1,0:T(8,128)S(1)}, bf16[4,16,16,1280]{3,2,1,0:T(8,128)(2,1)S(1)}) custom-call(s32[1]{0:T(128)} %bitcast.5.side_ref, s32[1,192]{1,0:T(1,128)S(1)} %bitcast.50, bf16[96,1280]{1,0:T(8,128)(2,1)S(1)} %get-tuple-element.155.near_ref, bf16[96,1280]{1,0:T(8,128)(2,1)S(1)} %select_bitcast_fusion.1.far_ref, ...), custom_call_target="tpu_custom_call" | custom-call | flops 1024 | bytes 1024 | tf_op jit(solution)/shard_map/project/pallas_call | solution.py:316
  115.6 2.6 %down.3.rest_0_ = f32[192,2048]{1,0:T(8,128)S(1)} custom-call(s32[1]{0:T(128)} %bitcast.5.side_ref, bf16[96,1024]{1,0:T(8,128)(2,1)S(1)} %get-tuple-element.157.near_ref, bf16[96,1024]{1,0:T(8,128)(2,1)S(1)} %select_bitcast_fusion.4.far_ref, bf16[3584,2048]{1,0:T(8,128)(2,1)} %down_ref.5), custom_call_target="tpu_custom_call" | custom-call | flops 1024 | bytes 1024 | tf_op jit(solution)/shard_map/down/pallas_call | solution.py:383
  124.0 2.9 %down.4 = (f32[192,2048]{1,0:T(8,128)S(1)}, bf16[32,16,2048]{2,1,0:T(8,128)(2,1)S(1)}) custom-call(s32[1]{0:T(128)} %bitcast.5.side_ref, bf16[96,1280]{1,0:T(8,128)(2,1)S(1)} %get-tuple-element.155.near_ref, bf16[96,1280]{1,0:T(8,128)(2,1)S(1)} %select_bitcast_fusion.1.far_ref, bf16[3584,2048]{1,0:T(8,128)(2,1)} %down_ref.5, f32[192,2048]{1,0:T(8,128)S(1)} %down.3.rest_0_, ...), custom_call_target="tpu_custom_call" | custom-call | flops 1024 | bytes 1024 | tf_op jit(solution)/shard_map/down/pallas_call | solution.py:383
  128.0 2.9 %down.5.sum_ref = f32[192,2048]{1,0:T(8,128)S(1)} custom-call(s32[1]{0:T(128)} %bitcast.5.side_ref, bf16[96,1280]{1,0:T(8,128)(2,1)S(1)} %get-tuple-element.165.near_ref, bf16[96,1280]{1,0:T(8,128)(2,1)S(1)} %get-tuple-element.164.far_ref, bf16[3584,2048]{1,0:T(8,128)(2,1)} %down_ref.5, f32[192,2048]{1,0:T(8,128)S(1)} %get-tuple-element.142.rest_0_), custom_call_target="tpu_custom_call" | custom-call | flops 1024 | bytes 1024 | tf_op jit(solution)/shard_map/down/pallas_call | solution.py:383
  131.8 3.9 %collective-permute-done.29 = f32[16,192]{1,0:T(8,128)S(1)} collective-permute-done((f32[16,192]{1,0:T(8,128)S(1)}, f32[16,192]{1,0:T(8,128)S(1)}, u32[]{:S(2)}, u32[]{:S(2)}) %collective-permute-start.29) | collective-permute-done | bytes 12320 | tf_op jit(solution)/shard_map/ppermute | solution.py:414
  143.7 3.0 %collective-permute-done.31 = bf16[24,2048]{1,0:T(8,128)(2,1)S(1)} collective-permute-done((bf16[24,2048]{1,0:T(8,128)(2,1)S(1)}, bf16[24,2048]{1,0:T(8,128)(2,1)S(1)}, u32[]{:S(2)}, u32[]{:S(2)}) %collective-permute-start.31) | collective-permute-done | bytes 98336 | tf_op jit(solution)/shard_map/ppermute | solution.py:414
  (111 shorter events, 52.9 us)
Async XLA Ops:
  0.0 6.3 %collective-permute-start = (bf16[24,2048]{1,0:T(8,128)(2,1)}, bf16[24,2048]{1,0:T(8,128)(2,1)S(1)}, u32[]{:S(2)}, u32[]{:S(2)}) collective-permute-start(bf16[24,2048]{1,0:T(8,128)(2,1)} %param.11), channel_id=1, source_target_pairs={{0,8},{4,12},{8,0},{12,4},{16,24},{20,28},{24,16},{28,20},{1,9},{5... | collective-permute-start | bytes 294920 | tf_op jit(solution)/shard_map/ppermute | solution.py:414
  2.9 5.9 %collective-permute-start.1 = (bf16[24,2048]{1,0:T(8,128)(2,1)}, bf16[24,2048]{1,0:T(8,128)(2,1)S(1)}, u32[]{:S(2)}, u32[]{:S(2)}) collective-permute-start(bf16[24,2048]{1,0:T(8,128)(2,1)} %param.11), channel_id=1, source_target_pairs={{0,16},{4,20},{8,24},{12,28},{16,0},{20,4},{24,8},{28,12},{1,17},{... | collective-permute-start | bytes 294920 | tf_op jit(solution)/shard_map/ppermute | solution.py:414
  4.5 5.7 %collective-permute-start.2 = (bf16[24,2048]{1,0:T(8,128)(2,1)}, bf16[24,2048]{1,0:T(8,128)(2,1)S(1)}, u32[]{:S(2)}, u32[]{:S(2)}) collective-permute-start(bf16[24,2048]{1,0:T(8,128)(2,1)} %param.11), channel_id=1, source_target_pairs={{0,24},{4,28},{8,16},{12,20},{16,8},{20,12},{24,0},{28,4},{1,25},{... | collective-permute-start | bytes 294920 | tf_op jit(solution)/shard_map/ppermute | solution.py:414
  17.9 6.1 %collective-permute-start.5 = (f32[32,192]{1,0:T(8,128)S(1)}, f32[32,192]{1,0:T(8,128)S(1)}, u32[]{:S(2)}, u32[]{:S(2)}) collective-permute-start(f32[32,192]{1,0:T(8,128)S(1)} %add.118), channel_id=1, source_target_pairs={{0,24},{4,28},{8,16},{12,20},{16,8},{20,12},{24,0},{28,4},{1,25},{... | collective-permute-start | bytes 73736 | tf_op jit(solution)/shard_map/ppermute | solution.py:414
  18.8 5.2 %collective-permute-start.6 = (f32[32,192]{1,0:T(8,128)S(1)}, f32[32,192]{1,0:T(8,128)S(1)}, u32[]{:S(2)}, u32[]{:S(2)}) collective-permute-start(f32[32,192]{1,0:T(8,128)S(1)} %add.118), channel_id=1, source_target_pairs={{0,8},{4,12},{8,0},{12,4},{16,24},{20,28},{24,16},{28,20},{1,9},{5... | collective-permute-start | bytes 73736 | tf_op jit(solution)/shard_map/ppermute | solution.py:414
  28.5 4.9 %collective-permute-start.9 = (f32[32,192]{1,0:T(8,128)S(1)}, f32[32,192]{1,0:T(8,128)S(1)}, u32[]{:S(2)}, u32[]{:S(2)}) collective-permute-start(f32[32,192]{1,0:T(8,128)S(1)} %add.122), channel_id=1, source_target_pairs={{0,2},{1,3},{2,0},{3,1},{4,6},{5,7},{6,4},{7,5},{8,10},{9,11},{10,... | collective-permute-start | bytes 73736 | tf_op jit(solution)/shard_map/ppermute | solution.py:414
  36.1 9.1 %collective-permute-start.10 = (bf16[2,96,1024]{2,1,0:T(8,128)(2,1)S(1)}, bf16[2,96,1024]{2,1,0:T(8,128)(2,1)S(1)}, u32[]{:S(2)}, u32[]{:S(2)}) collective-permute-start(bf16[2,96,1024]{2,1,0:T(8,128)(2,1)S(1)} %get-tuple-element.86), channel_id=1, source_target_pairs={{0,1},{1,0},{2,3},{3,2},{4,5},{5,4},{6,7},{7,6},{8,9},{9,8},{10,11... | collective-permute-start | bytes 1179656 | tf_op jit(solution)/shard_map/ppermute | solution.py:531
  46.0 10.2 %collective-permute-start.11 = (bf16[2,96,1280]{2,1,0:T(8,128)(2,1)S(1)}, bf16[2,96,1280]{2,1,0:T(8,128)(2,1)S(1)}, u32[]{:S(2)}, u32[]{:S(2)}) collective-permute-start(bf16[2,96,1280]{2,1,0:T(8,128)(2,1)S(1)} %get-tuple-element.93), channel_id=1, source_target_pairs={{0,1},{1,0},{2,3},{3,2},{4,5},{5,4},{6,7},{7,6},{8,9},{9,8},{10,11... | collective-permute-start | bytes 1474568 | tf_op jit(solution)/shard_map/ppermute | solution.py:531
  46.3 8.5 %collective-permute-start.12 = (bf16[2,96,1024]{2,1,0:T(8,128)(2,1)}, bf16[2,96,1024]{2,1,0:T(8,128)(2,1)}, u32[]{:S(2)}, u32[]{:S(2)}) collective-permute-start(bf16[2,96,1024]{2,1,0:T(8,128)(2,1)} %add_convert_fusion.2), channel_id=1, source_target_pairs={{1,2},{2,1},{5,6},{6,5},{9,10},{10,9},{13,14},{14,13},{17,18},{18,... | collective-permute-start | bytes 1179656 | tf_op jit(solution)/shard_map/ppermute | solution.py:533
  57.5 10.7 %collective-permute-start.13 = (bf16[2,96,1280]{2,1,0:T(8,128)(2,1)S(1)}, bf16[2,96,1280]{2,1,0:T(8,128)(2,1)S(1)}, u32[]{:S(2)}, u32[]{:S(2)}) collective-permute-start(bf16[2,96,1280]{2,1,0:T(8,128)(2,1)S(1)} %pad_select_fusion), channel_id=1, source_target_pairs={{0,1},{1,0},{2,3},{3,2},{4,5},{5,4},{6,7},{7,6},{8,9},{9,8},{10,11... | collective-permute-start | bytes 1474568 | tf_op jit(solution)/shard_map/ppermute | solution.py:531
  60.2 8.1 %collective-permute-start.14 = (bf16[2,96,1280]{2,1,0:T(8,128)(2,1)S(1)}, bf16[2,96,1280]{2,1,0:T(8,128)(2,1)S(1)}, u32[]{:S(2)}, u32[]{:S(2)}) collective-permute-start(bf16[2,96,1280]{2,1,0:T(8,128)(2,1)S(1)} %add_convert_fusion.1), channel_id=1, source_target_pairs={{1,2},{2,1},{5,6},{6,5},{9,10},{10,9},{13,14},{14,13},{17,18},{18,... | collective-permute-start | bytes 1474568 | tf_op jit(solution)/shard_map/ppermute | solution.py:533
  68.7 10.8 %collective-permute-start.15 = (bf16[2,96,1280]{2,1,0:T(8,128)(2,1)S(1)}, bf16[2,96,1280]{2,1,0:T(8,128)(2,1)S(1)}, u32[]{:S(2)}, u32[]{:S(2)}) collective-permute-start(bf16[2,96,1280]{2,1,0:T(8,128)(2,1)S(1)} %fusion.4), channel_id=1, source_target_pairs={{0,1},{1,0},{2,3},{3,2},{4,5},{5,4},{6,7},{7,6},{8,9},{9,8},{10,11... | collective-permute-start | bytes 1474568 | tf_op jit(solution)/shard_map/ppermute | solution.py:531
  72.5 7.1 %collective-permute-start.16 = (bf16[2,96,1280]{2,1,0:T(8,128)(2,1)S(1)}, bf16[2,96,1280]{2,1,0:T(8,128)(2,1)S(1)}, u32[]{:S(2)}, u32[]{:S(2)}) collective-permute-start(bf16[2,96,1280]{2,1,0:T(8,128)(2,1)S(1)} %add_convert_fusion), channel_id=1, source_target_pairs={{1,2},{2,1},{5,6},{6,5},{9,10},{10,9},{13,14},{14,13},{17,18},{18,... | collective-permute-start | bytes 1474568 | tf_op jit(solution)/shard_map/ppermute | solution.py:533
  80.2 13.4 %collective-permute-start.17 = (bf16[2,96,1280]{2,1,0:T(8,128)(2,1)S(1)}, bf16[2,96,1280]{2,1,0:T(8,128)(2,1)S(1)}, u32[]{:S(2)}, u32[]{:S(2)}) collective-permute-start(bf16[2,96,1280]{2,1,0:T(8,128)(2,1)S(1)} %fusion.5), channel_id=1, source_target_pairs={{0,1},{1,0},{2,3},{3,2},{4,5},{5,4},{6,7},{7,6},{8,9},{9,8},{10,11... | collective-permute-start | bytes 1474568 | tf_op jit(solution)/shard_map/ppermute | solution.py:531
  94.0 7.3 %collective-permute-start.19 = (bf16[1,96,1280]{2,1,0:T(8,128)(2,1)S(1)}, bf16[1,96,1280]{2,1,0:T(8,128)(2,1)S(1)}, u32[]{:S(2)}, u32[]{:S(2)}) collective-permute-start(bf16[1,96,1280]{2,1,0:T(8,128)(2,1)S(1)} %get-tuple-element.116), channel_id=1, source_target_pairs={{0,1},{1,0},{2,3},{3,2},{4,5},{5,4},{6,7},{7,6},{8,9},{9,8},{10,11... | collective-permute-start | bytes 737288 | tf_op jit(solution)/shard_map/ppermute | solution.py:531
  96.1 5.2 %collective-permute-start.20 = (bf16[1,96,1280]{2,1,0:T(8,128)(2,1)S(1)}, bf16[1,96,1280]{2,1,0:T(8,128)(2,1)S(1)}, u32[]{:S(2)}, u32[]{:S(2)}) collective-permute-start(bf16[1,96,1280]{2,1,0:T(8,128)(2,1)S(1)} %get-tuple-element.117), channel_id=1, source_target_pairs={{1,2},{2,1},{5,6},{6,5},{9,10},{10,9},{13,14},{14,13},{17,18},{18,... | collective-permute-start | bytes 737288 | tf_op jit(solution)/shard_map/ppermute | solution.py:533
  101.4 7.9 %collective-permute-start.21 = (bf16[1,96,1280]{2,1,0:T(8,128)(2,1)S(1)}, bf16[1,96,1280]{2,1,0:T(8,128)(2,1)S(1)}, u32[]{:S(2)}, u32[]{:S(2)}) collective-permute-start(bf16[1,96,1280]{2,1,0:T(8,128)(2,1)S(1)} %collective-permute-done.20), channel_id=1, source_target_pairs={{0,1},{1,0},{2,3},{3,2},{4,5},{5,4},{6,7},{7,6},{8,9},{9,8},{10,11... | collective-permute-start | bytes 737288 | tf_op jit(solution)/shard_map/ppermute | solution.py:531
  109.3 9.0 %collective-permute-start.23 = (bf16[1,96,1280]{2,1,0:T(8,128)(2,1)S(1)}, bf16[1,96,1280]{2,1,0:T(8,128)(2,1)S(1)}, u32[]{:S(2)}, u32[]{:S(2)}) collective-permute-start(bf16[1,96,1280]{2,1,0:T(8,128)(2,1)S(1)} %collective-permute-done.22), channel_id=1, source_target_pairs={{0,1},{1,0},{2,3},{3,2},{4,5},{5,4},{6,7},{7,6},{8,9},{9,8},{10,11... | collective-permute-start | bytes 737288 | tf_op jit(solution)/shard_map/ppermute | solution.py:531
  120.5 6.4 %collective-permute-start.25 = (f32[16,192]{1,0:T(8,128)S(1)}, f32[16,192]{1,0:T(8,128)S(1)}, u32[]{:S(2)}, u32[]{:S(2)}) collective-permute-start(f32[16,192]{1,0:T(8,128)S(1)} %add.136), channel_id=1, source_target_pairs={{0,24},{4,28},{8,16},{12,20},{16,8},{20,12},{24,0},{28,4},{1,25},{... | collective-permute-start | bytes 36872 | tf_op jit(solution)/shard_map/ppermute | solution.py:414
  121.4 5.5 %collective-permute-start.26 = (f32[16,192]{1,0:T(8,128)S(1)}, f32[16,192]{1,0:T(8,128)S(1)}, u32[]{:S(2)}, u32[]{:S(2)}) collective-permute-start(f32[16,192]{1,0:T(8,128)S(1)} %add.136), channel_id=1, source_target_pairs={{0,8},{4,12},{8,0},{12,4},{16,24},{20,28},{24,16},{28,20},{1,9},{5... | collective-permute-start | bytes 36872 | tf_op jit(solution)/shard_map/ppermute | solution.py:414
  131.0 4.7 %collective-permute-start.29 = (f32[16,192]{1,0:T(8,128)S(1)}, f32[16,192]{1,0:T(8,128)S(1)}, u32[]{:S(2)}, u32[]{:S(2)}) collective-permute-start(f32[16,192]{1,0:T(8,128)S(1)} %add.140), channel_id=1, source_target_pairs={{0,2},{1,3},{2,0},{3,1},{4,6},{5,7},{6,4},{7,5},{8,10},{9,11},{10,... | collective-permute-start | bytes 36872 | tf_op jit(solution)/shard_map/ppermute | solution.py:414
  140.1 6.6 %collective-permute-start.31 = (bf16[24,2048]{1,0:T(8,128)(2,1)S(1)}, bf16[24,2048]{1,0:T(8,128)(2,1)S(1)}, u32[]{:S(2)}, u32[]{:S(2)}) collective-permute-start(bf16[24,2048]{1,0:T(8,128)(2,1)S(1)} %get-tuple-element.159), channel_id=1, source_target_pairs={{0,24},{4,28},{8,16},{12,20},{16,8},{20,12},{24,0},{28,4},{1,25},{... | collective-permute-start | bytes 294920 | tf_op jit(solution)/shard_map/ppermute | solution.py:414
  141.1 6.2 %collective-permute-start.32 = (bf16[24,2048]{1,0:T(8,128)(2,1)S(1)}, bf16[24,2048]{1,0:T(8,128)(2,1)S(1)}, u32[]{:S(2)}, u32[]{:S(2)}) collective-permute-start(bf16[24,2048]{1,0:T(8,128)(2,1)S(1)} %get-tuple-element.161), channel_id=1, source_target_pairs={{0,8},{4,12},{8,0},{12,4},{16,24},{20,28},{24,16},{28,20},{1,9},{5... | collective-permute-start | bytes 294920 | tf_op jit(solution)/shard_map/ppermute | solution.py:414
  142.4 5.6 %collective-permute-start.33 = (bf16[24,2048]{1,0:T(8,128)(2,1)S(1)}, bf16[24,2048]{1,0:T(8,128)(2,1)S(1)}, u32[]{:S(2)}, u32[]{:S(2)}) collective-permute-start(bf16[24,2048]{1,0:T(8,128)(2,1)S(1)} %get-tuple-element.160), channel_id=1, source_target_pairs={{0,16},{4,20},{8,24},{12,28},{16,0},{20,4},{24,8},{28,12},{1,17},{... | collective-permute-start | bytes 294920 | tf_op jit(solution)/shard_map/ppermute | solution.py:414
  (16 other events, 104.4 us)

commit v5 on v4

--- a/solution.py
+++ b/solution.py
@@ -10,7 +10,7 @@
 CELL = 256
 CHUNKS = (4, 5, 5)
 VMEM_LIMIT = 40 << 20
-LIGHT = pl.CostEstimate(flops=1024, bytes_accessed=1024, transcendentals=0)
+COST = pl.CostEstimate(flops=8000000000, bytes_accessed=30000000, transcendentals=0)
 F32 = jnp.float32
 BF16 = jnp.bfloat16
 
@@ -135,7 +135,7 @@
         out_shape=outs,
         scratch_shapes=scratch,
         compiler_params=pltpu.CompilerParams(vmem_limit_bytes=VMEM_LIMIT),
-        cost_estimate=LIGHT,
+        cost_estimate=COST,
         name=name,
     )
 
@@ -574,11 +574,11 @@
     rank_out, made = sum_everywhere(
         ranks,
         [
-            (1, lambda tie: down_call(starts[1], after(side, tie), pair(1), down_weight, sums, adapter_lift_out)),
-            (2, lambda tie, before: (down_call(starts[2], after(side, tie), pair(2), down_weight, before[0]), before[1])),
+            (2, lambda tie: down_call(starts[1], after(side, tie), pair(1), down_weight, sums)),
+            (3, lambda tie, before: down_call(starts[2], after(side, tie), pair(2), down_weight, before)),
         ],
     )
-    return scatter_dp(last_call(slot_dp[None, :], rank_out.astype(BF16), *made[-1]))
+    return scatter_dp(last_call(slot_dp[None, :], rank_out.astype(BF16), made[-1], adapter_lift_out))
 
 
 def solution(mesh):

time: 149 us -> 145 us (0.973)
  local copies, waits for them, and re-layouts: 3.45 us -> 1.72 us
  other arithmetic: 7.88 us -> 6.3 us
    unnamed x12 -> x8, local copies, waits for them, and re-layouts: 3.17 us -> 1.47 us
  transfers between devices with their start and end apart: 34 -> 34, of which waited for: 20 -> 21; matrix products, arithmetic and copies ran while one was open for 1% -> 1% of each run, Pallas kernels for 22% -> 23%
where the time goes in v5:
time: 145 us
  waiting for transfers between devices  50 us (34%)
  starting transfers between devices  48.2 us (33%)
  Pallas kernels  38.5 us (27%)
  other arithmetic  6.3 us (4%)
  local copies, waits for them, and re-layouts  1.72 us (1%)
    ppermute x8, waiting for transfers between devices, line_device(): arrived[0] = lax.ppermute(sent[0], 'tensor', OUTER)  31 us
    ppermute x20, starting transfers between devices, swap(): return lax.ppermute(value, axis, [(i, i ^ mask) for i in range(size)])  22.5 us
    ppermute x8, starting transfers between devices, line_device(): arrived[0] = lax.ppermute(sent[0], 'tensor', OUTER)  21.3 us
    ppermute x20, waiting for transfers between devices, swap(): return lax.ppermute(value, axis, [(i, i ^ mask) for i in range(size)])  18.9 us
    pallas_call x2, Pallas kernels, into_call(): call(functools.partial(into_kernel, first, ready), 'into', [IN_SMEM, IN_V...  14.2 us
    pallas_call x3, Pallas kernels, down_call(): call(functools.partial(down_kernel, first, len(bring)), 'down', [IN_SMEM,...  8.44 us
    pallas_call x2, Pallas kernels, main_call(): call(functools.partial(main_kernel, first), 'main', [IN_VMEM, ANYWHERE],...  5.2 us
    pallas_call x2, Pallas kernels, project_call(): call(functools.partial(project_kernel, first, later), 'project', [IN_SMEM...  4.9 us
  transfers between devices with their start and end apart: 34, of which 21 were waited for; matrix products, arithmetic and copies ran while one was open for 1% of the time, Pallas kernels for 23%

profile of v5, /device:TPU:0, one launch (start us, length us, event | category | flops | bytes accessed | tf_op | source)
XLA Modules:
  0.0 145.1 jit_solution(2596930287919698523)
XLA Ops:
  0.0 2.9 %collective-permute-start = (bf16[24,2048]{1,0:T(8,128)(2,1)}, bf16[24,2048]{1,0:T(8,128)(2,1)S(1)}, u32[]{:S(2)}, u32[]{:S(2)}) collective-permute-start(bf16[24,2048]{1,0:T(8,128)(2,1)} %param.11), channel_id=1, source_target_pairs={{0,8},{4,12},{8,0},{12,4},{16,24},{20,28},{24,16},{28,20},{1,9},{5... | collective-permute-start | bytes 294920 | tf_op jit(solution)/shard_map/ppermute | solution.py:414
  6.3 2.5 %collective-permute-done.1 = bf16[24,2048]{1,0:T(8,128)(2,1)S(1)} collective-permute-done((bf16[24,2048]{1,0:T(8,128)(2,1)}, bf16[24,2048]{1,0:T(8,128)(2,1)S(1)}, u32[]{:S(2)}, u32[]{:S(2)}) %collective-permute-start.1) | collective-permute-done | bytes 98336 | tf_op jit(solution)/shard_map/ppermute | solution.py:414
  21.4 2.6 %main.2.gate_ref = f32[192,1024]{1,0:T(8,128)S(1)} custom-call(bf16[192,2048]{1,0:T(8,128)(2,1)S(1)} %bitcast.40, bf16[2048,3584]{1,0:T(8,128)(2,1)} %gate_ref.3), custom_call_target="tpu_custom_call" | custom-call | flops 8000000000 | bytes 30000000 | tf_op jit(solution)/shard_map/main/pallas_call | solution.py:210
  25.8 2.6 %main.3.up_ref = f32[192,1024]{1,0:T(8,128)S(1)} custom-call(bf16[192,2048]{1,0:T(8,128)(2,1)S(1)} %bitcast.41, bf16[2048,3584]{1,0:T(8,128)(2,1)} %up_ref.3), custom_call_target="tpu_custom_call" | custom-call | flops 8000000000 | bytes 30000000 | tf_op jit(solution)/shard_map/main/pallas_call | solution.py:210
  28.5 2.7 %collective-permute-start.9 = (f32[32,192]{1,0:T(8,128)S(1)}, f32[32,192]{1,0:T(8,128)S(1)}, u32[]{:S(2)}, u32[]{:S(2)}) collective-permute-start(f32[32,192]{1,0:T(8,128)S(1)} %add.122), channel_id=1, source_target_pairs={{0,2},{1,3},{2,0},{3,1},{4,6},{5,7},{6,4},{7,5},{8,10},{9,11},{10,... | collective-permute-start | bytes 73736 | tf_op jit(solution)/shard_map/ppermute | solution.py:414
  31.1 2.2 %collective-permute-done.9 = f32[32,192]{1,0:T(8,128)S(1)} collective-permute-done((f32[32,192]{1,0:T(8,128)S(1)}, f32[32,192]{1,0:T(8,128)S(1)}, u32[]{:S(2)}, u32[]{:S(2)}) %collective-permute-start.9) | collective-permute-done | bytes 24608 | tf_op jit(solution)/shard_map/ppermute | solution.py:414
  33.4 2.7 %first.1 = (bf16[2,96,1024]{2,1,0:T(8,128)(2,1)S(1)}, bf16[2,96,1024]{2,1,0:T(8,128)(2,1)S(1)}, bf16[2,192,1024]{2,1,0:T(8,128)(2,1)S(1)}) custom-call(s32[1]{0:T(128)} %bitcast.5.side_ref, s32[1,192]{1,0:T(1,128)S(1)} %bitcast.48, bf16[32,192]{1,0:T(8,128)(2,1)S(1)} %add_convert_fusion.3.rank_ref, f32[192,1024]{1,0:T(8,128)S(1)} %main.2.gate_ref, ...), custom_call_target="tpu_custom_call" | custom-call | flops 8000000000 | bytes 30000000 | tf_op jit(solution)/shard_map/first/pallas_call | solution.py:240
  37.3 7.1 %into.2 = (bf16[2,96,1280]{2,1,0:T(8,128)(2,1)S(1)}, bf16[2,96,1280]{2,1,0:T(8,128)(2,1)S(1)}) custom-call(s32[1]{0:T(128)} %bitcast.5.side_ref, bf16[192,2048]{1,0:T(8,128)(2,1)S(1)} %bitcast.42, bf16[2,192,1024]{2,1,0:T(8,128)(2,1)S(1)} %get-tuple-element.82.spread_ref, bf16[2048,3584]{1,0:T(8,128)(2,1)} %gate_ref.3, bf16[2048,3584]{1,0:T(8,128)(2,1)} %up_ref.3, ...), custom_call_target="tpu_custom_call" | custom-call | flops 8000000000 | bytes 30000000 | tf_op jit(solution)/shard_map/into/pallas_call | solution.py:271
  46.5 7.1 %into.3 = (bf16[2,96,1280]{2,1,0:T(8,128)(2,1)S(1)}, bf16[2,96,1280]{2,1,0:T(8,128)(2,1)S(1)}) custom-call(s32[1]{0:T(128)} %bitcast.5.side_ref, bf16[192,2048]{1,0:T(8,128)(2,1)S(1)} %bitcast.43, bf16[2,192,1024]{2,1,0:T(8,128)(2,1)S(1)} %get-tuple-element.82.spread_ref, bf16[2048,3584]{1,0:T(8,128)(2,1)} %gate_ref.3, bf16[2048,3584]{1,0:T(8,128)(2,1)} %up_ref.3, ...), custom_call_target="tpu_custom_call" | custom-call | flops 8000000000 | bytes 30000000 | tf_op jit(solution)/shard_map/into/pallas_call | solution.py:271
  56.0 2.5 %collective-permute-start.13 = (bf16[2,96,1280]{2,1,0:T(8,128)(2,1)S(1)}, bf16[2,96,1280]{2,1,0:T(8,128)(2,1)S(1)}, u32[]{:S(2)}, u32[]{:S(2)}) collective-permute-start(bf16[2,96,1280]{2,1,0:T(8,128)(2,1)S(1)} %pad_select_fusion), channel_id=1, source_target_pairs={{0,1},{1,0},{2,3},{3,2},{4,5},{5,4},{6,7},{7,6},{8,9},{9,8},{10,11... | collective-permute-start | bytes 1474568 | tf_op jit(solution)/shard_map/ppermute | solution.py:531
  59.2 7.4 %collective-permute-done.13 = bf16[2,96,1280]{2,1,0:T(8,128)(2,1)S(1)} collective-permute-done((bf16[2,96,1280]{2,1,0:T(8,128)(2,1)S(1)}, bf16[2,96,1280]{2,1,0:T(8,128)(2,1)S(1)}, u32[]{:S(2)}, u32[]{:S(2)}) %collective-permute-start.13) | collective-permute-done | bytes 491552 | tf_op jit(solution)/shard_map/ppermute | solution.py:531
  67.1 3.7 %collective-permute-start.15 = (bf16[2,96,1280]{2,1,0:T(8,128)(2,1)S(1)}, bf16[2,96,1280]{2,1,0:T(8,128)(2,1)S(1)}, u32[]{:S(2)}, u32[]{:S(2)}) collective-permute-start(bf16[2,96,1280]{2,1,0:T(8,128)(2,1)S(1)} %fusion.4), channel_id=1, source_target_pairs={{0,1},{1,0},{2,3},{3,2},{4,5},{5,4},{6,7},{7,6},{8,9},{9,8},{10,11... | collective-permute-start | bytes 1474568 | tf_op jit(solution)/shard_map/ppermute | solution.py:531
  71.5 6.5 %collective-permute-done.15 = bf16[2,96,1280]{2,1,0:T(8,128)(2,1)S(1)} collective-permute-done((bf16[2,96,1280]{2,1,0:T(8,128)(2,1)S(1)}, bf16[2,96,1280]{2,1,0:T(8,128)(2,1)S(1)}, u32[]{:S(2)}, u32[]{:S(2)}) %collective-permute-start.15) | collective-permute-done | bytes 491552 | tf_op jit(solution)/shard_map/ppermute | solution.py:531
  78.6 4.0 %collective-permute-start.17 = (bf16[2,96,1280]{2,1,0:T(8,128)(2,1)S(1)}, bf16[2,96,1280]{2,1,0:T(8,128)(2,1)S(1)}, u32[]{:S(2)}, u32[]{:S(2)}) collective-permute-start(bf16[2,96,1280]{2,1,0:T(8,128)(2,1)S(1)} %fusion.5), channel_id=1, source_target_pairs={{0,1},{1,0},{2,3},{3,2},{4,5},{5,4},{6,7},{7,6},{8,9},{9,8},{10,11... | collective-permute-start | bytes 1474568 | tf_op jit(solution)/shard_map/ppermute | solution.py:531
  83.2 8.8 %collective-permute-done.17 = bf16[2,96,1280]{2,1,0:T(8,128)(2,1)S(1)} collective-permute-done((bf16[2,96,1280]{2,1,0:T(8,128)(2,1)S(1)}, bf16[2,96,1280]{2,1,0:T(8,128)(2,1)S(1)}, u32[]{:S(2)}, u32[]{:S(2)}) %collective-permute-start.17) | collective-permute-done | bytes 491552 | tf_op jit(solution)/shard_map/ppermute | solution.py:531
  95.2 4.7 %collective-permute-done.19 = bf16[1,96,1280]{2,1,0:T(8,128)(2,1)S(1)} collective-permute-done((bf16[1,96,1280]{2,1,0:T(8,128)(2,1)S(1)}, bf16[1,96,1280]{2,1,0:T(8,128)(2,1)S(1)}, u32[]{:S(2)}, u32[]{:S(2)}) %collective-permute-start.19) | collective-permute-done | bytes 245792 | tf_op jit(solution)/shard_map/ppermute | solution.py:531
  99.9 3.7 %collective-permute-start.21 = (bf16[1,96,1280]{2,1,0:T(8,128)(2,1)S(1)}, bf16[1,96,1280]{2,1,0:T(8,128)(2,1)S(1)}, u32[]{:S(2)}, u32[]{:S(2)}) collective-permute-start(bf16[1,96,1280]{2,1,0:T(8,128)(2,1)S(1)} %collective-permute-done.20), channel_id=1, source_target_pairs={{0,1},{1,0},{2,3},{3,2},{4,5},{5,4},{6,7},{7,6},{8,9},{9,8},{10,11... | collective-permute-start | bytes 737288 | tf_op jit(solution)/shard_map/ppermute | solution.py:531
  104.5 2.4 %project.3 = (f32[16,192]{1,0:T(8,128)S(1)}, bf16[4,16,16,256]{3,2,1,0:T(8,128)(2,1)}) custom-call(s32[1]{0:T(128)} %bitcast.5.side_ref, s32[1,192]{1,0:T(1,128)S(1)} %bitcast.49, bf16[96,1024]{1,0:T(8,128)(2,1)S(1)} %get-tuple-element.145.near_ref, bf16[96,1024]{1,0:T(8,128)(2,1)S(1)} %select_bitcast_fusion.4.far_ref, bf16[64,16,3584]{2,1,0:T(8,128)(2,1)S(1)} %bitcast.53, ...), custom_call_target="tpu_custom_call" | custom-call | flops 8000000000 | bytes 30000000 | tf_op jit(solution)/shard_map/project/pallas_call | solution.py:316
  107.9 3.8 %collective-permute-start.23 = (bf16[1,96,1280]{2,1,0:T(8,128)(2,1)S(1)}, bf16[1,96,1280]{2,1,0:T(8,128)(2,1)S(1)}, u32[]{:S(2)}, u32[]{:S(2)}) collective-permute-start(bf16[1,96,1280]{2,1,0:T(8,128)(2,1)S(1)} %collective-permute-done.22), channel_id=1, source_target_pairs={{0,1},{1,0},{2,3},{3,2},{4,5},{5,4},{6,7},{7,6},{8,9},{9,8},{10,11... | collective-permute-start | bytes 737288 | tf_op jit(solution)/shard_map/ppermute | solution.py:531
  111.7 2.5 %project.4 = (f32[16,192]{1,0:T(8,128)S(1)}, bf16[4,16,16,1280]{3,2,1,0:T(8,128)(2,1)S(1)}) custom-call(s32[1]{0:T(128)} %bitcast.5.side_ref, s32[1,192]{1,0:T(1,128)S(1)} %bitcast.50, bf16[96,1280]{1,0:T(8,128)(2,1)S(1)} %get-tuple-element.143.near_ref, bf16[96,1280]{1,0:T(8,128)(2,1)S(1)} %select_bitcast_fusion.1.far_ref, ...), custom_call_target="tpu_custom_call" | custom-call | flops 8000000000 | bytes 30000000 | tf_op jit(solution)/shard_map/project/pallas_call | solution.py:316
  114.3 2.6 %down.3.rest_0_ = f32[192,2048]{1,0:T(8,128)S(1)} custom-call(s32[1]{0:T(128)} %bitcast.5.side_ref, bf16[96,1024]{1,0:T(8,128)(2,1)S(1)} %get-tuple-element.145.near_ref, bf16[96,1024]{1,0:T(8,128)(2,1)S(1)} %select_bitcast_fusion.4.far_ref, bf16[3584,2048]{1,0:T(8,128)(2,1)} %down_ref.5), custom_call_target="tpu_custom_call" | custom-call | flops 8000000000 | bytes 30000000 | tf_op jit(solution)/shard_map/down/pallas_call | solution.py:383
  126.0 2.9 %down.4.rest_0_ = f32[192,2048]{1,0:T(8,128)S(1)} custom-call(s32[1]{0:T(128)} %bitcast.5.side_ref, bf16[96,1280]{1,0:T(8,128)(2,1)S(1)} %get-tuple-element.143.near_ref, bf16[96,1280]{1,0:T(8,128)(2,1)S(1)} %select_bitcast_fusion.1.far_ref, bf16[3584,2048]{1,0:T(8,128)(2,1)} %down_ref.5, f32[192,2048]{1,0:T(8,128)S(1)} %down.3.rest_0_), custom_call_target="tpu_custom_call" | custom-call | flops 8000000000 | bytes 30000000 | tf_op jit(solution)/shard_map/down/pallas_call | solution.py:383
  130.7 2.9 %down.5.sum_ref = f32[192,2048]{1,0:T(8,128)S(1)} custom-call(s32[1]{0:T(128)} %bitcast.5.side_ref, bf16[96,1280]{1,0:T(8,128)(2,1)S(1)} %get-tuple-element.153.near_ref, bf16[96,1280]{1,0:T(8,128)(2,1)S(1)} %get-tuple-element.152.far_ref, bf16[3584,2048]{1,0:T(8,128)(2,1)} %down_ref.5, f32[192,2048]{1,0:T(8,128)S(1)} %down.4.rest_0_), custom_call_target="tpu_custom_call" | custom-call | flops 8000000000 | bytes 30000000 | tf_op jit(solution)/shard_map/down/pallas_call | solution.py:383
  140.1 3.0 %collective-permute-done.31 = bf16[24,2048]{1,0:T(8,128)(2,1)S(1)} collective-permute-done((bf16[24,2048]{1,0:T(8,128)(2,1)S(1)}, bf16[24,2048]{1,0:T(8,128)(2,1)S(1)}, u32[]{:S(2)}, u32[]{:S(2)}) %collective-permute-start.31) | collective-permute-done | bytes 98336 | tf_op jit(solution)/shard_map/ppermute | solution.py:414
  (107 shorter events, 50.9 us)
Async XLA Ops:
  0.0 6.3 %collective-permute-start = (bf16[24,2048]{1,0:T(8,128)(2,1)}, bf16[24,2048]{1,0:T(8,128)(2,1)S(1)}, u32[]{:S(2)}, u32[]{:S(2)}) collective-permute-start(bf16[24,2048]{1,0:T(8,128)(2,1)} %param.11), channel_id=1, source_target_pairs={{0,8},{4,12},{8,0},{12,4},{16,24},{20,28},{24,16},{28,20},{1,9},{5... | collective-permute-start | bytes 294920 | tf_op jit(solution)/shard_map/ppermute | solution.py:414
  2.9 5.9 %collective-permute-start.1 = (bf16[24,2048]{1,0:T(8,128)(2,1)}, bf16[24,2048]{1,0:T(8,128)(2,1)S(1)}, u32[]{:S(2)}, u32[]{:S(2)}) collective-permute-start(bf16[24,2048]{1,0:T(8,128)(2,1)} %param.11), channel_id=1, source_target_pairs={{0,16},{4,20},{8,24},{12,28},{16,0},{20,4},{24,8},{28,12},{1,17},{... | collective-permute-start | bytes 294920 | tf_op jit(solution)/shard_map/ppermute | solution.py:414
  4.5 5.7 %collective-permute-start.2 = (bf16[24,2048]{1,0:T(8,128)(2,1)}, bf16[24,2048]{1,0:T(8,128)(2,1)S(1)}, u32[]{:S(2)}, u32[]{:S(2)}) collective-permute-start(bf16[24,2048]{1,0:T(8,128)(2,1)} %param.11), channel_id=1, source_target_pairs={{0,24},{4,28},{8,16},{12,20},{16,8},{20,12},{24,0},{28,4},{1,25},{... | collective-permute-start | bytes 294920 | tf_op jit(solution)/shard_map/ppermute | solution.py:414
  17.9 6.1 %collective-permute-start.5 = (f32[32,192]{1,0:T(8,128)S(1)}, f32[32,192]{1,0:T(8,128)S(1)}, u32[]{:S(2)}, u32[]{:S(2)}) collective-permute-start(f32[32,192]{1,0:T(8,128)S(1)} %add.118), channel_id=1, source_target_pairs={{0,24},{4,28},{8,16},{12,20},{16,8},{20,12},{24,0},{28,4},{1,25},{... | collective-permute-start | bytes 73736 | tf_op jit(solution)/shard_map/ppermute | solution.py:414
  18.8 5.2 %collective-permute-start.6 = (f32[32,192]{1,0:T(8,128)S(1)}, f32[32,192]{1,0:T(8,128)S(1)}, u32[]{:S(2)}, u32[]{:S(2)}) collective-permute-start(f32[32,192]{1,0:T(8,128)S(1)} %add.118), channel_id=1, source_target_pairs={{0,8},{4,12},{8,0},{12,4},{16,24},{20,28},{24,16},{28,20},{1,9},{5... | collective-permute-start | bytes 73736 | tf_op jit(solution)/shard_map/ppermute | solution.py:414
  28.5 4.9 %collective-permute-start.9 = (f32[32,192]{1,0:T(8,128)S(1)}, f32[32,192]{1,0:T(8,128)S(1)}, u32[]{:S(2)}, u32[]{:S(2)}) collective-permute-start(f32[32,192]{1,0:T(8,128)S(1)} %add.122), channel_id=1, source_target_pairs={{0,2},{1,3},{2,0},{3,1},{4,6},{5,7},{6,4},{7,5},{8,10},{9,11},{10,... | collective-permute-start | bytes 73736 | tf_op jit(solution)/shard_map/ppermute | solution.py:414
  36.0 9.1 %collective-permute-start.10 = (bf16[2,96,1024]{2,1,0:T(8,128)(2,1)S(1)}, bf16[2,96,1024]{2,1,0:T(8,128)(2,1)S(1)}, u32[]{:S(2)}, u32[]{:S(2)}) collective-permute-start(bf16[2,96,1024]{2,1,0:T(8,128)(2,1)S(1)} %get-tuple-element.80), channel_id=1, source_target_pairs={{0,1},{1,0},{2,3},{3,2},{4,5},{5,4},{6,7},{7,6},{8,9},{9,8},{10,11... | collective-permute-start | bytes 1179656 | tf_op jit(solution)/shard_map/ppermute | solution.py:531
  45.3 10.3 %collective-permute-start.11 = (bf16[2,96,1280]{2,1,0:T(8,128)(2,1)S(1)}, bf16[2,96,1280]{2,1,0:T(8,128)(2,1)S(1)}, u32[]{:S(2)}, u32[]{:S(2)}) collective-permute-start(bf16[2,96,1280]{2,1,0:T(8,128)(2,1)S(1)} %get-tuple-element.87), channel_id=1, source_target_pairs={{0,1},{1,0},{2,3},{3,2},{4,5},{5,4},{6,7},{7,6},{8,9},{9,8},{10,11... | collective-permute-start | bytes 1474568 | tf_op jit(solution)/shard_map/ppermute | solution.py:531
  45.6 8.0 %collective-permute-start.12 = (bf16[2,96,1024]{2,1,0:T(8,128)(2,1)S(1)}, bf16[2,96,1024]{2,1,0:T(8,128)(2,1)S(1)}, u32[]{:S(2)}, u32[]{:S(2)}) collective-permute-start(bf16[2,96,1024]{2,1,0:T(8,128)(2,1)S(1)} %add_convert_fusion.2), channel_id=1, source_target_pairs={{1,2},{2,1},{5,6},{6,5},{9,10},{10,9},{13,14},{14,13},{17,18},{18,... | collective-permute-start | bytes 1179656 | tf_op jit(solution)/shard_map/ppermute | solution.py:533
  56.0 10.5 %collective-permute-start.13 = (bf16[2,96,1280]{2,1,0:T(8,128)(2,1)S(1)}, bf16[2,96,1280]{2,1,0:T(8,128)(2,1)S(1)}, u32[]{:S(2)}, u32[]{:S(2)}) collective-permute-start(bf16[2,96,1280]{2,1,0:T(8,128)(2,1)S(1)} %pad_select_fusion), channel_id=1, source_target_pairs={{0,1},{1,0},{2,3},{3,2},{4,5},{5,4},{6,7},{7,6},{8,9},{9,8},{10,11... | collective-permute-start | bytes 1474568 | tf_op jit(solution)/shard_map/ppermute | solution.py:531
  58.5 8.1 %collective-permute-start.14 = (bf16[2,96,1280]{2,1,0:T(8,128)(2,1)S(1)}, bf16[2,96,1280]{2,1,0:T(8,128)(2,1)S(1)}, u32[]{:S(2)}, u32[]{:S(2)}) collective-permute-start(bf16[2,96,1280]{2,1,0:T(8,128)(2,1)S(1)} %add_convert_fusion.1), channel_id=1, source_target_pairs={{1,2},{2,1},{5,6},{6,5},{9,10},{10,9},{13,14},{14,13},{17,18},{18,... | collective-permute-start | bytes 1474568 | tf_op jit(solution)/shard_map/ppermute | solution.py:533
  67.1 10.9 %collective-permute-start.15 = (bf16[2,96,1280]{2,1,0:T(8,128)(2,1)S(1)}, bf16[2,96,1280]{2,1,0:T(8,128)(2,1)S(1)}, u32[]{:S(2)}, u32[]{:S(2)}) collective-permute-start(bf16[2,96,1280]{2,1,0:T(8,128)(2,1)S(1)} %fusion.4), channel_id=1, source_target_pairs={{0,1},{1,0},{2,3},{3,2},{4,5},{5,4},{6,7},{7,6},{8,9},{9,8},{10,11... | collective-permute-start | bytes 1474568 | tf_op jit(solution)/shard_map/ppermute | solution.py:531
  70.8 7.1 %collective-permute-start.16 = (bf16[2,96,1280]{2,1,0:T(8,128)(2,1)S(1)}, bf16[2,96,1280]{2,1,0:T(8,128)(2,1)S(1)}, u32[]{:S(2)}, u32[]{:S(2)}) collective-permute-start(bf16[2,96,1280]{2,1,0:T(8,128)(2,1)S(1)} %add_convert_fusion), channel_id=1, source_target_pairs={{1,2},{2,1},{5,6},{6,5},{9,10},{10,9},{13,14},{14,13},{17,18},{18,... | collective-permute-start | bytes 1474568 | tf_op jit(solution)/shard_map/ppermute | solution.py:533
  78.6 13.4 %collective-permute-start.17 = (bf16[2,96,1280]{2,1,0:T(8,128)(2,1)S(1)}, bf16[2,96,1280]{2,1,0:T(8,128)(2,1)S(1)}, u32[]{:S(2)}, u32[]{:S(2)}) collective-permute-start(bf16[2,96,1280]{2,1,0:T(8,128)(2,1)S(1)} %fusion.5), channel_id=1, source_target_pairs={{0,1},{1,0},{2,3},{3,2},{4,5},{5,4},{6,7},{7,6},{8,9},{9,8},{10,11... | collective-permute-start | bytes 1474568 | tf_op jit(solution)/shard_map/ppermute | solution.py:531
  92.4 7.4 %collective-permute-start.19 = (bf16[1,96,1280]{2,1,0:T(8,128)(2,1)S(1)}, bf16[1,96,1280]{2,1,0:T(8,128)(2,1)S(1)}, u32[]{:S(2)}, u32[]{:S(2)}) collective-permute-start(bf16[1,96,1280]{2,1,0:T(8,128)(2,1)S(1)} %get-tuple-element.110), channel_id=1, source_target_pairs={{0,1},{1,0},{2,3},{3,2},{4,5},{5,4},{6,7},{7,6},{8,9},{9,8},{10,11... | collective-permute-start | bytes 737288 | tf_op jit(solution)/shard_map/ppermute | solution.py:531
  94.5 5.3 %collective-permute-start.20 = (bf16[1,96,1280]{2,1,0:T(8,128)(2,1)S(1)}, bf16[1,96,1280]{2,1,0:T(8,128)(2,1)S(1)}, u32[]{:S(2)}, u32[]{:S(2)}) collective-permute-start(bf16[1,96,1280]{2,1,0:T(8,128)(2,1)S(1)} %get-tuple-element.111), channel_id=1, source_target_pairs={{1,2},{2,1},{5,6},{6,5},{9,10},{10,9},{13,14},{14,13},{17,18},{18,... | collective-permute-start | bytes 737288 | tf_op jit(solution)/shard_map/ppermute | solution.py:533
  99.9 8.0 %collective-permute-start.21 = (bf16[1,96,1280]{2,1,0:T(8,128)(2,1)S(1)}, bf16[1,96,1280]{2,1,0:T(8,128)(2,1)S(1)}, u32[]{:S(2)}, u32[]{:S(2)}) collective-permute-start(bf16[1,96,1280]{2,1,0:T(8,128)(2,1)S(1)} %collective-permute-done.20), channel_id=1, source_target_pairs={{0,1},{1,0},{2,3},{3,2},{4,5},{5,4},{6,7},{7,6},{8,9},{9,8},{10,11... | collective-permute-start | bytes 737288 | tf_op jit(solution)/shard_map/ppermute | solution.py:531
  103.6 4.3 %collective-permute-start.22 = (bf16[1,96,1280]{2,1,0:T(8,128)(2,1)S(1)}, bf16[1,96,1280]{2,1,0:T(8,128)(2,1)S(1)}, u32[]{:S(2)}, u32[]{:S(2)}) collective-permute-start(bf16[1,96,1280]{2,1,0:T(8,128)(2,1)S(1)} %collective-permute-done.19), channel_id=1, source_target_pairs={{1,2},{2,1},{5,6},{6,5},{9,10},{10,9},{13,14},{14,13},{17,18},{18,... | collective-permute-start | bytes 737288 | tf_op jit(solution)/shard_map/ppermute | solution.py:533
  107.9 8.9 %collective-permute-start.23 = (bf16[1,96,1280]{2,1,0:T(8,128)(2,1)S(1)}, bf16[1,96,1280]{2,1,0:T(8,128)(2,1)S(1)}, u32[]{:S(2)}, u32[]{:S(2)}) collective-permute-start(bf16[1,96,1280]{2,1,0:T(8,128)(2,1)S(1)} %collective-permute-done.22), channel_id=1, source_target_pairs={{0,1},{1,0},{2,3},{3,2},{4,5},{5,4},{6,7},{7,6},{8,9},{9,8},{10,11... | collective-permute-start | bytes 737288 | tf_op jit(solution)/shard_map/ppermute | solution.py:531
  119.1 4.7 %collective-permute-start.25 = (f32[16,192]{1,0:T(8,128)S(1)}, f32[16,192]{1,0:T(8,128)S(1)}, u32[]{:S(2)}, u32[]{:S(2)}) collective-permute-start(f32[16,192]{1,0:T(8,128)S(1)} %add.136), channel_id=1, source_target_pairs={{0,24},{4,28},{8,16},{12,20},{16,8},{20,12},{24,0},{28,4},{1,25},{... | collective-permute-start | bytes 36872 | tf_op jit(solution)/shard_map/ppermute | solution.py:414
  128.9 4.7 %collective-permute-start.29 = (f32[16,192]{1,0:T(8,128)S(1)}, f32[16,192]{1,0:T(8,128)S(1)}, u32[]{:S(2)}, u32[]{:S(2)}) collective-permute-start(f32[16,192]{1,0:T(8,128)S(1)} %add.140), channel_id=1, source_target_pairs={{0,2},{1,3},{2,0},{3,1},{4,6},{5,7},{6,4},{7,5},{8,10},{9,11},{10,... | collective-permute-start | bytes 36872 | tf_op jit(solution)/shard_map/ppermute | solution.py:414
  136.5 6.6 %collective-permute-start.31 = (bf16[24,2048]{1,0:T(8,128)(2,1)S(1)}, bf16[24,2048]{1,0:T(8,128)(2,1)S(1)}, u32[]{:S(2)}, u32[]{:S(2)}) collective-permute-start(bf16[24,2048]{1,0:T(8,128)(2,1)S(1)} %get-tuple-element.147), channel_id=1, source_target_pairs={{0,24},{4,28},{8,16},{12,20},{16,8},{20,12},{24,0},{28,4},{1,25},{... | collective-permute-start | bytes 294920 | tf_op jit(solution)/shard_map/ppermute | solution.py:414
  138.0 6.3 %collective-permute-start.32 = (bf16[24,2048]{1,0:T(8,128)(2,1)S(1)}, bf16[24,2048]{1,0:T(8,128)(2,1)S(1)}, u32[]{:S(2)}, u32[]{:S(2)}) collective-permute-start(bf16[24,2048]{1,0:T(8,128)(2,1)S(1)} %get-tuple-element.149), channel_id=1, source_target_pairs={{0,8},{4,12},{8,0},{12,4},{16,24},{20,28},{24,16},{28,20},{1,9},{5... | collective-permute-start | bytes 294920 | tf_op jit(solution)/shard_map/ppermute | solution.py:414
  139.4 5.0 %collective-permute-start.33 = (bf16[24,2048]{1,0:T(8,128)(2,1)S(1)}, bf16[24,2048]{1,0:T(8,128)(2,1)S(1)}, u32[]{:S(2)}, u32[]{:S(2)}) collective-permute-start(bf16[24,2048]{1,0:T(8,128)(2,1)S(1)} %get-tuple-element.148), channel_id=1, source_target_pairs={{0,16},{4,20},{8,24},{12,28},{16,0},{20,4},{24,8},{28,12},{1,17},{... | collective-permute-start | bytes 294920 | tf_op jit(solution)/shard_map/ppermute | solution.py:414
  (14 other events, 97.1 us)

commit v6 on v5

--- a/solution.py
+++ b/solution.py
@@ -417,9 +417,10 @@
 def gather_dp(block, beside):
     me = lax.axis_index("dp")
     chip = me >> 1
-    near = jnp.stack([block] + [swap(block, "dp", 8, 2 * mask) for mask in (1, 2, 3)])
-    near, beside = lax.optimization_barrier((near, beside))
-    other = swap(near, "dp", 8, 1)
+    blocks = [block] + [swap(block, "dp", 8, 2 * mask) for mask in (1, 2, 3)]
+    blocks, beside = lax.optimization_barrier((blocks, beside))
+    other = jnp.stack([swap(one, "dp", 8, 1) for one in blocks])
+    near = jnp.stack(blocks)
     both = jnp.where((me & 1) == 0, jnp.stack([near, other], 1), jnp.stack([other, near], 1))
     both = jnp.where((chip & 1) == 0, both, jnp.stack([both[1], both[0], both[3], both[2]]))
     both = jnp.where((chip & 2) == 0, both, jnp.stack([both[2], both[3], both[0], both[1]]))

time: 145 us -> 145 us (level)
    ppermute x20 -> x23, waiting for transfers between devices: 18.9 us -> 18.2 us  [swap(): return lax.ppermute(value, axis, [(i, i ^ mask) for i in range(size)])]
    ppermute x20 -> x23, starting transfers between devices: 22.5 us -> 22.5 us  [swap(): return lax.ppermute(value, axis, [(i, i ^ mask) for i in range(size)])]
  transfers between devices with their start and end apart: 34 -> 37, of which waited for: 21 -> 22; matrix products, arithmetic and copies ran while one was open for 1% -> 2% of each run, Pallas kernels for 23% -> 23%
where the time goes in v6:
time: 145 us
  waiting for transfers between devices  50 us (34%)
  starting transfers between devices  48 us (33%)
  Pallas kernels  38.5 us (27%)
  other arithmetic  6.22 us (4%)
  local copies, waits for them, and re-layouts  1.85 us (1%)
    ppermute x8, waiting for transfers between devices, line_device(): arrived[0] = lax.ppermute(sent[0], 'tensor', OUTER)  31.8 us
    ppermute x23, starting transfers between devices, swap(): return lax.ppermute(value, axis, [(i, i ^ mask) for i in range(size)])  22.5 us
    ppermute x8, starting transfers between devices, line_device(): arrived[0] = lax.ppermute(sent[0], 'tensor', OUTER)  21.1 us
    ppermute x23, waiting for transfers between devices, swap(): return lax.ppermute(value, axis, [(i, i ^ mask) for i in range(size)])  18.2 us
    pallas_call x2, Pallas kernels, into_call(): call(functools.partial(into_kernel, first, ready), 'into', [IN_SMEM, IN_V...  14.2 us
    pallas_call x3, Pallas kernels, down_call(): call(functools.partial(down_kernel, first, len(bring)), 'down', [IN_SMEM,...  8.44 us
    pallas_call x2, Pallas kernels, main_call(): call(functools.partial(main_kernel, first), 'main', [IN_VMEM, ANYWHERE],...  5.2 us
    pallas_call x2, Pallas kernels, project_call(): call(functools.partial(project_kernel, first, later), 'project', [IN_SMEM...  4.9 us
  transfers between devices with their start and end apart: 37, of which 22 were waited for; matrix products, arithmetic and copies ran while one was open for 2% of the time, Pallas kernels for 23%

profile of v6, /device:TPU:0, one launch (start us, length us, event | category | flops | bytes accessed | tf_op | source)
XLA Modules:
  0.0 145.1 jit_solution(18238199957316576569)
XLA Ops:
  0.0 2.9 %collective-permute-start = (bf16[24,2048]{1,0:T(8,128)(2,1)}, bf16[24,2048]{1,0:T(8,128)(2,1)S(1)}, u32[]{:S(2)}, u32[]{:S(2)}) collective-permute-start(bf16[24,2048]{1,0:T(8,128)(2,1)} %param.11), channel_id=1, source_target_pairs={{0,8},{4,12},{8,0},{12,4},{16,24},{20,28},{24,16},{28,20},{1,9},{5... | collective-permute-start | bytes 294920 | tf_op jit(solution)/shard_map/ppermute | solution.py:414
  6.3 2.5 %collective-permute-done.1 = bf16[24,2048]{1,0:T(8,128)(2,1)S(1)} collective-permute-done((bf16[24,2048]{1,0:T(8,128)(2,1)}, bf16[24,2048]{1,0:T(8,128)(2,1)S(1)}, u32[]{:S(2)}, u32[]{:S(2)}) %collective-permute-start.1) | collective-permute-done | bytes 98336 | tf_op jit(solution)/shard_map/ppermute | solution.py:414
  20.8 2.6 %main.2.gate_ref = f32[192,1024]{1,0:T(8,128)S(1)} custom-call(bf16[192,2048]{1,0:T(8,128)(2,1)S(1)} %bitcast.46, bf16[2048,3584]{1,0:T(8,128)(2,1)} %gate_ref.3), custom_call_target="tpu_custom_call" | custom-call | flops 8000000000 | bytes 30000000 | tf_op jit(solution)/shard_map/main/pallas_call | solution.py:210
  25.1 2.6 %main.3.up_ref = f32[192,1024]{1,0:T(8,128)S(1)} custom-call(bf16[192,2048]{1,0:T(8,128)(2,1)S(1)} %bitcast.47, bf16[2048,3584]{1,0:T(8,128)(2,1)} %up_ref.3), custom_call_target="tpu_custom_call" | custom-call | flops 8000000000 | bytes 30000000 | tf_op jit(solution)/shard_map/main/pallas_call | solution.py:210
  27.8 2.7 %collective-permute-start.12 = (f32[32,192]{1,0:T(8,128)S(1)}, f32[32,192]{1,0:T(8,128)S(1)}, u32[]{:S(2)}, u32[]{:S(2)}) collective-permute-start(f32[32,192]{1,0:T(8,128)S(1)} %add.122), channel_id=1, source_target_pairs={{0,2},{1,3},{2,0},{3,1},{4,6},{5,7},{6,4},{7,5},{8,10},{9,11},{10,... | collective-permute-start | bytes 73736 | tf_op jit(solution)/shard_map/ppermute | solution.py:414
  30.4 2.2 %collective-permute-done.12 = f32[32,192]{1,0:T(8,128)S(1)} collective-permute-done((f32[32,192]{1,0:T(8,128)S(1)}, f32[32,192]{1,0:T(8,128)S(1)}, u32[]{:S(2)}, u32[]{:S(2)}) %collective-permute-start.12) | collective-permute-done | bytes 24608 | tf_op jit(solution)/shard_map/ppermute | solution.py:414
  32.7 2.7 %first.1 = (bf16[2,96,1024]{2,1,0:T(8,128)(2,1)S(1)}, bf16[2,96,1024]{2,1,0:T(8,128)(2,1)S(1)}, bf16[2,192,1024]{2,1,0:T(8,128)(2,1)S(1)}) custom-call(s32[1]{0:T(128)} %bitcast.1.side_ref, s32[1,192]{1,0:T(1,128)S(1)} %bitcast.54, bf16[32,192]{1,0:T(8,128)(2,1)S(1)} %add_convert_fusion.3.rank_ref, f32[192,1024]{1,0:T(8,128)S(1)} %main.2.gate_ref, ...), custom_call_target="tpu_custom_call" | custom-call | flops 8000000000 | bytes 30000000 | tf_op jit(solution)/shard_map/first/pallas_call | solution.py:240
  36.6 7.1 %into.2 = (bf16[2,96,1280]{2,1,0:T(8,128)(2,1)S(1)}, bf16[2,96,1280]{2,1,0:T(8,128)(2,1)S(1)}) custom-call(s32[1]{0:T(128)} %bitcast.1.side_ref, bf16[192,2048]{1,0:T(8,128)(2,1)S(1)} %bitcast.48, bf16[2,192,1024]{2,1,0:T(8,128)(2,1)S(1)} %get-tuple-element.88.spread_ref, bf16[2048,3584]{1,0:T(8,128)(2,1)} %gate_ref.3, bf16[2048,3584]{1,0:T(8,128)(2,1)} %up_ref.3, ...), custom_call_target="tpu_custom_call" | custom-call | flops 8000000000 | bytes 30000000 | tf_op jit(solution)/shard_map/into/pallas_call | solution.py:271
  45.9 7.1 %into.3 = (bf16[2,96,1280]{2,1,0:T(8,128)(2,1)S(1)}, bf16[2,96,1280]{2,1,0:T(8,128)(2,1)S(1)}) custom-call(s32[1]{0:T(128)} %bitcast.1.side_ref, bf16[192,2048]{1,0:T(8,128)(2,1)S(1)} %bitcast.49, bf16[2,192,1024]{2,1,0:T(8,128)(2,1)S(1)} %get-tuple-element.88.spread_ref, bf16[2048,3584]{1,0:T(8,128)(2,1)} %gate_ref.3, bf16[2048,3584]{1,0:T(8,128)(2,1)} %up_ref.3, ...), custom_call_target="tpu_custom_call" | custom-call | flops 8000000000 | bytes 30000000 | tf_op jit(solution)/shard_map/into/pallas_call | solution.py:271
  55.5 2.3 %collective-permute-start.16 = (bf16[2,96,1280]{2,1,0:T(8,128)(2,1)S(1)}, bf16[2,96,1280]{2,1,0:T(8,128)(2,1)S(1)}, u32[]{:S(2)}, u32[]{:S(2)}) collective-permute-start(bf16[2,96,1280]{2,1,0:T(8,128)(2,1)S(1)} %pad_select_fusion), channel_id=1, source_target_pairs={{0,1},{1,0},{2,3},{3,2},{4,5},{5,4},{6,7},{7,6},{8,9},{9,8},{10,11... | collective-permute-start | bytes 1474568 | tf_op jit(solution)/shard_map/ppermute | solution.py:532
  58.5 7.5 %collective-permute-done.16 = bf16[2,96,1280]{2,1,0:T(8,128)(2,1)S(1)} collective-permute-done((bf16[2,96,1280]{2,1,0:T(8,128)(2,1)S(1)}, bf16[2,96,1280]{2,1,0:T(8,128)(2,1)S(1)}, u32[]{:S(2)}, u32[]{:S(2)}) %collective-permute-start.16) | collective-permute-done | bytes 491552 | tf_op jit(solution)/shard_map/ppermute | solution.py:532
  66.6 3.7 %collective-permute-start.18 = (bf16[2,96,1280]{2,1,0:T(8,128)(2,1)S(1)}, bf16[2,96,1280]{2,1,0:T(8,128)(2,1)S(1)}, u32[]{:S(2)}, u32[]{:S(2)}) collective-permute-start(bf16[2,96,1280]{2,1,0:T(8,128)(2,1)S(1)} %fusion.4), channel_id=1, source_target_pairs={{0,1},{1,0},{2,3},{3,2},{4,5},{5,4},{6,7},{7,6},{8,9},{9,8},{10,11... | collective-permute-start | bytes 1474568 | tf_op jit(solution)/shard_map/ppermute | solution.py:532
  71.0 6.6 %collective-permute-done.18 = bf16[2,96,1280]{2,1,0:T(8,128)(2,1)S(1)} collective-permute-done((bf16[2,96,1280]{2,1,0:T(8,128)(2,1)S(1)}, bf16[2,96,1280]{2,1,0:T(8,128)(2,1)S(1)}, u32[]{:S(2)}, u32[]{:S(2)}) %collective-permute-start.18) | collective-permute-done | bytes 491552 | tf_op jit(solution)/shard_map/ppermute | solution.py:532
  78.2 4.0 %collective-permute-start.20 = (bf16[2,96,1280]{2,1,0:T(8,128)(2,1)S(1)}, bf16[2,96,1280]{2,1,0:T(8,128)(2,1)S(1)}, u32[]{:S(2)}, u32[]{:S(2)}) collective-permute-start(bf16[2,96,1280]{2,1,0:T(8,128)(2,1)S(1)} %fusion.5), channel_id=1, source_target_pairs={{0,1},{1,0},{2,3},{3,2},{4,5},{5,4},{6,7},{7,6},{8,9},{9,8},{10,11... | collective-permute-start | bytes 1474568 | tf_op jit(solution)/shard_map/ppermute | solution.py:532
  82.9 8.8 %collective-permute-done.20 = bf16[2,96,1280]{2,1,0:T(8,128)(2,1)S(1)} collective-permute-done((bf16[2,96,1280]{2,1,0:T(8,128)(2,1)S(1)}, bf16[2,96,1280]{2,1,0:T(8,128)(2,1)S(1)}, u32[]{:S(2)}, u32[]{:S(2)}) %collective-permute-start.20) | collective-permute-done | bytes 491552 | tf_op jit(solution)/shard_map/ppermute | solution.py:532
  94.9 4.8 %collective-permute-done.22 = bf16[1,96,1280]{2,1,0:T(8,128)(2,1)S(1)} collective-permute-done((bf16[1,96,1280]{2,1,0:T(8,128)(2,1)S(1)}, bf16[1,96,1280]{2,1,0:T(8,128)(2,1)S(1)}, u32[]{:S(2)}, u32[]{:S(2)}) %collective-permute-start.22) | collective-permute-done | bytes 245792 | tf_op jit(solution)/shard_map/ppermute | solution.py:532
  99.7 3.7 %collective-permute-start.24 = (bf16[1,96,1280]{2,1,0:T(8,128)(2,1)S(1)}, bf16[1,96,1280]{2,1,0:T(8,128)(2,1)S(1)}, u32[]{:S(2)}, u32[]{:S(2)}) collective-permute-start(bf16[1,96,1280]{2,1,0:T(8,128)(2,1)S(1)} %collective-permute-done.23), channel_id=1, source_target_pairs={{0,1},{1,0},{2,3},{3,2},{4,5},{5,4},{6,7},{7,6},{8,9},{9,8},{10,11... | collective-permute-start | bytes 737288 | tf_op jit(solution)/shard_map/ppermute | solution.py:532
  104.3 2.4 %project.3 = (f32[16,192]{1,0:T(8,128)S(1)}, bf16[4,16,16,256]{3,2,1,0:T(8,128)(2,1)}) custom-call(s32[1]{0:T(128)} %bitcast.1.side_ref, s32[1,192]{1,0:T(1,128)S(1)} %bitcast.55, bf16[96,1024]{1,0:T(8,128)(2,1)S(1)} %get-tuple-element.151.near_ref, bf16[96,1024]{1,0:T(8,128)(2,1)S(1)} %select_bitcast_fusion.4.far_ref, bf16[64,16,3584]{2,1,0:T(8,128)(2,1)S(1)} %bitcast.59, ...), custom_call_target="tpu_custom_call" | custom-call | flops 8000000000 | bytes 30000000 | tf_op jit(solution)/shard_map/project/pallas_call | solution.py:316
  107.9 3.7 %collective-permute-start.26 = (bf16[1,96,1280]{2,1,0:T(8,128)(2,1)S(1)}, bf16[1,96,1280]{2,1,0:T(8,128)(2,1)S(1)}, u32[]{:S(2)}, u32[]{:S(2)}) collective-permute-start(bf16[1,96,1280]{2,1,0:T(8,128)(2,1)S(1)} %collective-permute-done.25), channel_id=1, source_target_pairs={{0,1},{1,0},{2,3},{3,2},{4,5},{5,4},{6,7},{7,6},{8,9},{9,8},{10,11... | collective-permute-start | bytes 737288 | tf_op jit(solution)/shard_map/ppermute | solution.py:532
  111.5 2.5 %project.4 = (f32[16,192]{1,0:T(8,128)S(1)}, bf16[4,16,16,1280]{3,2,1,0:T(8,128)(2,1)S(1)}) custom-call(s32[1]{0:T(128)} %bitcast.1.side_ref, s32[1,192]{1,0:T(1,128)S(1)} %bitcast.56, bf16[96,1280]{1,0:T(8,128)(2,1)S(1)} %get-tuple-element.149.near_ref, bf16[96,1280]{1,0:T(8,128)(2,1)S(1)} %select_bitcast_fusion.1.far_ref, ...), custom_call_target="tpu_custom_call" | custom-call | flops 8000000000 | bytes 30000000 | tf_op jit(solution)/shard_map/project/pallas_call | solution.py:316
  114.1 2.6 %down.3.rest_0_ = f32[192,2048]{1,0:T(8,128)S(1)} custom-call(s32[1]{0:T(128)} %bitcast.1.side_ref, bf16[96,1024]{1,0:T(8,128)(2,1)S(1)} %get-tuple-element.151.near_ref, bf16[96,1024]{1,0:T(8,128)(2,1)S(1)} %select_bitcast_fusion.4.far_ref, bf16[3584,2048]{1,0:T(8,128)(2,1)} %down_ref.5), custom_call_target="tpu_custom_call" | custom-call | flops 8000000000 | bytes 30000000 | tf_op jit(solution)/shard_map/down/pallas_call | solution.py:383
  126.0 2.9 %down.4.rest_0_ = f32[192,2048]{1,0:T(8,128)S(1)} custom-call(s32[1]{0:T(128)} %bitcast.1.side_ref, bf16[96,1280]{1,0:T(8,128)(2,1)S(1)} %get-tuple-element.149.near_ref, bf16[96,1280]{1,0:T(8,128)(2,1)S(1)} %select_bitcast_fusion.1.far_ref, bf16[3584,2048]{1,0:T(8,128)(2,1)} %down_ref.5, f32[192,2048]{1,0:T(8,128)S(1)} %down.3.rest_0_), custom_call_target="tpu_custom_call" | custom-call | flops 8000000000 | bytes 30000000 | tf_op jit(solution)/shard_map/down/pallas_call | solution.py:383
  129.8 2.9 %down.5.sum_ref = f32[192,2048]{1,0:T(8,128)S(1)} custom-call(s32[1]{0:T(128)} %bitcast.1.side_ref, bf16[96,1280]{1,0:T(8,128)(2,1)S(1)} %get-tuple-element.159.near_ref, bf16[96,1280]{1,0:T(8,128)(2,1)S(1)} %get-tuple-element.158.far_ref, bf16[3584,2048]{1,0:T(8,128)(2,1)} %down_ref.5, f32[192,2048]{1,0:T(8,128)S(1)} %down.4.rest_0_), custom_call_target="tpu_custom_call" | custom-call | flops 8000000000 | bytes 30000000 | tf_op jit(solution)/shard_map/down/pallas_call | solution.py:383
  140.1 3.0 %collective-permute-done.34 = bf16[24,2048]{1,0:T(8,128)(2,1)S(1)} collective-permute-done((bf16[24,2048]{1,0:T(8,128)(2,1)S(1)}, bf16[24,2048]{1,0:T(8,128)(2,1)S(1)}, u32[]{:S(2)}, u32[]{:S(2)}) %collective-permute-start.34) | collective-permute-done | bytes 98336 | tf_op jit(solution)/shard_map/ppermute | solution.py:414
  (114 shorter events, 50.7 us)
Async XLA Ops:
  0.0 6.3 %collective-permute-start = (bf16[24,2048]{1,0:T(8,128)(2,1)}, bf16[24,2048]{1,0:T(8,128)(2,1)S(1)}, u32[]{:S(2)}, u32[]{:S(2)}) collective-permute-start(bf16[24,2048]{1,0:T(8,128)(2,1)} %param.11), channel_id=1, source_target_pairs={{0,8},{4,12},{8,0},{12,4},{16,24},{20,28},{24,16},{28,20},{1,9},{5... | collective-permute-start | bytes 294920 | tf_op jit(solution)/shard_map/ppermute | solution.py:414
  2.9 5.9 %collective-permute-start.1 = (bf16[24,2048]{1,0:T(8,128)(2,1)}, bf16[24,2048]{1,0:T(8,128)(2,1)S(1)}, u32[]{:S(2)}, u32[]{:S(2)}) collective-permute-start(bf16[24,2048]{1,0:T(8,128)(2,1)} %param.11), channel_id=1, source_target_pairs={{0,16},{4,20},{8,24},{12,28},{16,0},{20,4},{24,8},{28,12},{1,17},{... | collective-permute-start | bytes 294920 | tf_op jit(solution)/shard_map/ppermute | solution.py:414
  4.5 5.7 %collective-permute-start.2 = (bf16[24,2048]{1,0:T(8,128)(2,1)}, bf16[24,2048]{1,0:T(8,128)(2,1)S(1)}, u32[]{:S(2)}, u32[]{:S(2)}) collective-permute-start(bf16[24,2048]{1,0:T(8,128)(2,1)} %param.11), channel_id=1, source_target_pairs={{0,24},{4,28},{8,16},{12,20},{16,8},{20,12},{24,0},{28,4},{1,25},{... | collective-permute-start | bytes 294920 | tf_op jit(solution)/shard_map/ppermute | solution.py:414
  17.3 6.1 %collective-permute-start.10 = (f32[32,192]{1,0:T(8,128)S(1)}, f32[32,192]{1,0:T(8,128)S(1)}, u32[]{:S(2)}, u32[]{:S(2)}) collective-permute-start(f32[32,192]{1,0:T(8,128)S(1)} %add.118), channel_id=1, source_target_pairs={{0,16},{4,20},{8,24},{12,28},{16,0},{20,4},{24,8},{28,12},{1,17},{... | collective-permute-start | bytes 73736 | tf_op jit(solution)/shard_map/ppermute | solution.py:414
  18.3 5.2 %collective-permute-start.8 = (f32[32,192]{1,0:T(8,128)S(1)}, f32[32,192]{1,0:T(8,128)S(1)}, u32[]{:S(2)}, u32[]{:S(2)}) collective-permute-start(f32[32,192]{1,0:T(8,128)S(1)} %add.118), channel_id=1, source_target_pairs={{0,24},{4,28},{8,16},{12,20},{16,8},{20,12},{24,0},{28,4},{1,25},{... | collective-permute-start | bytes 73736 | tf_op jit(solution)/shard_map/ppermute | solution.py:414
  27.8 4.9 %collective-permute-start.12 = (f32[32,192]{1,0:T(8,128)S(1)}, f32[32,192]{1,0:T(8,128)S(1)}, u32[]{:S(2)}, u32[]{:S(2)}) collective-permute-start(f32[32,192]{1,0:T(8,128)S(1)} %add.122), channel_id=1, source_target_pairs={{0,2},{1,3},{2,0},{3,1},{4,6},{5,7},{6,4},{7,5},{8,10},{9,11},{10,... | collective-permute-start | bytes 73736 | tf_op jit(solution)/shard_map/ppermute | solution.py:414
  35.3 9.2 %collective-permute-start.13 = (bf16[2,96,1024]{2,1,0:T(8,128)(2,1)S(1)}, bf16[2,96,1024]{2,1,0:T(8,128)(2,1)S(1)}, u32[]{:S(2)}, u32[]{:S(2)}) collective-permute-start(bf16[2,96,1024]{2,1,0:T(8,128)(2,1)S(1)} %get-tuple-element.86), channel_id=1, source_target_pairs={{0,1},{1,0},{2,3},{3,2},{4,5},{5,4},{6,7},{7,6},{8,9},{9,8},{10,11... | collective-permute-start | bytes 1179656 | tf_op jit(solution)/shard_map/ppermute | solution.py:532
  44.7 10.4 %collective-permute-start.14 = (bf16[2,96,1280]{2,1,0:T(8,128)(2,1)S(1)}, bf16[2,96,1280]{2,1,0:T(8,128)(2,1)S(1)}, u32[]{:S(2)}, u32[]{:S(2)}) collective-permute-start(bf16[2,96,1280]{2,1,0:T(8,128)(2,1)S(1)} %get-tuple-element.93), channel_id=1, source_target_pairs={{0,1},{1,0},{2,3},{3,2},{4,5},{5,4},{6,7},{7,6},{8,9},{9,8},{10,11... | collective-permute-start | bytes 1474568 | tf_op jit(solution)/shard_map/ppermute | solution.py:532
  45.1 8.0 %collective-permute-start.15 = (bf16[2,96,1024]{2,1,0:T(8,128)(2,1)S(1)}, bf16[2,96,1024]{2,1,0:T(8,128)(2,1)S(1)}, u32[]{:S(2)}, u32[]{:S(2)}) collective-permute-start(bf16[2,96,1024]{2,1,0:T(8,128)(2,1)S(1)} %add_convert_fusion.2), channel_id=1, source_target_pairs={{1,2},{2,1},{5,6},{6,5},{9,10},{10,9},{13,14},{14,13},{17,18},{18,... | collective-permute-start | bytes 1179656 | tf_op jit(solution)/shard_map/ppermute | solution.py:534
  55.5 10.5 %collective-permute-start.16 = (bf16[2,96,1280]{2,1,0:T(8,128)(2,1)S(1)}, bf16[2,96,1280]{2,1,0:T(8,128)(2,1)S(1)}, u32[]{:S(2)}, u32[]{:S(2)}) collective-permute-start(bf16[2,96,1280]{2,1,0:T(8,128)(2,1)S(1)} %pad_select_fusion), channel_id=1, source_target_pairs={{0,1},{1,0},{2,3},{3,2},{4,5},{5,4},{6,7},{7,6},{8,9},{9,8},{10,11... | collective-permute-start | bytes 1474568 | tf_op jit(solution)/shard_map/ppermute | solution.py:532
  57.8 8.2 %collective-permute-start.17 = (bf16[2,96,1280]{2,1,0:T(8,128)(2,1)S(1)}, bf16[2,96,1280]{2,1,0:T(8,128)(2,1)S(1)}, u32[]{:S(2)}, u32[]{:S(2)}) collective-permute-start(bf16[2,96,1280]{2,1,0:T(8,128)(2,1)S(1)} %add_convert_fusion.1), channel_id=1, source_target_pairs={{1,2},{2,1},{5,6},{6,5},{9,10},{10,9},{13,14},{14,13},{17,18},{18,... | collective-permute-start | bytes 1474568 | tf_op jit(solution)/shard_map/ppermute | solution.py:534
  66.6 11.0 %collective-permute-start.18 = (bf16[2,96,1280]{2,1,0:T(8,128)(2,1)S(1)}, bf16[2,96,1280]{2,1,0:T(8,128)(2,1)S(1)}, u32[]{:S(2)}, u32[]{:S(2)}) collective-permute-start(bf16[2,96,1280]{2,1,0:T(8,128)(2,1)S(1)} %fusion.4), channel_id=1, source_target_pairs={{0,1},{1,0},{2,3},{3,2},{4,5},{5,4},{6,7},{7,6},{8,9},{9,8},{10,11... | collective-permute-start | bytes 1474568 | tf_op jit(solution)/shard_map/ppermute | solution.py:532
  70.3 7.3 %collective-permute-start.19 = (bf16[2,96,1280]{2,1,0:T(8,128)(2,1)S(1)}, bf16[2,96,1280]{2,1,0:T(8,128)(2,1)S(1)}, u32[]{:S(2)}, u32[]{:S(2)}) collective-permute-start(bf16[2,96,1280]{2,1,0:T(8,128)(2,1)S(1)} %add_convert_fusion), channel_id=1, source_target_pairs={{1,2},{2,1},{5,6},{6,5},{9,10},{10,9},{13,14},{14,13},{17,18},{18,... | collective-permute-start | bytes 1474568 | tf_op jit(solution)/shard_map/ppermute | solution.py:534
  78.2 13.4 %collective-permute-start.20 = (bf16[2,96,1280]{2,1,0:T(8,128)(2,1)S(1)}, bf16[2,96,1280]{2,1,0:T(8,128)(2,1)S(1)}, u32[]{:S(2)}, u32[]{:S(2)}) collective-permute-start(bf16[2,96,1280]{2,1,0:T(8,128)(2,1)S(1)} %fusion.5), channel_id=1, source_target_pairs={{0,1},{1,0},{2,3},{3,2},{4,5},{5,4},{6,7},{7,6},{8,9},{9,8},{10,11... | collective-permute-start | bytes 1474568 | tf_op jit(solution)/shard_map/ppermute | solution.py:532
  92.1 7.6 %collective-permute-start.22 = (bf16[1,96,1280]{2,1,0:T(8,128)(2,1)S(1)}, bf16[1,96,1280]{2,1,0:T(8,128)(2,1)S(1)}, u32[]{:S(2)}, u32[]{:S(2)}) collective-permute-start(bf16[1,96,1280]{2,1,0:T(8,128)(2,1)S(1)} %get-tuple-element.116), channel_id=1, source_target_pairs={{0,1},{1,0},{2,3},{3,2},{4,5},{5,4},{6,7},{7,6},{8,9},{9,8},{10,11... | collective-permute-start | bytes 737288 | tf_op jit(solution)/shard_map/ppermute | solution.py:532
  94.2 5.5 %collective-permute-start.23 = (bf16[1,96,1280]{2,1,0:T(8,128)(2,1)S(1)}, bf16[1,96,1280]{2,1,0:T(8,128)(2,1)S(1)}, u32[]{:S(2)}, u32[]{:S(2)}) collective-permute-start(bf16[1,96,1280]{2,1,0:T(8,128)(2,1)S(1)} %get-tuple-element.117), channel_id=1, source_target_pairs={{1,2},{2,1},{5,6},{6,5},{9,10},{10,9},{13,14},{14,13},{17,18},{18,... | collective-permute-start | bytes 737288 | tf_op jit(solution)/shard_map/ppermute | solution.py:534
  99.7 8.2 %collective-permute-start.24 = (bf16[1,96,1280]{2,1,0:T(8,128)(2,1)S(1)}, bf16[1,96,1280]{2,1,0:T(8,128)(2,1)S(1)}, u32[]{:S(2)}, u32[]{:S(2)}) collective-permute-start(bf16[1,96,1280]{2,1,0:T(8,128)(2,1)S(1)} %collective-permute-done.23), channel_id=1, source_target_pairs={{0,1},{1,0},{2,3},{3,2},{4,5},{5,4},{6,7},{7,6},{8,9},{9,8},{10,11... | collective-permute-start | bytes 737288 | tf_op jit(solution)/shard_map/ppermute | solution.py:532
  103.4 4.4 %collective-permute-start.25 = (bf16[1,96,1280]{2,1,0:T(8,128)(2,1)S(1)}, bf16[1,96,1280]{2,1,0:T(8,128)(2,1)S(1)}, u32[]{:S(2)}, u32[]{:S(2)}) collective-permute-start(bf16[1,96,1280]{2,1,0:T(8,128)(2,1)S(1)} %collective-permute-done.22), channel_id=1, source_target_pairs={{1,2},{2,1},{5,6},{6,5},{9,10},{10,9},{13,14},{14,13},{17,18},{18,... | collective-permute-start | bytes 737288 | tf_op jit(solution)/shard_map/ppermute | solution.py:534
  107.9 8.8 %collective-permute-start.26 = (bf16[1,96,1280]{2,1,0:T(8,128)(2,1)S(1)}, bf16[1,96,1280]{2,1,0:T(8,128)(2,1)S(1)}, u32[]{:S(2)}, u32[]{:S(2)}) collective-permute-start(bf16[1,96,1280]{2,1,0:T(8,128)(2,1)S(1)} %collective-permute-done.25), channel_id=1, source_target_pairs={{0,1},{1,0},{2,3},{3,2},{4,5},{5,4},{6,7},{7,6},{8,9},{9,8},{10,11... | collective-permute-start | bytes 737288 | tf_op jit(solution)/shard_map/ppermute | solution.py:532
  118.9 4.6 %collective-permute-start.28 = (f32[16,192]{1,0:T(8,128)S(1)}, f32[16,192]{1,0:T(8,128)S(1)}, u32[]{:S(2)}, u32[]{:S(2)}) collective-permute-start(f32[16,192]{1,0:T(8,128)S(1)} %add.136), channel_id=1, source_target_pairs={{0,24},{4,28},{8,16},{12,20},{16,8},{20,12},{24,0},{28,4},{1,25},{... | collective-permute-start | bytes 36872 | tf_op jit(solution)/shard_map/ppermute | solution.py:414
  129.0 4.7 %collective-permute-start.32 = (f32[16,192]{1,0:T(8,128)S(1)}, f32[16,192]{1,0:T(8,128)S(1)}, u32[]{:S(2)}, u32[]{:S(2)}) collective-permute-start(f32[16,192]{1,0:T(8,128)S(1)} %add.140), channel_id=1, source_target_pairs={{0,2},{1,3},{2,0},{3,1},{4,6},{5,7},{6,4},{7,5},{8,10},{9,11},{10,... | collective-permute-start | bytes 36872 | tf_op jit(solution)/shard_map/ppermute | solution.py:414
  136.5 6.6 %collective-permute-start.34 = (bf16[24,2048]{1,0:T(8,128)(2,1)S(1)}, bf16[24,2048]{1,0:T(8,128)(2,1)S(1)}, u32[]{:S(2)}, u32[]{:S(2)}) collective-permute-start(bf16[24,2048]{1,0:T(8,128)(2,1)S(1)} %get-tuple-element.153), channel_id=1, source_target_pairs={{0,24},{4,28},{8,16},{12,20},{16,8},{20,12},{24,0},{28,4},{1,25},{... | collective-permute-start | bytes 294920 | tf_op jit(solution)/shard_map/ppermute | solution.py:414
  137.8 6.3 %collective-permute-start.35 = (bf16[24,2048]{1,0:T(8,128)(2,1)S(1)}, bf16[24,2048]{1,0:T(8,128)(2,1)S(1)}, u32[]{:S(2)}, u32[]{:S(2)}) collective-permute-start(bf16[24,2048]{1,0:T(8,128)(2,1)S(1)} %get-tuple-element.155), channel_id=1, source_target_pairs={{0,8},{4,12},{8,0},{12,4},{16,24},{20,28},{24,16},{28,20},{1,9},{5... | collective-permute-start | bytes 294920 | tf_op jit(solution)/shard_map/ppermute | solution.py:414
  139.2 5.2 %collective-permute-start.36 = (bf16[24,2048]{1,0:T(8,128)(2,1)S(1)}, bf16[24,2048]{1,0:T(8,128)(2,1)S(1)}, u32[]{:S(2)}, u32[]{:S(2)}) collective-permute-start(bf16[24,2048]{1,0:T(8,128)(2,1)S(1)} %get-tuple-element.154), channel_id=1, source_target_pairs={{0,16},{4,20},{8,24},{12,28},{16,0},{20,4},{24,8},{28,12},{1,17},{... | collective-permute-start | bytes 294920 | tf_op jit(solution)/shard_map/ppermute | solution.py:414
  (17 other events, 103.0 us)
